TPU v7x, 128 devices: a whole 4x4x4 slice. The times are simulated.
128 devices in a mesh: gx: 16 (over y, z), gy: 8 (over x, core).
Axes of the slice: x: 4, y: 4, z: 4, core: 2. Of those that a mesh axis runs over, the one named last changes fastest.
Arguments:
- features: bfloat16 [48, 64, 32, 128], P(None, 'gx', 'gy'), may hold values from -6 to 6
- conv_one: bfloat16 [3, 3, 3, 1152], replicated, may hold values from -0.25 to 0.25
- conv_two: bfloat16 [3, 3, 3, 1152], replicated, may hold values from -0.25 to 0.25
- down_weight: bfloat16 [2, 2, 2, 4608], replicated, may hold values from -0.3125 to 0.3125
- coarse_weight: bfloat16 [3, 3, 3, 18432], replicated, may hold values from -0.125 to 0.125
- cotangent: float32 [192, 32, 1024], P('gx', None, 'gy'), may hold values from -6 to 6
Outputs:
- coarse_out: bfloat16 [192, 32, 1024], P('gx', None, 'gy')
- grad_input: bfloat16 [48, 64, 32, 128], P(None, 'gx', 'gy')
- grad_one: float32 [3, 3, 3, 1152], replicated
- grad_two: float32 [3, 3, 3, 1152], replicated
- grad_down: float32 [2, 2, 2, 4608], replicated
- grad_coarse: float32 [3, 3, 3, 18432], replicated
All inputs are finite; a program needn't handle non-finite values.
Results may differ from a plain program's by a relative error of at most 0.02.
Values may be sent and summed in bfloat16 or wider, within the bound.
No kernel may reach another device: no remote copies, remote signals or barrier semaphores. Data moves between devices by JAX's collectives and lax.ppermute only.
A program may use at most 128 MiB of HBM per device.

v0:
```python
import jax
import jax.numpy as jnp
from jax import lax
from jax.sharding import PartitionSpec as P

GROUPS = 2


def extended_2(array, sides, width):
    for axis, dim in sides:
        size, length = (lax.axis_size(axis), array.shape[dim])
        up = [(i, (i + 1) % size) for i in range(size - 1)]
        down = [(j, i) for i, j in up]
        last = lax.slice_in_dim(array, length - width, length, axis=dim)
        leading = lax.slice_in_dim(array, 0, width, axis=dim)
        before = lax.ppermute(last, axis, up)
        after = lax.ppermute(leading, axis, down)
        array = jnp.concatenate([before, array, after], axis=dim)
    return array


def as_kernel(flat, outer):
    extent = flat.shape[0]
    inner = flat.shape[3] // outer
    return jnp.transpose(flat.reshape(extent, extent, extent, outer, inner), (3, 4, 0, 1, 2))


def as_flat(kernel):
    outer, inner, extent = (kernel.shape[0], kernel.shape[1], kernel.shape[2])
    return jnp.transpose(kernel, (2, 3, 4, 0, 1)).reshape(extent, extent, extent, outer * inner)


def conv_valid(field, kernel, groups):
    return lax.conv_general_dilated(
        field[None],
        kernel,
        (1, 1, 1),
        "VALID",
        dimension_numbers=("NCDHW", "OIDHW", "NCDHW"),
        feature_group_count=groups,
        preferred_element_type=jnp.float32,
    )[0]


def transposed(kernel, groups):
    outer = kernel.shape[0]
    inner = kernel.shape[1]
    per_group = outer // groups
    reshaped = kernel.reshape((groups, per_group, inner) + kernel.shape[2:])
    swapped = jnp.swapaxes(reshaped, 1, 2).reshape((groups * inner, per_group) + kernel.shape[2:])
    return swapped[:, :, ::-1, ::-1, ::-1]


def kernel_grad(grad, padded, groups):
    outer = grad.shape[0]
    inner = padded.shape[0] // groups
    span_x = grad.shape[1]
    span_y = grad.shape[2]
    span_z = grad.shape[3]
    grouped_grad = grad.reshape(groups, outer // groups, span_x * span_y * span_z)
    taps = []
    for off_x in range(3):
        for off_y in range(3):
            for off_z in range(3):
                window = padded[
                    :, off_x : off_x + span_x, off_y : off_y + span_y, off_z : off_z + span_z
                ]
                window = window.reshape(groups, inner, span_x * span_y * span_z)
                taps.append(
                    jnp.einsum(
                        "gox,gix->goi", grouped_grad, window, preferred_element_type=jnp.float32
                    )
                )
    stacked = jnp.stack(taps, axis=-1)
    return stacked.reshape(outer, inner, 3, 3, 3)


def blocked(fine):
    chans, span_x, span_y, span_z = fine.shape
    return fine.reshape(chans, span_x // 2, 2, span_y // 2, 2, span_z // 2, 2)


def slope(value):
    sig = jax.nn.sigmoid(value)
    return sig * (1.0 + value * (1.0 - sig))


def fine_pad(field):
    extended = extended_2(field, (("gx", 1), ("gy", 2)), 1)
    return jnp.pad(extended, ((0, 0), (0, 0), (0, 0), (1, 1)))


def coarse_pad(field):
    extended = extended_2(field, (("gy", 2),), 1)
    return jnp.pad(extended, ((0, 0), (1, 1), (0, 0), (1, 1)))


def per_device(features, conv_one, conv_two, down_weight, coarse_weight, cotangent):
    groups = GROUPS
    chans = features.shape[0]
    kernel_one_w = as_kernel(conv_one, chans)
    kernel_two_w = as_kernel(conv_two, chans)
    down_kernel = as_kernel(down_weight, down_weight.shape[3] // chans)
    down_chans = down_kernel.shape[0]
    coarse_kernel = as_kernel(coarse_weight, coarse_weight.shape[3] // down_chans)
    rim_zero = fine_pad(features)
    pre_one = conv_valid(rim_zero, kernel_one_w, groups)
    act_one = jax.nn.silu(pre_one).astype(jnp.bfloat16)
    rim_one = fine_pad(act_one)
    pre_two = conv_valid(rim_one, kernel_two_w, groups)
    act_two = jax.nn.silu(pre_two).astype(jnp.bfloat16)
    blocks_two = blocked(act_two)
    coarse_in = jnp.einsum(
        "oiabc,ixaybzc->oxyz", down_kernel, blocks_two, preferred_element_type=jnp.float32
    ).astype(jnp.bfloat16)
    half_y = coarse_in.shape[2]
    half_z = coarse_in.shape[3]
    cot_cells = cotangent.reshape(cotangent.shape[0], cotangent.shape[1], half_y, half_z)
    ranks = lax.axis_size("gx")
    rank = lax.axis_index("gx")
    share = coarse_in.shape[0] // ranks
    embedded = jnp.zeros(coarse_kernel.shape, jnp.float32)
    by_channel = lax.all_to_all(coarse_in, "gx", split_axis=0, concat_axis=1, tiled=True)
    rim_coarse = coarse_pad(by_channel)
    own_part = lax.dynamic_slice_in_dim(coarse_kernel, rank * share, share, 1)
    pre_three = lax.psum_scatter(
        conv_valid(rim_coarse, own_part, 1).astype(jnp.bfloat16),
        "gx",
        scatter_dimension=0,
        tiled=True,
    ).astype(jnp.float32)
    coarse_out = jax.nn.silu(pre_three).astype(jnp.bfloat16)
    grad_three = (cot_cells * slope(pre_three)).astype(jnp.bfloat16)
    rim_grad = coarse_pad(grad_three)
    start_back = jnp.zeros(by_channel.shape, jnp.float32)
    start_kernel = jnp.zeros((coarse_kernel.shape[0], share) + coarse_kernel.shape[2:], jnp.float32)
    piece = lax.all_gather(rim_grad, "gx", axis=0, tiled=True)
    start = jnp.int32(0)
    back_sum = start_back
    kernel_sum = start_kernel
    chosen = lax.dynamic_slice_in_dim(own_part, start, piece.shape[0], 0)
    back_sum = back_sum + conv_valid(piece, transposed(chosen, 1), 1)
    fresh = kernel_grad(piece[:, 1:-1, 1:-1, 1:-1], rim_coarse, 1)
    kernel_sum = lax.dynamic_update_slice_in_dim(kernel_sum, fresh, start, 0)
    back_sum, kernel_sum = (back_sum, kernel_sum)
    coarse_back = lax.all_to_all(
        back_sum.astype(jnp.bfloat16), "gx", split_axis=1, concat_axis=0, tiled=True
    )
    embedded = lax.dynamic_update_slice_in_dim(embedded, kernel_sum, rank * share, 1)
    grad_down = jnp.einsum(
        "oxyz,ixaybzc->oiabc", coarse_back, blocks_two, preferred_element_type=jnp.float32
    )
    spread = jnp.einsum(
        "oiabc,oxyz->ixaybzc", down_kernel, coarse_back, preferred_element_type=jnp.float32
    )
    grad_act_two = spread.reshape(act_two.shape)
    grad_mid_two = (grad_act_two * slope(pre_two)).astype(jnp.bfloat16)
    kernel_two = kernel_grad(grad_mid_two, rim_one, groups)
    grad_act_one = conv_valid(fine_pad(grad_mid_two), transposed(kernel_two_w, groups), groups)
    grad_mid_one = (grad_act_one * slope(pre_one)).astype(jnp.bfloat16)
    kernel_one = kernel_grad(grad_mid_one, rim_zero, groups)
    grad_input = conv_valid(
        fine_pad(grad_mid_one), transposed(kernel_one_w, groups), groups
    ).astype(jnp.bfloat16)
    sum_one, sum_two, sum_down, sum_coarse = lax.psum(
        (as_flat(kernel_one), as_flat(kernel_two), as_flat(grad_down), as_flat(embedded)),
        ("gx", "gy"),
    )
    merged_out = coarse_out.reshape(coarse_out.shape[0], coarse_out.shape[1], half_y * half_z)
    return (merged_out, grad_input, sum_one, sum_two, sum_down, sum_coarse)


def solution(mesh):
    placed = (P(None, "gx", "gy", None), P(), P(), P(), P(), P("gx", None, "gy"))
    return jax.shard_map(
        per_device,
        mesh=mesh,
        in_specs=placed,
        out_specs=(P("gx", None, "gy"), P(None, "gx", "gy", None), P(), P(), P(), P()),
        check_vma=False,
    )
```

profile of v0, /device:TPU:1, one launch (start us, length us, event | category | flops | bytes accessed | tf_op | source)
XLA Modules:
  0.0 808.3 jit_solution(3621222152574614700)
XLA Ops:
  17.5 4.9 collective-permute-start.2
  28.6 9.0 %copy.670 = bf16[1,2,24,6,6,130]{2,0,1,5,4,3:T(2,128)(2,1)} copy(bf16[1,2,24,6,6,130]{5,2,1,4,3,0:T(8,128)(2,1)S(1)} %bitcast.698) | data formatting | bytes 898560 | tf_op jit(solution)/shard_map/broadcast_in_dim | solution.py:35
  37.6 49.3 %fusion.187 = f32[1,2,24,4,4,128]{2,0,1,5,4,3:T(1,128)S(1)} fusion(bf16[1,2,24,6,6,130]{2,0,1,5,4,3:T(2,128)(2,1)} %copy.670, bf16[2,24,24,3,3,3]{2,1,0,5,4,3:T(8,128)(2,1)S(1)} %bitcast.719), kind=kOutput, calls=%fused_computation.339 | convolution fusion | flops 127401984 | bytes 904704 | tf_op jit(solution)/shard_map/conv_general_dilated | solution.py:34
  107.4 8.9 %copy.672 = bf16[1,2,24,6,6,130]{2,0,1,5,4,3:T(2,128)(2,1)} copy(bf16[1,2,24,6,6,130]{5,2,1,4,3,0:T(8,128)(2,1)S(1)} %bitcast.697) | data formatting | bytes 898560 | tf_op jit(solution)/shard_map/broadcast_in_dim | solution.py:35
  116.8 57.9 %fusion.186 = (f32[2,24,4,4,128]{1,0,4,3,2:T(2,128)}, f32[1,2,24,4,4,128]{2,0,1,5,4,3:T(1,128)}) fusion(f32[]{:T(128)} %broadcast.228, bf16[1,2,24,6,6,130]{2,0,1,5,4,3:T(2,128)(2,1)} %copy.672, bf16[2,24,24,3,3,3]{2,1,0,5,4,3:T(8,128)(2,1)S(1)} %bitcast.721), kind=kOutput, calls=%fused_computation.338 | convolution fusion | flops 127401984 | bytes 1297924 | tf_op jit(solution)/shard_map/conv_general_dilated | solution.py:34
  181.9 8.0 all-to-all-start
  208.6 5.2 copy.681
  215.1 6.1 select_convert_fusion
  222.2 5.1 copy.684
  228.5 70.1 %reduce-scatter.2.cloned.1.call-done = bf16[12,32,2,64]{3,1,2,0:T(8,128)(2,1)} async-done(((bf16[192,32,2,64]{3,1,2,0:T(8,128)(2,1)}), bf16[12,32,2,64]{3,1,2,0:T(8,128)(2,1)}) %reduce-scatter.2.cloned.1.call-update) | async-done | bytes 98320 | tf_op jit(solution)/shard_map/reduce_scatter | solution.py:126
  300.5 5.3 collective-permute-start.10
  425.4 9.3 %slice.516 = bf16[192,32,2,64]{3,2,1,0:T(2,128)(2,1)} slice(bf16[192,34,4,66]{3,2,1,0:T(4,128)(2,1)} %all-gather.2.cloned.1.call-done), slice={[0:192], [1:33], [1:3], [1:65]} | slice | bytes 3145728 | tf_op jit(solution)/shard_map/slice | solution.py:143
  434.7 7.6 copy.823
  454.5 14.8 %copy.826 = bf16[192,34,4,1,66]{0,2,4,1,3:T(4,128)(2,1)} copy(bf16[192,34,4,1,66]{4,2,1,0,3:T(4,128)(2,1)} %bitcast.701) | data formatting | bytes 6893568
  469.3 5.0 pad.29.clone
  476.1 17.1 %fusion.3 = bf16[32,2,8,9,6]{4,2,3,1,0:T(8,128)(2,1)S(1)} fusion(bf16[192,34,4,1,7,2]{0,4,5,2,1,3:T(8,128)(2,1)S(1)} %slice.460, bf16[192,34,4,1,8,9]{0,4,5,2,1,3:T(8,128)(2,1)S(1)} %copy.690, bf16[3,3,3,192,6]{3,4,2,1,0:T(8,128)(2,1)S(1)} %copy-done.119), kind=kOutput, calls=%fused_computation.4 | convolution fusion | flops 300441600 | bytes 4608768 | tf_op jit(solution)/shard_map/conv_general_dilated | solution.py:34
  506.7 11.2 %dynamic_update_slice.3 = f32[192,96,3,3,3]{1,0,4,3,2:T(8,128)} dynamic-update-slice(f32[192,96,3,3,3]{1,0,4,3,2:T(8,128)} %broadcast_in_dim.27, f32[192,6,3,3,3]{1,0,4,3,2:T(8,128)S(1)} %copy.774, s32[]{:T(128)} %constant.26.clone.1, s32[]{:T(128)S(6)} %select_n.4, s32[]{:T(128)} %constant.26.clone.1, s32[]{:T(128)} %constant.26.clone.1, s32[]{:T(128)} %constant.26.clone.1) | dynamic-update-slice | bytes 248836 | tf_op jit(solution)/shard_map/dynamic_update_slice | solution.py:149
  518.0 5.1 reshape.531
  529.3 6.6 collective-permute-start.12
  554.9 8.9 %copy.702 = bf16[1,2,24,6,6,130]{2,0,1,5,4,3:T(2,128)(2,1)} copy(bf16[1,2,24,6,6,130]{5,2,1,4,3,0:T(8,128)(2,1)S(1)} %bitcast.714) | data formatting | bytes 898560 | tf_op jit(solution)/shard_map/broadcast_in_dim | solution.py:35
  563.8 49.5 %fusion.188 = f32[1,2,24,4,4,128]{2,0,1,5,4,3:T(1,128)S(1)} fusion(bf16[1,2,24,6,6,130]{2,0,1,5,4,3:T(2,128)(2,1)} %copy.702, bf16[2,24,24,3,3,3]{2,1,0,5,4,3:T(8,128)(2,1)S(1)} %bitcast.737), kind=kOutput, calls=%fused_computation.340 | convolution fusion | flops 127401984 | bytes 904704 | tf_op jit(solution)/shard_map/conv_general_dilated | solution.py:34
  637.9 8.9 %copy.706 = bf16[1,2,24,6,6,130]{2,0,1,5,4,3:T(2,128)(2,1)} copy(bf16[1,2,24,6,6,130]{5,2,1,4,3,0:T(8,128)(2,1)S(1)} %bitcast.715) | data formatting | bytes 898560 | tf_op jit(solution)/shard_map/broadcast_in_dim | solution.py:35
  646.9 49.9 %convolution_convert_fusion = bf16[1,2,24,4,4,128]{2,0,1,5,4,3:T(2,128)(2,1)S(1)} fusion(bf16[1,2,24,6,6,130]{2,0,1,5,4,3:T(2,128)(2,1)} %copy.706, bf16[2,24,24,3,3,3]{2,1,0,5,4,3:T(8,128)(2,1)S(1)} %bitcast.736), kind=kOutput, calls=%fused_computation.18 | convolution fusion | flops 127500288 | bytes 708096 | tf_op jit(solution)/shard_map/conv_general_dilated | solution.py:34
  698.5 94.3 %all-reduce.9.cloned.1.call-done = (f32[3,3,3,1152]{3,2,1,0:T(4,128)}, f32[3,3,3,1152]{3,2,1,0:T(4,128)}, f32[2,2,2,4608]{3,2,1,0:T(2,128)}, f32[3,3,3,18432]{3,2,1,0:T(4,128)}) async-done(((f32[3,3,3,1152]{3,2,1,0:T(4,128)}, f32[3,3,3,1152]{3,2,1,0:T(4,128)}, f32[2,2,2,4608]{3,2,1,0:T(2,128)}, f32[3,3,3,18432]{3,2,1,0:T(4,128)}), (f32[3,3,3,1152]{3,2,1,0:T(4,128)}, f32[3,3,3,1152]{3,2,1,0:T(4,128)}, ...) | async-done | bytes 2386960 | tf_op jit(solution)/shard_map/psum | solution.py:165
  (586 shorter events, 273.9 us)
Async XLA Ops:
  8.0 5.7 collective-permute-start
  12.4 5.0 collective-permute-start.1
  17.5 8.3 %collective-permute-start.2 = (bf16[48,6,1,128]{3,0,2,1:T(8,128)(2,1)S(1)}, bf16[48,6,1,128]{3,0,2,1:T(8,128)(2,1)S(1)}, u32[]{:S(2)}, u32[]{:S(2)}) collective-permute-start(bf16[48,6,1,128]{3,0,2,1:T(8,128)(2,1)S(1)} %get-tuple-element.105), channel_id=1, source_target_pairs={{0,1},{1,2},{2,3},{3,4},{4,5},{5,6},{6,7},{8,9},{9,10},{10,11},{11... | collective-permute-start | bytes 221192 | tf_op jit(solution)/shard_map/ppermute | solution.py:16
  22.5 5.7 collective-permute-start.3
  88.4 4.9 collective-permute-start.4
  97.5 7.1 collective-permute-start.6
  101.0 5.9 collective-permute-start.7
  181.9 14.5 %all-to-all-start = ((bf16[16,2,768]{2,1,0:T(2,128)(2,1)}), bf16[16,2,768]{2,1,0:T(2,128)(2,1)S(1)}, u32[]{:S(2)}, u32[]{:S(2)}) async-start(bf16[16,2,768]{2,1,0:T(2,128)(2,1)} %reshape.597), calls=%async_computation | async-start | bytes 98304 | tf_op jit(solution)/shard_map/all_to_all | solution.py:123
  189.9 108.8 %reduce-scatter.2.cloned.1.call-start = ((), (), s32[]{:S(2)}) async-start(), calls=%async_computation.3 | async-start | bytes 3342336 | tf_op jit(solution)/shard_map/reduce_scatter | solution.py:126
  196.5 7.1 collective-permute-start.8
  199.9 5.6 collective-permute-start.9
  227.4 198.0 %all-gather.2.cloned.1.call-start = ((), (), s32[]{:S(2)}) async-start(), calls=%async_computation.4 | async-start | bytes 7102464 | tf_op jit(solution)/shard_map/all_gather | solution.py:137
  300.5 7.5 collective-permute-start.10
  305.8 5.9 collective-permute-start.11
  497.4 25.7 %all-to-all-start.1 = ((bf16[16,2,768]{2,1,0:T(2,128)(2,1)}), bf16[16,2,768]{2,1,0:T(2,128)(2,1)S(1)}, u32[]{:S(2)}, u32[]{:S(2)}) async-start(bf16[16,2,768]{2,1,0:T(2,128)(2,1)} %reshape.599), calls=%async_computation.2 | async-start | bytes 98304 | tf_op jit(solution)/shard_map/all_to_all | solution.py:146
  501.9 290.9 %all-reduce.9.cloned.1.call-start = ((), (), s32[]{:S(2)}) async-start(), calls=%async_computation.5 | async-start | bytes 6266880 | tf_op jit(solution)/shard_map/psum | solution.py:165
  529.3 16.8 %collective-permute-start.12 = (bf16[48,1,4,128]{3,0,2,1:T(8,128)(2,1)S(1)}, bf16[48,1,4,128]{3,0,2,1:T(8,128)(2,1)S(1)}, u32[]{:S(2)}, u32[]{:S(2)}) collective-permute-start(bf16[48,1,4,128]{3,0,2,1:T(8,128)(2,1)S(1)} %get-tuple-element.113), channel_id=1, source_target_pairs={{0,8},{8,16},{16,24},{24,32},{32,40},{40,48},{48,56},{56,64},{64,7... | collective-permute-start | bytes 147464 | tf_op jit(solution)/shard_map/ppermute | solution.py:16
  535.9 10.2 %collective-permute-start.13 = (bf16[48,1,4,128]{3,0,2,1:T(8,128)(2,1)S(1)}, bf16[48,1,4,128]{3,0,2,1:T(8,128)(2,1)S(1)}, u32[]{:S(2)}, u32[]{:S(2)}) collective-permute-start(bf16[48,1,4,128]{3,0,2,1:T(8,128)(2,1)S(1)} %get-tuple-element.114), channel_id=1, source_target_pairs={{8,0},{16,8},{24,16},{32,24},{40,32},{48,40},{56,48},{64,56},{72,6... | collective-permute-start | bytes 147464 | tf_op jit(solution)/shard_map/ppermute | solution.py:17
  546.2 6.0 collective-permute-start.14
  548.7 5.7 collective-permute-start.15
  617.8 11.0 %collective-permute-start.16 = (bf16[48,1,4,128]{3,0,2,1:T(8,128)(2,1)S(1)}, bf16[48,1,4,128]{3,0,2,1:T(8,128)(2,1)S(1)}, u32[]{:S(2)}, u32[]{:S(2)}) collective-permute-start(bf16[48,1,4,128]{3,0,2,1:T(8,128)(2,1)S(1)} %get-tuple-element.111), channel_id=1, source_target_pairs={{0,8},{8,16},{16,24},{24,32},{32,40},{40,48},{48,56},{56,64},{64,7... | collective-permute-start | bytes 147464 | tf_op jit(solution)/shard_map/ppermute | solution.py:16
  622.2 6.6 collective-permute-start.17
  628.8 5.7 collective-permute-start.18
  631.0 5.7 collective-permute-start.19
  (123 other events, 944.6 us)
Sparse Core Ops, SparseCore 0:
  227.5 71.0 reduce-scatter.1
  313.3 61.4 all-gather.1
  634.6 158.2 all-reduce.8
where the time goes:
time: 821 us; the launch traced here: 808 us
  local copies, waits for them, and re-layouts  264 us (32%)
  matrix products  256 us (31%)
  waiting for transfers between devices  189 us (23%)
  starting transfers between devices  70.7 us (9%)
  between operations  16.1 us (2%)
  other arithmetic  12.4 us (2%)
    conv_general_dilated x6, matrix products, conv_valid(): lax.conv_general_dilated(field[None], kernel, (1, 1, 1), 'VALID', dimensi...  230 us
    psum x1, waiting for transfers between devices, per_device(): lax.psum((as_flat(kernel_one), as_flat(kernel_two), as_flat(grad_down), a...  94.3 us
    reduce_scatter x1, waiting for transfers between devices, per_device(): lax.psum_scatter(conv_valid(rim_coarse, own_part, 1).astype(jnp.bfloat16)...  70.1 us
    reshape x53, local copies, waits for them, and re-layouts, kernel_grad(): window = window.reshape(groups, inner, span_x * span_y * span_z)  58.3 us
    unnamed x263, local copies, waits for them, and re-layouts  42.9 us
    broadcast_in_dim x6, local copies, waits for them, and re-layouts, conv_valid(): field[None]  41.9 us
    ppermute x10, starting transfers between devices, extended_2(): before = lax.ppermute(last, axis, up)  40.7 us
    slice x53, local copies, waits for them, and re-layouts, kernel_grad(): padded[:, off_x:off_x + span_x, off_y:off_y + span_y, off_z:off_z + span_z]  27.9 us
  transfers between devices with their start and end apart: 25, of which 11 were waited for; matrix products, arithmetic and copies ran while one was open for 27% of the time, Pallas kernels for 0%

commit v1 on v0

v1 whole, which is shorter than its diff:
```python
import jax
import jax.numpy as jnp
from jax import lax
from jax.experimental import pallas as pl
from jax.experimental.pallas import tpu as pltpu
from jax.sharding import PartitionSpec as P

BF = jnp.bfloat16
F32 = jnp.float32
C = 48
CD = 96
CC = 192
Z = 128
ALL = ("gx", "gy")
VMEM_LIMIT = 24 * 1024 * 1024


def dot(a, b):
    return jnp.dot(a, b, preferred_element_type=F32)


def dot_t(a, b):
    return lax.dot_general(a, b, (((1,), (1,)), ((), ())), preferred_element_type=F32)


def sigmoid(v):
    return 0.5 * jnp.tanh(0.5 * v) + 0.5


def from_before(v, segment):
    lane = lax.broadcasted_iota(jnp.int32, v.shape, 1)
    return jnp.where(lane % segment == 0, 0.0, pltpu.roll(v, 1, 1))


def from_after(v, segment):
    lane = lax.broadcasted_iota(jnp.int32, v.shape, 1)
    return jnp.where(lane % segment == segment - 1, 0.0, pltpu.roll(v, Z - 1, 1))


def tap_sum(y, lanes, rows, segment, flipped):
    one, two, three = (y[k * rows : (k + 1) * rows, lanes * Z : (lanes + 1) * Z] for k in range(3))
    if flipped:
        return from_after(one, segment) + two + from_before(three, segment)
    return from_before(one, segment) + two + from_after(three, segment)


def swap_halves(v):
    return pltpu.roll(v.astype(F32), Z // 2, 1)


def low_lanes(shape):
    return lax.broadcasted_iota(jnp.int32, shape, 1) < Z // 2


def fine_kernel(
    flags, feat_l, feat_m, feat_r, w_one, w_two, w_down,
    act_one, slope_one, slope_two, down_own, coarse_in,
    stack, field, rows_two, down_all,
):
    feats = (feat_l, feat_m, feat_r)

    def valid(x, lo, hi):
        ok_l = jnp.where(x < lo, flags[0], 1.0)
        return jnp.where(x >= hi, flags[1], ok_l)

    def valid_y(y, lo, hi):
        if y < lo:
            return flags[2]
        if y >= hi:
            return flags[3]
        return 1.0

    def step_one(x, carry):
        for a in range(3):
            for y in range(12):
                piece = feats[y // 4][x + a, (y % 4) * C : (y % 4 + 1) * C, :]
                for b in range(3):
                    if 0 <= y - b < 10:
                        stack[(a * 3 + b) * C : (a * 3 + b + 1) * C, (y - b) * Z : (y - b + 1) * Z] = piece
        prod = dot(w_one[...], stack[...])
        ok_x = valid(x, 3, 7)
        for y in range(10):
            pre = tap_sum(prod, y, C, Z, False)
            sig = sigmoid(pre)
            ok = ok_x * valid_y(y, 3, 7)
            act = (pre * sig * ok).astype(BF)
            field[x, y * C : (y + 1) * C, :] = act
            if 2 <= y < 8:
                slp = sig * (1.0 + pre * (1.0 - sig)) * ok

                @pl.when(jnp.logical_and(x >= 2, x < 8))
                def _():
                    act_one[x - 2, (y - 2) * C : (y - 1) * C, :] = act
                    slope_one[x - 2, (y - 2) * C : (y - 1) * C, :] = slp

        return carry

    lax.fori_loop(0, 10, step_one, 0)

    row = lax.broadcasted_iota(jnp.int32, (2 * Z, 2 * Z), 0)
    col = lax.broadcasted_iota(jnp.int32, (2 * Z, 2 * Z), 1)
    same = (row // Z) == (col % Z) // (Z // 2)
    select = jnp.where(same & (row % Z == 2 * (col % (Z // 2)) + col // Z), 1.0, 0.0).astype(BF)

    def step_two(x, carry):
        for a in range(3):
            for y in range(10):
                piece = field[x + a, y * C : (y + 1) * C, :]
                for b in range(3):
                    if 0 <= y - b < 8:
                        stack[(a * 3 + b) * C : (a * 3 + b + 1) * C, (y - b) * Z : (y - b + 1) * Z] = piece
        prod = dot(w_two[...], stack[:, : 8 * Z])
        ok_x = valid(x, 2, 6)
        for y in range(8):
            pre = tap_sum(prod, y, C, Z, False)
            sig = sigmoid(pre)
            ok = ok_x * valid_y(y, 2, 6)
            act = (pre * sig * ok).astype(BF)
            slope_two[x, y * C : (y + 1) * C, :] = sig * (1.0 + pre * (1.0 - sig)) * ok
            pair, b = y // 2, y % 2
            if pair < 3:
                rows_two[(pair * 2 + b) * C : (pair * 2 + b + 1) * C, :Z] = act
            if pair > 0:
                rows_two[((pair - 1) * 2 + b) * C : ((pair - 1) * 2 + b + 1) * C, Z:] = act
        picked = dot(rows_two[...], select).astype(BF)
        a = x % 2
        for pair in range(3):
            for b in range(2):
                for c in range(2):
                    at = pl.multiple_of(a * (4 * C) + (b * 2 + c) * C, 16)
                    down_all[x // 2, pl.ds(at, C), pair * Z : (pair + 1) * Z] = picked[
                        (pair * 2 + b) * C : (pair * 2 + b + 1) * C, c * Z : (c + 1) * Z
                    ]
        return carry

    lax.fori_loop(0, 8, step_two, 0)

    for x in range(2):
        down_own[x] = down_all[x + 1, :, Z : 2 * Z]
    for x in range(4):
        coarse_in[x] = dot(w_down[...], down_all[x]).astype(BF)


def coarse_kernel(coarse_in, w_coarse, cot, coarse_out, grad_three):
    total = jnp.zeros((3 * CC, 2 * Z), F32)
    for a in range(3):
        for b in range(3):
            cells = jnp.concatenate(
                [coarse_in[a + x, :, b * Z : (b + 1) * Z] for x in range(2)], axis=1
            )
            total = total + dot(w_coarse[a * 3 + b], cells)
    for x in range(2):
        pre = tap_sum(total, x, CC, Z // 2, False)
        sig = sigmoid(pre)
        coarse_out[x] = (pre * sig).astype(BF)
        grad_three[x] = (cot[x].astype(F32) * (sig * (1.0 + pre * (1.0 - sig)))).astype(BF)


def grouped(taps, c):
    first = lax.broadcasted_iota(jnp.int32, (C, C // 2), 0) < C // 2
    parts = []
    for ab in range(9):
        tap = taps[ab * 3 + c].astype(F32)
        parts += [jnp.where(first, tap, 0.0), jnp.where(first, 0.0, tap)]
    return jnp.concatenate(parts, axis=1)


def ahead_kernel(one, two, down, w_one, w_two, w_down):
    for taps, out in ((one, w_one), (two, w_two)):
        for c in range(3):
            out[c * C : (c + 1) * C, :] = grouped(taps, c).astype(BF)
    w_down[...] = jnp.concatenate([down[k].astype(F32) for k in range(8)], axis=1).astype(BF)


def back_kernel(one, two, down, coarse, w_one_t, w_two_t, w_down_t, w_coarse_t):
    for taps, out in ((one, w_one_t), (two, w_two_t)):
        for c in range(3):
            turned = grouped(taps, c).T
            out[c * C : (c + 1) * C, :] = jnp.concatenate(
                [turned[ab * C : (ab + 1) * C, :] for ab in range(9)], axis=1
            ).astype(BF)
    for ab in range(4):
        w_down_t[ab * C : (ab + 1) * C, :] = jnp.concatenate(
            [down[ab * 2 + c].astype(F32).T for c in range(2)], axis=1
        ).astype(BF)

    def turn(ab, carry):
        for c in range(3):
            w_coarse_t[ab, c * CD : (c + 1) * CD, :] = (
                coarse[ab, c * CC : (c + 1) * CC, :].astype(F32).T.astype(BF)
            )
        return carry

    lax.fori_loop(0, 9, turn, 0)


def final_kernel(rows, out, wide):
    wide[...] = rows[...].astype(F32)
    for ab in range(9):
        for r in range(144):
            q, s = r // 3, r % 3
            out[ab // 3, ab % 3, :, r * Z : (r + 1) * Z] = wide[
                pl.ds(ab * 432 + s * 48 + q, 3, stride=144), :
            ]


def coarse_grad_kernel(grad_three, coarse_in, out, shifted, left):
    for x in range(2):
        grad = grad_three[x].astype(F32)
        lanes = slice(x * Z, (x + 1) * Z)
        shifted[x, 0] = from_after(grad, Z // 2)
        shifted[x, 1] = grad
        shifted[x, 2] = from_before(grad, Z // 2)
        for c in range(3):
            for r in range(4):
                left[(c * 4 + r) * 48 : (c * 4 + r + 1) * 48, lanes] = shifted[
                    x, c, pl.ds(r, 48, stride=4), :
                ].astype(BF)
    for a in range(3):
        for b in range(3):
            cells = jnp.concatenate(
                [coarse_in[a + x, :, b * Z : (b + 1) * Z] for x in range(2)], axis=1
            )
            part = dot_t(left[...], cells)
            for c in range(3):
                wide = jnp.concatenate(
                    [part[(c * 4 + r) * 48 : (c * 4 + r + 1) * 48, :] for r in range(4)], axis=1
                ).astype(BF)
                tap = (a * 3 + b) * 3 + c
                for s in range(3):
                    at = (tap * 3 + s) * 48
                    out[at : at + 48, :] = wide[:, s * Z : (s + 1) * Z]
    out[81 * 48 :, :] = jnp.zeros((4096 - 81 * 48, Z), BF)


def backward_kernel(
    g_l, g_m, g_r, feat_l, feat_m, feat_r, act_one, slope_one, slope_two, down_own,
    w_one_t, w_two_t, w_down_t, w_coarse_t,
    grad_input, small,
    halves, spread, mid_two, mid_one, stack, left,
):
    low = low_lanes((CC, Z))

    def prepare(x, carry):
        p0, p1, p2 = g_l[x], g_m[x], g_r[x]
        s0, s1, s2 = swap_halves(p0), swap_halves(p1), swap_halves(p2)
        halves[0, x, :, :Z] = p1
        halves[0, x, :, Z:] = p2
        halves[1, x, :, :Z] = jnp.where(low, s0, s1).astype(BF)
        halves[1, x, :, Z:] = jnp.where(low, s1, s2).astype(BF)
        halves[2, x, :, :Z] = p0
        halves[2, x, :, Z:] = p1
        return carry

    lax.fori_loop(0, 6, prepare, 0)

    row = lax.broadcasted_iota(jnp.int32, (Z, 4 * Z), 0)
    col = lax.broadcasted_iota(jnp.int32, (Z, 4 * Z), 1)
    same = row // (Z // 2) == col // (2 * Z)
    place = jnp.where(same & (col % Z == 2 * (row % (Z // 2)) + (col // Z) % 2), 1.0, 0.0).astype(BF)
    low_down = low_lanes((CD, Z))

    grad_down = jnp.zeros((CD, 8 * C), F32)
    for x in range(4):
        total = jnp.zeros((3 * CD, 2 * Z), F32)
        for a in range(3):
            for b in range(3):
                total = total + dot(w_coarse_t[a * 3 + b], halves[b, x + 2 - a])
        back = [tap_sum(total, k, CD, Z // 2, True).astype(BF) for k in range(2)]
        if x == 1 or x == 2:
            own = jnp.where(low_down, swap_halves(back[0]), swap_halves(back[1])).astype(BF)
            grad_down = grad_down + dot_t(own, down_own[x - 1])
        for k in range(2):
            wide = dot(back[k], place).astype(BF)
            for y in range(2):
                for c in range(2):
                    spread[c * CD : (c + 1) * CD, (k * 2 + y) * Z : (k * 2 + y + 1) * Z] = wide[
                        :, (y * 2 + c) * Z : (y * 2 + c + 1) * Z
                    ]
        fine = dot(w_down_t[...], spread[...])
        for a in range(2):
            for b in range(2):
                for y in range(4):
                    rows = slice((2 * y + b) * C, (2 * y + b + 1) * C)
                    part = fine[(a * 2 + b) * C : (a * 2 + b + 1) * C, y * Z : (y + 1) * Z]
                    mid_two[2 * x + a, rows, :] = (part * slope_two[2 * x + a, rows, :]).astype(BF)
    for s in range(3):
        small[1152 + s * CD : 1152 + (s + 1) * CD, :] = grad_down[:, s * Z : (s + 1) * Z].astype(BF)

    def kernel_grad(grad_of, field_of, at):
        for x in range(4):
            for y in range(4):
                lanes = slice((x * 4 + y) * Z, (x * 4 + y + 1) * Z)
                grad = grad_of(x, y).astype(F32)
                left[:C, lanes] = from_after(grad, Z).astype(BF)
                left[C : 2 * C, lanes] = grad.astype(BF)
                left[2 * C :, lanes] = from_before(grad, Z).astype(BF)
        for x in range(6):
            for y in range(6):
                piece = field_of(x, y)
                for a in range(3):
                    for b in range(3):
                        if 0 <= x - a < 4 and 0 <= y - b < 4:
                            cell = (x - a) * 4 + (y - b)
                            stack[(a * 3 + b) * C : (a * 3 + b + 1) * C, cell * Z : (cell + 1) * Z] = piece
        part = dot_t(left[...], stack[...]).astype(BF)
        for s in range(3):
            small[at + s * 144 : at + (s + 1) * 144, :] = part[:, s * Z : (s + 1) * Z]
        small[at + 432 : at + 576, :48] = part[:, 3 * Z :]
        small[at + 432 : at + 576, 48:] = jnp.zeros((144, Z - 48), BF)

    kernel_grad(
        lambda x, y: mid_two[x + 2, (y + 2) * C : (y + 3) * C, :],
        lambda x, y: act_one[x, y * C : (y + 1) * C, :],
        576,
    )

    def step_two(x, carry):
        for a in range(3):
            for y in range(8):
                piece = mid_two[x + 2 - a, y * C : (y + 1) * C, :]
                for b in range(3):
                    at = y - 2 + b
                    if 0 <= at < 6:
                        stack[(a * 3 + b) * C : (a * 3 + b + 1) * C, at * Z : (at + 1) * Z] = piece
        prod = dot(w_two_t[...], stack[:, : 6 * Z])
        for y in range(6):
            rows = slice(y * C, (y + 1) * C)
            grad = tap_sum(prod, y, C, Z, True)
            mid_one[x, rows, :] = (grad * slope_one[x, rows, :]).astype(BF)
        return carry

    lax.fori_loop(0, 6, step_two, 0)

    feats = {-1: feat_l, 0: feat_m, 1: feat_r}

    def feature(x, y):
        fine_y = y - 1
        block = fine_y // 4
        return feats[block][x + 3, (fine_y % 4) * C : (fine_y % 4 + 1) * C, :]

    kernel_grad(lambda x, y: mid_one[x + 1, (y + 1) * C : (y + 2) * C, :], feature, 0)

    def step_one(x, carry):
        for a in range(3):
            for y in range(6):
                piece = mid_one[x + 2 - a, y * C : (y + 1) * C, :]
                for b in range(3):
                    at = y - 2 + b
                    if 0 <= at < 4:
                        stack[(a * 3 + b) * C : (a * 3 + b + 1) * C, at * Z : (at + 1) * Z] = piece
        prod = dot(w_one_t[...], stack[:, : 4 * Z])
        for y in range(4):
            grad_input[x, y * C : (y + 1) * C, :] = tap_sum(prod, y, C, Z, True).astype(BF)
        return carry

    lax.fori_loop(0, 4, step_one, 0)


def call(kernel, outs, scratch, n_smem, flops, *args):
    vmem = pl.BlockSpec(memory_space=pltpu.VMEM)
    smem = pl.BlockSpec(memory_space=pltpu.SMEM)
    moved = sum(a.size * a.dtype.itemsize for a in args) + sum(
        o.size * o.dtype.itemsize for o in outs
    )
    return pl.pallas_call(
        kernel,
        out_shape=outs,
        in_specs=[smem] * n_smem + [vmem] * (len(args) - n_smem),
        out_specs=[vmem] * len(outs),
        scratch_shapes=scratch,
        compiler_params=pltpu.CompilerParams(vmem_limit_bytes=VMEM_LIMIT),
        cost_estimate=pl.CostEstimate(flops=flops, bytes_accessed=moved, transcendentals=0),
    )(*args)


def shape(dims, dtype=BF):
    return jax.ShapeDtypeStruct(dims, dtype)


def neighbours(array, axis):
    size = lax.axis_size(axis)
    up = [(i, i + 1) for i in range(size - 1)]
    down = [(j, i) for i, j in up]
    return lax.ppermute(array, axis, up), lax.ppermute(array, axis, down)


def shares(parts):
    devices = lax.axis_size("gx") * lax.axis_size("gy")
    rows = parts.shape[0] // devices
    got = lax.all_to_all(parts.reshape(devices, rows, Z), ALL, 0, 0, tiled=True)
    return jnp.sum(got.astype(F32), axis=0).astype(BF)


def gathered(mine):
    devices = lax.axis_size("gx") * lax.axis_size("gy")
    spread = jnp.broadcast_to(mine[None], (devices,) + mine.shape)
    return lax.all_to_all(spread, ALL, 0, 0, tiled=True)


def fine_grad(rows):
    part = jnp.transpose(rows.reshape(4, 144, Z), (1, 0, 2)).reshape(144, 512)[:, :432]
    part = part.reshape(3, 2, 24, 3, 3, 2, 24)
    own = jnp.stack([part[:, g, :, :, :, g, :] for g in range(2)], axis=1)
    return jnp.transpose(own, (3, 4, 0, 1, 2, 5)).reshape(3, 3, 3, 1152).astype(F32)


def per_device(features, conv_one, conv_two, down_weight, coarse_weight, cotangent):
    gx, gy = lax.axis_index("gx"), lax.axis_index("gy")
    last_x, last_y = lax.axis_size("gx") - 1, lax.axis_size("gy") - 1
    flags = jnp.stack([gx > 0, gx < last_x, gy > 0, gy < last_y]).astype(F32)

    feat = jnp.transpose(features, (1, 2, 0, 3)).reshape(4, 4 * C, Z)
    before, after = neighbours(feat, "gx")
    feat = jnp.concatenate([before, feat, after], axis=0)
    feat, cot = lax.optimization_barrier((feat, cotangent.astype(BF)))
    feat_l, feat_r = neighbours(feat, "gy")

    cot = lax.all_to_all(
        cot.reshape(12, 16, 2, Z), "gx", split_axis=1, concat_axis=0, tiled=True
    )
    cot = jnp.transpose(cot.reshape(CC, 2, Z), (1, 0, 2))

    one = conv_one.reshape(27, C, C // 2)
    two = conv_two.reshape(27, C, C // 2)
    down = down_weight.reshape(8, CD, C)
    w_coarse = coarse_weight.reshape(9, 3 * CC, CD)
    w_one, w_two, w_down = call(
        ahead_kernel, [shape((144, 432)), shape((144, 432)), shape((CD, 8 * C))], [], 0, 0,
        one, two, down,
    )

    act_one, slope_one, slope_two, down_own, coarse_in = call(
        fine_kernel,
        [
            shape((6, 6 * C, Z)), shape((6, 6 * C, Z), F32), shape((8, 8 * C, Z), F32),
            shape((2, 8 * C, Z)), shape((4, CD, 3 * Z)),
        ],
        [
            pltpu.VMEM((9 * C, 10 * Z), BF), pltpu.VMEM((10, 10 * C, Z), BF),
            pltpu.VMEM((6 * C, 2 * Z), BF), pltpu.VMEM((4, 8 * C, 3 * Z), BF),
        ],
        1, 16_000_000_000,
        flags, feat_l, feat, feat_r, w_one, w_two, w_down,
    )
    coarse_out, grad_three = call(
        coarse_kernel, [shape((2, CC, Z)), shape((2, CC, Z))], [], 0, 300_000_000,
        coarse_in, w_coarse, cot,
    )

    before, after = neighbours(grad_three, "gx")
    one, two, down, coarse_t, grad_three = lax.optimization_barrier(
        (one, two, down, w_coarse, grad_three)
    )
    w_one_t, w_two_t, w_down_t, w_coarse_t = call(
        back_kernel,
        [shape((144, 432)), shape((144, 432)), shape((4 * C, 2 * CD)), shape((9, 3 * CD, CC))],
        [], 0, 0, one, two, down, coarse_t,
    )
    (coarse_part,) = call(
        coarse_grad_kernel,
        [shape((4096, Z))],
        [pltpu.VMEM((2, 3, CC, Z), F32), pltpu.VMEM((3 * CC, 2 * Z), BF)],
        0, 500_000_000,
        grad_three, coarse_in,
    )
    wide = jnp.concatenate([before, grad_three, after], axis=0)
    g_l, g_r = neighbours(wide, "gy")
    out = lax.all_to_all(
        coarse_out.reshape(2, 16, 12, Z), "gx", split_axis=1, concat_axis=0, tiled=True
    )
    g_l, g_r, coarse_part, out = lax.optimization_barrier((g_l, g_r, coarse_part, out))
    out = jnp.transpose(out.reshape(32, 12, Z), (1, 0, 2))
    coarse_mine = shares(coarse_part)

    grad_input, small = call(
        backward_kernel,
        [shape((4, 4 * C, Z)), shape((1536, Z))],
        [
            pltpu.VMEM((3, 6, CC, 2 * Z), BF), pltpu.VMEM((2 * CD, 4 * Z), BF),
            pltpu.VMEM((8, 8 * C, Z), BF), pltpu.VMEM((6, 6 * C, Z), BF),
            pltpu.VMEM((9 * C, 16 * Z), BF), pltpu.VMEM((144, 16 * Z), BF),
        ],
        0, 12_000_000_000,
        g_l, wide, g_r, feat_l, feat, feat_r, act_one, slope_one, slope_two, down_own,
        w_one_t, w_two_t, w_down_t, w_coarse_t,
    )
    small, coarse_mine = lax.optimization_barrier((small, coarse_mine))
    sums = gathered(jnp.concatenate([coarse_mine, shares(small)], axis=0))
    small_sum = sums[:, 32:].reshape(1536, Z)

    grad_input = jnp.transpose(grad_input.reshape(4, 4, C, Z), (2, 0, 1, 3))
    grad_one = fine_grad(small_sum[:576])
    grad_two = fine_grad(small_sum[576:1152])
    grad_down = jnp.transpose(
        small_sum[1152:1440].reshape(3, CD, Z), (1, 0, 2)
    ).reshape(CD, 8, C)
    grad_down = jnp.swapaxes(grad_down, 0, 1).reshape(2, 2, 2, CD * C).astype(F32)
    (grad_coarse,) = call(
        final_kernel, [shape((3, 3, 3, CC * CD), F32)], [pltpu.VMEM((4096, Z), F32)], 0, 0,
        sums[:, :32].reshape(4096, Z),
    )
    return out, grad_input, grad_one, grad_two, grad_down, grad_coarse


def solution(mesh):
    placed = (P(None, "gx", "gy", None), P(), P(), P(), P(), P("gx", None, "gy"))
    return jax.shard_map(
        per_device,
        mesh=mesh,
        in_specs=placed,
        out_specs=(P("gx", None, "gy"), P(None, "gx", "gy", None), P(), P(), P(), P()),
        check_vma=False,
    )
```

time: 821 us -> 185 us (0.23); the launches traced: 808 us -> 184 us
  matrix products: 256 us -> 0 us
  local copies, waits for them, and re-layouts: 264 us -> 25.1 us
  waiting for transfers between devices: 189 us -> 40.7 us
  Pallas kernels: 0 us -> 37.9 us
  blocking collectives: 0 us -> 19.9 us
  between operations: 16.1 us -> 1.13 us
  starting transfers between devices: 70.7 us -> 56.6 us
  other arithmetic: 12.4 us -> 2.86 us
    conv_general_dilated x6 -> x0, matrix products: 230 us -> none  [conv_valid(): lax.conv_general_dilated(field[None], kernel, (1, 1, 1), 'VALID', dimensi...]
    psum x1 -> x0, waiting for transfers between devices: 94.3 us -> none  [per_device(): lax.psum((as_flat(kernel_one), as_flat(kernel_two), as_flat(grad_down), a...]
    reshape x69 -> x14, local copies, waits for them, and re-layouts: 80.2 us -> 7.17 us  [the longest x1 2.81 us: per_device(): w_coarse = coarse_weight.reshape(9, 3 * CC, CD)]
    reduce_scatter x1 -> x0, waiting for transfers between devices: 70.1 us -> none  [per_device(): lax.psum_scatter(conv_valid(rim_coarse, own_part, 1).astype(jnp.bfloat16)...]
    broadcast_in_dim x7 -> x1, local copies, waits for them, and re-layouts: 43.7 us -> 1.35 us  [gathered(): spread = jnp.broadcast_to(mine[None], (devices,) + mine.shape)]
    pallas_call x0 -> x7, Pallas kernels: none -> 37.9 us  [call(): pl.pallas_call(kernel, out_shape=outs, in_specs=[smem] * n_smem + [vmem]...]
    slice x61 -> x4, local copies, waits for them, and re-layouts: 38.2 us -> 1.27 us  [the longest x2 1.17 us: fine_grad(): own = jnp.stack([part[:, g, :, :, :, g, :] for g in range(2)], axis=1)]
    unnamed x263 -> x40, local copies, waits for them, and re-layouts: 42.9 us -> 8.13 us
  transfers between devices with their start and end apart: 25 -> 12, of which waited for: 11 -> 7; matrix products, arithmetic and copies ran while one was open for 27% -> 5% of each run, Pallas kernels for 0% -> 9%
where the time goes in v1:
time: 185 us; the launch traced here: 184 us
  starting transfers between devices  56.6 us (31%)
  waiting for transfers between devices  40.7 us (22%)
  Pallas kernels  37.9 us (20%)
  local copies, waits for them, and re-layouts  25.1 us (14%)
  blocking collectives  19.9 us (11%)
  other arithmetic  2.86 us (2%)
    pallas_call x7, Pallas kernels, call(): pl.pallas_call(kernel, out_shape=outs, in_specs=[smem] * n_smem + [vmem]...  37.9 us
    all_to_all x1, waiting for transfers between devices, gathered(): return lax.all_to_all(spread, ALL, 0, 0, tiled=True)  24.2 us
    ppermute x8, starting transfers between devices, neighbours(): return (lax.ppermute(array, axis, up), lax.ppermute(array, axis, down))  23.6 us
    all_to_all x1, blocking collectives, shares(): got = lax.all_to_all(parts.reshape(devices, rows, Z), ALL, 0, 0, tiled=True)  19.9 us
    all_to_all x1, starting transfers between devices, per_device(): lax.all_to_all(cot.reshape(12, 16, 2, Z), 'gx', split_axis=1, concat_axis...  10.7 us
    all_to_all x1, starting transfers between devices, shares(): got = lax.all_to_all(parts.reshape(devices, rows, Z), ALL, 0, 0, tiled=True)  10.3 us
    unnamed x40, local copies, waits for them, and re-layouts  8.13 us
    all_to_all x1, starting transfers between devices, per_device(): lax.all_to_all(coarse_out.reshape(2, 16, 12, Z), 'gx', split_axis=1, conc...  7.47 us
  transfers between devices with their start and end apart: 12, of which 7 were waited for; matrix products, arithmetic and copies ran while one was open for 5% of the time, Pallas kernels for 9%

profile of v1, /device:TPU:1, one launch (start us, length us, event | category | flops | bytes accessed | tf_op | source)
XLA Modules:
  0.0 184.2 jit_solution(1674594307470189645)
XLA Ops:
  3.0 5.0 %collective-permute-start = (bf16[4,192,128]{2,1,0:T(8,128)(2,1)S(1)}, bf16[4,192,128]{2,1,0:T(8,128)(2,1)S(1)}, u32[]{:S(2)}, u32[]{:S(2)}) collective-permute-start(bf16[4,192,128]{2,1,0:T(8,128)(2,1)S(1)} %bitcast.67), channel_id=1, source_target_pairs={{0,8},{8,16},{16,24},{24,32},{32,40},{40,48},{48,56},{56,64},{64,7... | collective-permute-start | bytes 589832 | tf_op jit(solution)/shard_map/ppermute | solution.py:385
  9.0 1.7 collective-permute-done.1
  11.6 3.5 %collective-permute-start.3 = (bf16[12,192,128]{2,1,0:T(8,128)(2,1)S(1)}, bf16[12,192,128]{2,1,0:T(8,128)(2,1)}, u32[]{:S(2)}, u32[]{:S(2)}) collective-permute-start(bf16[12,192,128]{2,1,0:T(8,128)(2,1)S(1)} %pad_maximum_fusion.feat_m), channel_id=1, source_target_pairs={{1,0},{2,1},{3,2},{4,3},{5,4},{6,5},{7,6},{9,8},{10,9},{11,10},{12... | collective-permute-start | bytes 1769480 | tf_op jit(solution)/shard_map/ppermute | solution.py:385
  15.1 3.0 %collective-permute-start.2 = (bf16[12,192,128]{2,1,0:T(8,128)(2,1)S(1)}, bf16[12,192,128]{2,1,0:T(8,128)(2,1)}, u32[]{:S(2)}, u32[]{:S(2)}) collective-permute-start(bf16[12,192,128]{2,1,0:T(8,128)(2,1)S(1)} %pad_maximum_fusion.feat_m), channel_id=1, source_target_pairs={{0,1},{1,2},{2,3},{3,4},{4,5},{5,6},{6,7},{8,9},{9,10},{10,11},{11... | collective-permute-start | bytes 1769480 | tf_op jit(solution)/shard_map/ppermute | solution.py:385
  19.3 2.8 %reshape.97.w_coarse.coarse = bf16[9,576,96]{2,1,0:T(8,128)(2,1)S(1)} reshape(bf16[3,3,3,18432]{3,2,1,0:T(4,128)(2,1)} %param.10) | data formatting | bytes 1990656 | tf_op jit(solution)/shard_map/reshape | solution.py:427
  23.2 10.7 %all-to-all-start = ((bf16[12,16,2,128]{3,2,0,1:T(2,128)(2,1)}), bf16[12,16,2,128]{3,2,0,1:T(2,128)(2,1)S(1)}, u32[]{:S(2)}, u32[]{:S(2)}) async-start(bf16[12,16,2,128]{3,2,0,1:T(2,128)(2,1)} %copy.46), calls=%async_computation | async-start | bytes 196608 | tf_op jit(solution)/shard_map/all_to_all | solution.py:419
  34.0 6.5 %all-to-all-done = bf16[12,16,2,128]{3,2,0,1:T(2,128)(2,1)S(1)} async-done(((bf16[12,16,2,128]{3,2,0,1:T(2,128)(2,1)}), bf16[12,16,2,128]{3,2,0,1:T(2,128)(2,1)S(1)}, u32[]{:S(2)}, u32[]{:S(2)}) %all-to-all-start) | async-done | bytes 98336 | tf_op jit(solution)/shard_map/all_to_all | solution.py:419
  40.6 17.0 %shard_map.110 = (bf16[6,288,128]{2,1,0:T(8,128)(2,1)S(1)}, f32[6,288,128]{2,1,0:T(8,128)S(1)}, f32[8,384,128]{2,1,0:T(8,128)S(1)}, bf16[2,384,128]{2,1,0:T(8,128)(2,1)S(1)}, bf16[4,96,384]{2,1,0:T(8,128)(2,1)S(1)}) custom-call(f32[4]{0:T(128)S(1)} %add_convert_fusion.flags, bf16[12,192,128]{2,1,0:T(8,128)(2,1)} %collective-permute-done.2.feat_l, ...), custom_call_target="tpu_custom_call" | custom-call | flops 16000000000 | bytes 5483536 | tf_op jit(solution)/shard_map/pallas_call | solution.py:366
  60.0 2.2 %collective-permute-start.4 = (bf16[2,192,128]{2,1,0:T(8,128)(2,1)S(1)}, bf16[2,192,128]{2,1,0:T(8,128)(2,1)S(1)}, u32[]{:S(2)}, u32[]{:S(2)}) collective-permute-start(bf16[2,192,128]{2,1,0:T(8,128)(2,1)S(1)} %get-tuple-element.42.grad_three), channel_id=1, source_target_pairs={{0,8},{8,16},{16,24},{24,32},{32,40},{40,48},{48,56},{56,64},{64,7... | collective-permute-start | bytes 294920 | tf_op jit(solution)/shard_map/ppermute | solution.py:385
  63.9 3.7 %collective-permute-done.5 = bf16[2,192,128]{2,1,0:T(8,128)(2,1)S(1)} collective-permute-done((bf16[2,192,128]{2,1,0:T(8,128)(2,1)S(1)}, bf16[2,192,128]{2,1,0:T(8,128)(2,1)S(1)}, u32[]{:S(2)}, u32[]{:S(2)}) %collective-permute-start.5) | collective-permute-done | bytes 98336 | tf_op jit(solution)/shard_map/ppermute | solution.py:385
  67.6 4.9 %collective-permute-start.7 = (bf16[6,192,128]{2,1,0:T(8,128)(2,1)S(1)}, bf16[6,192,128]{2,1,0:T(8,128)(2,1)}, u32[]{:S(2)}, u32[]{:S(2)}) collective-permute-start(bf16[6,192,128]{2,1,0:T(8,128)(2,1)S(1)} %constant_dynamic-update-slice_fusion.g_m), channel_id=1, source_target_pairs={{1,0},{2,1},{3,2},{4,3},{5,4},{6,5},{7,6},{9,8},{10,9},{11,10},{12... | collective-permute-start | bytes 884744 | tf_op jit(solution)/shard_map/ppermute | solution.py:385
  72.5 2.4 %collective-permute-start.6 = (bf16[6,192,128]{2,1,0:T(8,128)(2,1)S(1)}, bf16[6,192,128]{2,1,0:T(8,128)(2,1)}, u32[]{:S(2)}, u32[]{:S(2)}) collective-permute-start(bf16[6,192,128]{2,1,0:T(8,128)(2,1)S(1)} %constant_dynamic-update-slice_fusion.g_m), channel_id=1, source_target_pairs={{0,1},{1,2},{2,3},{3,4},{4,5},{5,6},{6,7},{8,9},{9,10},{10,11},{11... | collective-permute-start | bytes 884744 | tf_op jit(solution)/shard_map/ppermute | solution.py:385
  75.7 7.5 %all-to-all-start.1 = ((bf16[2,16,12,128]{3,0,2,1:T(2,128)(2,1)}), bf16[2,16,12,128]{3,0,2,1:T(2,128)(2,1)}, u32[]{:S(2)}, u32[]{:S(2)}) async-start(bf16[2,16,12,128]{3,0,2,1:T(2,128)(2,1)} %bitcast.73), calls=%async_computation.1 | async-start | bytes 196608 | tf_op jit(solution)/shard_map/all_to_all | solution.py:469
  83.2 3.0 %shard_map.113 = (bf16[144,432]{1,0:T(8,128)(2,1)S(1)}, bf16[144,432]{1,0:T(8,128)(2,1)S(1)}, bf16[192,192]{1,0:T(8,128)(2,1)S(1)}, bf16[9,288,192]{2,1,0:T(8,128)(2,1)S(1)}) custom-call(bf16[27,48,24]{2,1,0:T(8,128)(2,1)S(1)} %reshape.94.one, bf16[27,48,24]{2,1,0:T(8,128)(2,1)S(1)} %reshape.95.two, bf16[8,96,48]{2,1,0:T(8,128)(2,1)S(1)} %reshape.96.down, ...), custom_call_target="tpu_custom_call" | custom-call | bytes 2511360 | tf_op jit(solution)/shard_map/pallas_call | solution.py:366
  89.3 2.0 %shard_map.112 = bf16[4096,128]{1,0:T(8,128)(2,1)} custom-call(bf16[2,192,128]{2,1,0:T(8,128)(2,1)S(1)} %get-tuple-element.42.grad_three, bf16[4,96,384]{2,1,0:T(8,128)(2,1)S(1)} %get-tuple-element.39.coarse_in), custom_call_target="tpu_custom_call" | custom-call | flops 500000000 | bytes 1441792 | tf_op jit(solution)/shard_map/pallas_call | solution.py:366
  91.3 1.7 copy.49
  93.0 10.3 %all-to-all-start.2 = ((bf16[128,32,128]{2,1,0:T(8,128)(2,1)}), bf16[128,32,128]{2,1,0:T(8,128)(2,1)}, u32[]{:S(2)}, u32[]{:S(2)}) async-start(bf16[128,32,128]{2,1,0:T(8,128)(2,1)} %bitcast.19), calls=%async_computation.2 | async-start | bytes 2097152 | tf_op jit(solution)/shard_map/all_to_all | solution.py:391
  107.0 11.9 %shard_map.114 = (bf16[4,192,128]{2,1,0:T(8,128)(2,1)S(1)}, bf16[1536,128]{1,0:T(8,128)(2,1)S(1)}) custom-call(bf16[6,192,128]{2,1,0:T(8,128)(2,1)} %collective-permute-done.6.g_l, bf16[6,192,128]{2,1,0:T(8,128)(2,1)S(1)} %constant_dynamic-update-slice_fusion.g_m, bf16[6,192,128]{2,1,0:T(8,128)(2,1)} %collective-permute-done.7.g_r, ...), custom_call_target="tpu_custom_call" | custom-call | flops 12000000000 | bytes 7658496 | tf_op jit(solution)/shard_map/pallas_call | solution.py:366
  118.9 3.4 %all-to-all-done.2 = bf16[128,32,128]{2,1,0:T(8,128)(2,1)} async-done(((bf16[128,32,128]{2,1,0:T(8,128)(2,1)}), bf16[128,32,128]{2,1,0:T(8,128)(2,1)}, u32[]{:S(2)}, u32[]{:S(2)}) %all-to-all-start.2) | async-done | bytes 1048608 | tf_op jit(solution)/shard_map/all_to_all | solution.py:391
  122.3 1.4 reduce_sum.24
  123.8 19.9 %all_to_all.48 = bf16[128,12,128]{2,1,0:T(8,128)(2,1)S(1)} all-to-all(bf16[128,12,128]{2,1,0:T(8,128)(2,1)S(1)} %reshape.104), channel_id=1, replica_groups=mesh['gx'=16,'gy'=8] {'gx','gy'}, dimensions={0} | all-to-all | bytes 786432 | tf_op jit(solution)/shard_map/all_to_all | solution.py:391
  145.2 4.5 %all-to-all-start.4 = ((bf16[128,44,128]{2,1,0:T(8,128)(2,1)}), bf16[128,44,128]{2,1,0:T(8,128)(2,1)S(1)}, u32[]{:S(2)}, u32[]{:S(2)}) async-start(bf16[128,44,128]{2,1,0:T(8,128)(2,1)} %broadcast_in_dim.2), calls=%async_computation.4 | async-start | bytes 3145728 | tf_op jit(solution)/shard_map/all_to_all | solution.py:398
  150.5 24.2 %all-to-all-done.4 = bf16[128,44,128]{2,1,0:T(8,128)(2,1)S(1)} async-done(((bf16[128,44,128]{2,1,0:T(8,128)(2,1)}), bf16[128,44,128]{2,1,0:T(8,128)(2,1)S(1)}, u32[]{:S(2)}, u32[]{:S(2)}) %all-to-all-start.4) | async-done | bytes 1441824 | tf_op jit(solution)/shard_map/all_to_all | solution.py:398
  181.6 2.6 %shard_map.115 = f32[3,3,3,18432]{3,2,1,0:T(4,128)} custom-call(bf16[4096,128]{1,0:T(8,128)(2,1)S(1)} %bitcast.63), custom_call_target="tpu_custom_call" | custom-call | bytes 3039232 | tf_op jit(solution)/shard_map/pallas_call | solution.py:366
  (90 shorter events, 27.1 us)
Async XLA Ops:
  0.6 17.5 %copy-start.18 = (bf16[2,2,2,4608]{3,2,1,0:T(2,128)(2,1)S(1)}, bf16[2,2,2,4608]{3,2,1,0:T(2,128)(2,1)}, u32[]{:S(2)}) copy-start(bf16[2,2,2,4608]{3,2,1,0:T(2,128)(2,1)} %param.9) | copy-start | bytes 221188
  0.6 17.7 %copy-start.16 = (bf16[3,3,3,1152]{3,2,1,0:T(4,128)(2,1)S(1)}, bf16[3,3,3,1152]{3,2,1,0:T(4,128)(2,1)}, u32[]{:S(2)}) copy-start(bf16[3,3,3,1152]{3,2,1,0:T(4,128)(2,1)} %param.7) | copy-start | bytes 186628
  0.7 18.2 %copy-start.17 = (bf16[3,3,3,1152]{3,2,1,0:T(4,128)(2,1)S(1)}, bf16[3,3,3,1152]{3,2,1,0:T(4,128)(2,1)}, u32[]{:S(2)}) copy-start(bf16[3,3,3,1152]{3,2,1,0:T(4,128)(2,1)} %param.8) | copy-start | bytes 186628
  1.7 9.0 %collective-permute-start.1 = (bf16[4,192,128]{2,1,0:T(8,128)(2,1)S(1)}, bf16[4,192,128]{2,1,0:T(8,128)(2,1)S(1)}, u32[]{:S(2)}, u32[]{:S(2)}) collective-permute-start(bf16[4,192,128]{2,1,0:T(8,128)(2,1)S(1)} %bitcast.66), channel_id=1, source_target_pairs={{8,0},{16,8},{24,16},{32,24},{40,32},{48,40},{56,48},{64,56},{72,6... | collective-permute-start | bytes 589832 | tf_op jit(solution)/shard_map/ppermute | solution.py:385
  3.0 8.5 %collective-permute-start = (bf16[4,192,128]{2,1,0:T(8,128)(2,1)S(1)}, bf16[4,192,128]{2,1,0:T(8,128)(2,1)S(1)}, u32[]{:S(2)}, u32[]{:S(2)}) collective-permute-start(bf16[4,192,128]{2,1,0:T(8,128)(2,1)S(1)} %bitcast.67), channel_id=1, source_target_pairs={{0,8},{8,16},{16,24},{24,32},{32,40},{40,48},{48,56},{56,64},{64,7... | collective-permute-start | bytes 589832 | tf_op jit(solution)/shard_map/ppermute | solution.py:385
  11.6 29.0 %collective-permute-start.3 = (bf16[12,192,128]{2,1,0:T(8,128)(2,1)S(1)}, bf16[12,192,128]{2,1,0:T(8,128)(2,1)}, u32[]{:S(2)}, u32[]{:S(2)}) collective-permute-start(bf16[12,192,128]{2,1,0:T(8,128)(2,1)S(1)} %pad_maximum_fusion.feat_m), channel_id=1, source_target_pairs={{1,0},{2,1},{3,2},{4,3},{5,4},{6,5},{7,6},{9,8},{10,9},{11,10},{12... | collective-permute-start | bytes 1769480 | tf_op jit(solution)/shard_map/ppermute | solution.py:385
  15.1 25.5 %collective-permute-start.2 = (bf16[12,192,128]{2,1,0:T(8,128)(2,1)S(1)}, bf16[12,192,128]{2,1,0:T(8,128)(2,1)}, u32[]{:S(2)}, u32[]{:S(2)}) collective-permute-start(bf16[12,192,128]{2,1,0:T(8,128)(2,1)S(1)} %pad_maximum_fusion.feat_m), channel_id=1, source_target_pairs={{0,1},{1,2},{2,3},{3,4},{4,5},{5,6},{6,7},{8,9},{9,10},{10,11},{11... | collective-permute-start | bytes 1769480 | tf_op jit(solution)/shard_map/ppermute | solution.py:385
  23.2 17.3 %all-to-all-start = ((bf16[12,16,2,128]{3,2,0,1:T(2,128)(2,1)}), bf16[12,16,2,128]{3,2,0,1:T(2,128)(2,1)S(1)}, u32[]{:S(2)}, u32[]{:S(2)}) async-start(bf16[12,16,2,128]{3,2,0,1:T(2,128)(2,1)} %copy.46), calls=%async_computation | async-start | bytes 196608 | tf_op jit(solution)/shard_map/all_to_all | solution.py:419
  59.0 16.6 %copy-start.8 = (f32[8,384,128]{2,1,0:T(8,128)}, f32[8,384,128]{2,1,0:T(8,128)S(1)}, u32[]{:S(2)}) copy-start(f32[8,384,128]{2,1,0:T(8,128)S(1)} %get-tuple-element.49.slope_two) | copy-start | bytes 4718596
  59.0 16.6 %copy-start.10 = (f32[6,288,128]{2,1,0:T(8,128)}, f32[6,288,128]{2,1,0:T(8,128)S(1)}, u32[]{:S(2)}) copy-start(f32[6,288,128]{2,1,0:T(8,128)S(1)} %get-tuple-element.48.slope_one) | copy-start | bytes 2654212
  60.0 3.9 %collective-permute-start.4 = (bf16[2,192,128]{2,1,0:T(8,128)(2,1)S(1)}, bf16[2,192,128]{2,1,0:T(8,128)(2,1)S(1)}, u32[]{:S(2)}, u32[]{:S(2)}) collective-permute-start(bf16[2,192,128]{2,1,0:T(8,128)(2,1)S(1)} %get-tuple-element.42.grad_three), channel_id=1, source_target_pairs={{0,8},{8,16},{16,24},{24,32},{32,40},{40,48},{48,56},{56,64},{64,7... | collective-permute-start | bytes 294920 | tf_op jit(solution)/shard_map/ppermute | solution.py:385
  62.2 5.4 %collective-permute-start.5 = (bf16[2,192,128]{2,1,0:T(8,128)(2,1)S(1)}, bf16[2,192,128]{2,1,0:T(8,128)(2,1)S(1)}, u32[]{:S(2)}, u32[]{:S(2)}) collective-permute-start(bf16[2,192,128]{2,1,0:T(8,128)(2,1)S(1)} %get-tuple-element.42.grad_three), channel_id=1, source_target_pairs={{8,0},{16,8},{24,16},{32,24},{40,32},{48,40},{56,48},{64,56},{72,6... | collective-permute-start | bytes 294920 | tf_op jit(solution)/shard_map/ppermute | solution.py:385
  67.6 25.4 %collective-permute-start.7 = (bf16[6,192,128]{2,1,0:T(8,128)(2,1)S(1)}, bf16[6,192,128]{2,1,0:T(8,128)(2,1)}, u32[]{:S(2)}, u32[]{:S(2)}) collective-permute-start(bf16[6,192,128]{2,1,0:T(8,128)(2,1)S(1)} %constant_dynamic-update-slice_fusion.g_m), channel_id=1, source_target_pairs={{1,0},{2,1},{3,2},{4,3},{5,4},{6,5},{7,6},{9,8},{10,9},{11,10},{12... | collective-permute-start | bytes 884744 | tf_op jit(solution)/shard_map/ppermute | solution.py:385
  72.5 20.5 %collective-permute-start.6 = (bf16[6,192,128]{2,1,0:T(8,128)(2,1)S(1)}, bf16[6,192,128]{2,1,0:T(8,128)(2,1)}, u32[]{:S(2)}, u32[]{:S(2)}) collective-permute-start(bf16[6,192,128]{2,1,0:T(8,128)(2,1)S(1)} %constant_dynamic-update-slice_fusion.g_m), channel_id=1, source_target_pairs={{0,1},{1,2},{2,3},{3,4},{4,5},{5,6},{6,7},{8,9},{9,10},{10,11},{11... | collective-permute-start | bytes 884744 | tf_op jit(solution)/shard_map/ppermute | solution.py:385
  75.7 15.6 %all-to-all-start.1 = ((bf16[2,16,12,128]{3,0,2,1:T(2,128)(2,1)}), bf16[2,16,12,128]{3,0,2,1:T(2,128)(2,1)}, u32[]{:S(2)}, u32[]{:S(2)}) async-start(bf16[2,16,12,128]{3,0,2,1:T(2,128)(2,1)} %bitcast.73), calls=%async_computation.1 | async-start | bytes 196608 | tf_op jit(solution)/shard_map/all_to_all | solution.py:469
  91.3 12.1 %copy-start.1 = (bf16[9,288,192]{2,1,0:T(8,128)(2,1)S(1)}, bf16[9,288,192]{2,1,0:T(8,128)(2,1)}, u32[]{:S(2)}) copy-start(bf16[9,288,192]{2,1,0:T(8,128)(2,1)} %copy-done) | copy-start | bytes 2985988
  91.3 12.1 %copy-start.3 = (bf16[144,432]{1,0:T(8,128)(2,1)S(1)}, bf16[144,432]{1,0:T(8,128)(2,1)}, u32[]{:S(2)}) copy-start(bf16[144,432]{1,0:T(8,128)(2,1)} %copy-done.2) | copy-start | bytes 373252
  91.3 12.1 %copy-start.5 = (bf16[144,432]{1,0:T(8,128)(2,1)S(1)}, bf16[144,432]{1,0:T(8,128)(2,1)}, u32[]{:S(2)}) copy-start(bf16[144,432]{1,0:T(8,128)(2,1)} %copy-done.4) | copy-start | bytes 373252
  91.3 12.1 %copy-start.7 = (bf16[192,192]{1,0:T(8,128)(2,1)S(1)}, bf16[192,192]{1,0:T(8,128)(2,1)}, u32[]{:S(2)}) copy-start(bf16[192,192]{1,0:T(8,128)(2,1)} %copy-done.6) | copy-start | bytes 221188
  91.3 12.1 %copy-start.15 = (bf16[2,384,128]{2,1,0:T(8,128)(2,1)S(1)}, bf16[2,384,128]{2,1,0:T(8,128)(2,1)}, u32[]{:S(2)}) copy-start(bf16[2,384,128]{2,1,0:T(8,128)(2,1)} %copy-done.14) | copy-start | bytes 589828
  93.0 29.3 %all-to-all-start.2 = ((bf16[128,32,128]{2,1,0:T(8,128)(2,1)}), bf16[128,32,128]{2,1,0:T(8,128)(2,1)}, u32[]{:S(2)}, u32[]{:S(2)}) async-start(bf16[128,32,128]{2,1,0:T(8,128)(2,1)} %bitcast.19), calls=%async_computation.2 | async-start | bytes 2097152 | tf_op jit(solution)/shard_map/all_to_all | solution.py:391
  103.4 1.4 copy-start.9
  104.8 1.2 copy-start.11
  145.2 29.4 %all-to-all-start.4 = ((bf16[128,44,128]{2,1,0:T(8,128)(2,1)}), bf16[128,44,128]{2,1,0:T(8,128)(2,1)S(1)}, u32[]{:S(2)}, u32[]{:S(2)}) async-start(bf16[128,44,128]{2,1,0:T(8,128)(2,1)} %broadcast_in_dim.2), calls=%async_computation.4 | async-start | bytes 3145728 | tf_op jit(solution)/shard_map/all_to_all | solution.py:398
  (7 other events, 5.5 us)

commit v2 on v1

--- a/solution.py
+++ b/solution.py
@@ -11,8 +11,9 @@
 CD = 96
 CC = 192
 Z = 128
-ALL = ("gx", "gy")
-VMEM_LIMIT = 24 * 1024 * 1024
+GY = ("x", "core")
+ALL = ("gx", "x", "core")
+SAME_CORE = ("gx", "x")
 
 
 def dot(a, b):
@@ -53,11 +54,37 @@
 
 
 def fine_kernel(
-    flags, feat_l, feat_m, feat_r, w_one, w_two, w_down,
-    act_one, slope_one, slope_two, down_own, coarse_in,
-    stack, field, rows_two, down_all,
+    flags, feat_l, feat_m, feat_r, one, two, down,
+    kept_six, kept_eight, coarse_in,
+    w_one, w_two, w_down, stack, field, rows_two, down_all, slope_a, slope_b, sems,
 ):
     feats = (feat_l, feat_m, feat_r)
+    inner = pl.ds(3, 6)
+    copies = [
+        pltpu.make_async_copy(
+            feat_l.at[inner, pl.ds(3 * C, C), :], kept_six.at[pl.ds(12, 6), pl.ds(0, C), :], sems.at[0]
+        ),
+        pltpu.make_async_copy(
+            feat_m.at[inner], kept_six.at[pl.ds(12, 6), pl.ds(C, 4 * C), :], sems.at[1]
+        ),
+        pltpu.make_async_copy(
+            feat_r.at[inner, pl.ds(0, C), :], kept_six.at[pl.ds(12, 6), pl.ds(5 * C, C), :], sems.at[2]
+        ),
+        pltpu.make_async_copy(
+            field.at[pl.ds(2, 6), pl.ds(2 * C, 6 * C), :], kept_six.at[pl.ds(0, 6)], sems.at[3]
+        ),
+        pltpu.make_async_copy(slope_a, kept_six.at[pl.ds(6, 6)], sems.at[4]),
+        pltpu.make_async_copy(slope_b, kept_eight.at[pl.ds(0, 8)], sems.at[5]),
+        pltpu.make_async_copy(
+            down_all.at[pl.ds(1, 2), :, pl.ds(Z, Z)], kept_eight.at[pl.ds(8, 2)], sems.at[6]
+        ),
+    ]
+    for copy in copies[:3]:
+        copy.start()
+    for taps, w in ((one, w_one), (two, w_two)):
+        for c in range(3):
+            w[c * C : (c + 1) * C, :] = grouped(taps, c).astype(BF)
+    w_down[...] = jnp.concatenate([down[k].astype(F32) for k in range(8)], axis=1).astype(BF)
 
     def valid(x, lo, hi):
         ok_l = jnp.where(x < lo, flags[0], 1.0)
@@ -86,16 +113,17 @@
             act = (pre * sig * ok).astype(BF)
             field[x, y * C : (y + 1) * C, :] = act
             if 2 <= y < 8:
-                slp = sig * (1.0 + pre * (1.0 - sig)) * ok
+                slp = (sig * (1.0 + pre * (1.0 - sig)) * ok).astype(BF)
 
                 @pl.when(jnp.logical_and(x >= 2, x < 8))
                 def _():
-                    act_one[x - 2, (y - 2) * C : (y - 1) * C, :] = act
-                    slope_one[x - 2, (y - 2) * C : (y - 1) * C, :] = slp
+                    slope_a[x - 2, (y - 2) * C : (y - 1) * C, :] = slp
 
         return carry
 
     lax.fori_loop(0, 10, step_one, 0)
+    copies[3].start()
+    copies[4].start()
 
     row = lax.broadcasted_iota(jnp.int32, (2 * Z, 2 * Z), 0)
     col = lax.broadcasted_iota(jnp.int32, (2 * Z, 2 * Z), 1)
@@ -116,7 +144,7 @@
             sig = sigmoid(pre)
             ok = ok_x * valid_y(y, 2, 6)
             act = (pre * sig * ok).astype(BF)
-            slope_two[x, y * C : (y + 1) * C, :] = sig * (1.0 + pre * (1.0 - sig)) * ok
+            slope_b[x, y * C : (y + 1) * C, :] = (sig * (1.0 + pre * (1.0 - sig)) * ok).astype(BF)
             pair, b = y // 2, y % 2
             if pair < 3:
                 rows_two[(pair * 2 + b) * C : (pair * 2 + b + 1) * C, :Z] = act
@@ -134,11 +162,12 @@
         return carry
 
     lax.fori_loop(0, 8, step_two, 0)
-
-    for x in range(2):
-        down_own[x] = down_all[x + 1, :, Z : 2 * Z]
+    copies[5].start()
+    copies[6].start()
     for x in range(4):
         coarse_in[x] = dot(w_down[...], down_all[x]).astype(BF)
+    for copy in copies:
+        copy.wait()
 
 
 def coarse_kernel(coarse_in, w_coarse, cot, coarse_out, grad_three):
@@ -165,14 +194,14 @@
     return jnp.concatenate(parts, axis=1)
 
 
-def ahead_kernel(one, two, down, w_one, w_two, w_down):
-    for taps, out in ((one, w_one), (two, w_two)):
-        for c in range(3):
-            out[c * C : (c + 1) * C, :] = grouped(taps, c).astype(BF)
-    w_down[...] = jnp.concatenate([down[k].astype(F32) for k in range(8)], axis=1).astype(BF)
-
-
-def back_kernel(one, two, down, coarse, w_one_t, w_two_t, w_down_t, w_coarse_t):
+def back_kernel(one, two, down, coarse, one_out, two_out, down_out, coarse_out,
+                w_one_t, w_two_t, w_down_t, w_coarse_t, sems):
+    copies = [
+        pltpu.make_async_copy(src, dst, sems.at[k])
+        for k, (src, dst) in enumerate((
+            (w_one_t, one_out), (w_two_t, two_out), (w_down_t, down_out), (w_coarse_t, coarse_out)
+        ))
+    ]
     for taps, out in ((one, w_one_t), (two, w_two_t)):
         for c in range(3):
             turned = grouped(taps, c).T
@@ -191,16 +220,60 @@
             )
         return carry
 
+    for copy in copies[:3]:
+        copy.start()
     lax.fori_loop(0, 9, turn, 0)
-
-
-def final_kernel(rows, out, wide):
-    wide[...] = rows[...].astype(F32)
+    copies[3].start()
+    for copy in copies:
+        copy.wait()
+
+
+def final_kernel(core, got, other, out, out_one, out_two, out_down, wide, small, lined):
+    for c in range(2):
+        for mine, rows in ((True, got), (False, other)):
+
+            @pl.when((core[0] == c) == mine)
+            def _():
+                for j in range(64):
+                    at = c * 2048 + j * 32
+                    wide[at : at + 32, :] = rows[j, :32, :].astype(F32)
+                    at = c * 512 + j * 8
+                    small[at : at + 8, :] = rows[j, 32:, :].astype(F32)
+
     for ab in range(9):
         for r in range(144):
             q, s = r // 3, r % 3
             out[ab // 3, ab % 3, :, r * Z : (r + 1) * Z] = wide[
                 pl.ds(ab * 432 + s * 48 + q, 3, stride=144), :
+            ]
+
+    for base, result in ((0, out_one), (288, out_two)):
+        picked = [
+            jnp.concatenate(
+                [small[pl.ds(base + s * 144 + k, 9, stride=16), :] for s in range(2)], axis=1
+            )
+            for k in range(16)
+        ]
+        for ab in range(9):
+            line = jnp.concatenate([p[:, ab * 24 : (ab + 1) * 24] for p in picked], axis=1)
+            for s in range(3):
+                lined[s, :9, :] = line[:, s * Z : (s + 1) * Z]
+                for k in range(3):
+                    at = k * 384 + s * Z
+                    result[ab // 3, ab % 3, :, at : at + Z] = lined[
+                        s, pl.ds(k, 3, stride=3), :
+                    ]
+    picked = [
+        jnp.concatenate(
+            [small[pl.ds(576 + s * CD + k, 12, stride=8), :] for s in range(3)], axis=1
+        )
+        for k in range(8)
+    ]
+    for abc in range(8):
+        line = jnp.concatenate([p[:, abc * C : (abc + 1) * C] for p in picked], axis=1)
+        for k in range(12):
+            out_down[abc // 4, abc // 2 % 2, abc % 2 : abc % 2 + 1, k * 384 : (k + 1) * 384] = line[
+                k : k + 1, :
             ]
 
 
@@ -234,11 +307,23 @@
 
 
 def backward_kernel(
-    g_l, g_m, g_r, feat_l, feat_m, feat_r, act_one, slope_one, slope_two, down_own,
-    w_one_t, w_two_t, w_down_t, w_coarse_t,
-    grad_input, small,
-    halves, spread, mid_two, mid_one, stack, left,
+    g_l, g_m, g_r, coarse_hbm, down_hbm, two_hbm, kept_six, kept_eight,
+    mid_out, small,
+    w_coarse_t, down_own, w_down_t, slope_two, act_one, w_two_t, slope_one, feat_six,
+    halves, spread, mid_two, mid_one, stack, left, sems,
 ):
+    loads = [
+        pltpu.make_async_copy(src, dst, sems.at[k])
+        for k, (src, dst) in enumerate((
+            (coarse_hbm, w_coarse_t), (kept_eight.at[pl.ds(8, 2)], down_own),
+            (down_hbm, w_down_t), (kept_eight.at[pl.ds(0, 8)], slope_two),
+            (kept_six.at[pl.ds(0, 6)], act_one), (two_hbm, w_two_t),
+            (kept_six.at[pl.ds(6, 6)], slope_one), (kept_six.at[pl.ds(12, 6)], feat_six),
+        ))
+    ]
+    for load in loads:
+        load.start()
+    store = pltpu.make_async_copy(mid_one, mid_out, sems.at[8])
     low = low_lanes((CC, Z))
 
     def prepare(x, carry):
@@ -260,6 +345,8 @@
     place = jnp.where(same & (col % Z == 2 * (row % (Z // 2)) + (col // Z) % 2), 1.0, 0.0).astype(BF)
     low_down = low_lanes((CD, Z))
 
+    for load in loads[:4]:
+        load.wait()
     grad_down = jnp.zeros((CD, 8 * C), F32)
     for x in range(4):
         total = jnp.zeros((3 * CD, 2 * Z), F32)
@@ -283,9 +370,13 @@
                 for y in range(4):
                     rows = slice((2 * y + b) * C, (2 * y + b + 1) * C)
                     part = fine[(a * 2 + b) * C : (a * 2 + b + 1) * C, y * Z : (y + 1) * Z]
-                    mid_two[2 * x + a, rows, :] = (part * slope_two[2 * x + a, rows, :]).astype(BF)
+                    mid_two[2 * x + a, rows, :] = (
+                        part * slope_two[2 * x + a, rows, :].astype(F32)
+                    ).astype(BF)
     for s in range(3):
-        small[1152 + s * CD : 1152 + (s + 1) * CD, :] = grad_down[:, s * Z : (s + 1) * Z].astype(BF)
+        small[576 + s * CD : 576 + (s + 1) * CD, :] = grad_down[:, s * Z : (s + 1) * Z].astype(BF)
+
+    small[864:, :] = jnp.zeros((1024 - 864, Z), BF)
 
     def kernel_grad(grad_of, field_of, at):
         for x in range(4):
@@ -303,17 +394,26 @@
                         if 0 <= x - a < 4 and 0 <= y - b < 4:
                             cell = (x - a) * 4 + (y - b)
                             stack[(a * 3 + b) * C : (a * 3 + b + 1) * C, cell * Z : (cell + 1) * Z] = piece
-        part = dot_t(left[...], stack[...]).astype(BF)
-        for s in range(3):
+        part = dot_t(left[...], stack[...])
+        row = lax.broadcasted_iota(jnp.int32, part.shape, 0)
+        col = lax.broadcasted_iota(jnp.int32, part.shape, 1)
+        part = jnp.where((row % C) // 24 == (col % C) // 24, part, 0.0).astype(BF)
+        row = lax.broadcasted_iota(jnp.int32, (432, 256), 0)
+        col = lax.broadcasted_iota(jnp.int32, (432, 256), 1)
+        fold = jnp.where((row // C == col // 24) & (row % 24 == col % 24), 1.0, 0.0).astype(BF)
+        part = dot(part, fold).astype(BF)
+        for s in range(2):
             small[at + s * 144 : at + (s + 1) * 144, :] = part[:, s * Z : (s + 1) * Z]
-        small[at + 432 : at + 576, :48] = part[:, 3 * Z :]
-        small[at + 432 : at + 576, 48:] = jnp.zeros((144, Z - 48), BF)
-
+
+    loads[4].wait()
     kernel_grad(
         lambda x, y: mid_two[x + 2, (y + 2) * C : (y + 3) * C, :],
         lambda x, y: act_one[x, y * C : (y + 1) * C, :],
-        576,
-    )
+        288,
+    )
+
+    loads[5].wait()
+    loads[6].wait()
 
     def step_two(x, carry):
         for a in range(3):
@@ -327,20 +427,22 @@
         for y in range(6):
             rows = slice(y * C, (y + 1) * C)
             grad = tap_sum(prod, y, C, Z, True)
-            mid_one[x, rows, :] = (grad * slope_one[x, rows, :]).astype(BF)
+            mid_one[x, rows, :] = (grad * slope_one[x, rows, :].astype(F32)).astype(BF)
         return carry
 
     lax.fori_loop(0, 6, step_two, 0)
 
-    feats = {-1: feat_l, 0: feat_m, 1: feat_r}
-
-    def feature(x, y):
-        fine_y = y - 1
-        block = fine_y // 4
-        return feats[block][x + 3, (fine_y % 4) * C : (fine_y % 4 + 1) * C, :]
-
-    kernel_grad(lambda x, y: mid_one[x + 1, (y + 1) * C : (y + 2) * C, :], feature, 0)
-
+    store.start()
+    loads[7].wait()
+    kernel_grad(
+        lambda x, y: mid_one[x + 1, (y + 1) * C : (y + 2) * C, :],
+        lambda x, y: feat_six[x, y * C : (y + 1) * C, :],
+        0,
+    )
+    store.wait()
+
+
+def input_kernel(mid_one, w_one_t, grad_input, stack):
     def step_one(x, carry):
         for a in range(3):
             for y in range(6):
@@ -357,8 +459,9 @@
     lax.fori_loop(0, 4, step_one, 0)
 
 
-def call(kernel, outs, scratch, n_smem, flops, *args):
+def call(kernel, outs, scratch, n_smem, flops, *args, far_in=(), far_out=()):
     vmem = pl.BlockSpec(memory_space=pltpu.VMEM)
+    hbm = pl.BlockSpec(memory_space=pltpu.HBM)
     smem = pl.BlockSpec(memory_space=pltpu.SMEM)
     moved = sum(a.size * a.dtype.itemsize for a in args) + sum(
         o.size * o.dtype.itemsize for o in outs
@@ -366,10 +469,12 @@
     return pl.pallas_call(
         kernel,
         out_shape=outs,
-        in_specs=[smem] * n_smem + [vmem] * (len(args) - n_smem),
-        out_specs=[vmem] * len(outs),
+        in_specs=[
+            smem if k < n_smem else hbm if k in far_in else vmem for k in range(len(args))
+        ],
+        out_specs=[hbm if k in far_out else vmem for k in range(len(outs))],
         scratch_shapes=scratch,
-        compiler_params=pltpu.CompilerParams(vmem_limit_bytes=VMEM_LIMIT),
+        compiler_params=pltpu.CompilerParams(vmem_limit_bytes=14 * 1024 * 1024),
         cost_estimate=pl.CostEstimate(flops=flops, bytes_accessed=moved, transcendentals=0),
     )(*args)
 
@@ -385,130 +490,139 @@
     return lax.ppermute(array, axis, up), lax.ppermute(array, axis, down)
 
 
-def shares(parts):
-    devices = lax.axis_size("gx") * lax.axis_size("gy")
-    rows = parts.shape[0] // devices
-    got = lax.all_to_all(parts.reshape(devices, rows, Z), ALL, 0, 0, tiled=True)
-    return jnp.sum(got.astype(F32), axis=0).astype(BF)
-
-
-def gathered(mine):
-    devices = lax.axis_size("gx") * lax.axis_size("gy")
-    spread = jnp.broadcast_to(mine[None], (devices,) + mine.shape)
-    return lax.all_to_all(spread, ALL, 0, 0, tiled=True)
-
-
-def fine_grad(rows):
-    part = jnp.transpose(rows.reshape(4, 144, Z), (1, 0, 2)).reshape(144, 512)[:, :432]
-    part = part.reshape(3, 2, 24, 3, 3, 2, 24)
-    own = jnp.stack([part[:, g, :, :, :, g, :] for g in range(2)], axis=1)
-    return jnp.transpose(own, (3, 4, 0, 1, 2, 5)).reshape(3, 3, 3, 1152).astype(F32)
+def other_core(array):
+    return lax.ppermute(array, "core", [(0, 1), (1, 0)])
+
+
+def pair_sum(parts, core):
+    half = parts.shape[0] // 2
+    keep = lax.dynamic_slice_in_dim(parts, core * half, half, 0)
+    send = lax.dynamic_slice_in_dim(parts, (1 - core) * half, half, 0)
+    both = keep.astype(F32) + other_core(send).astype(F32)
+    return both.astype(BF).reshape(64, half // 64, Z)
 
 
 def per_device(features, conv_one, conv_two, down_weight, coarse_weight, cotangent):
-    gx, gy = lax.axis_index("gx"), lax.axis_index("gy")
-    last_x, last_y = lax.axis_size("gx") - 1, lax.axis_size("gy") - 1
+    gx, gy, core = lax.axis_index("gx"), lax.axis_index(GY), lax.axis_index("core")
+    last_x, last_y = lax.axis_size("gx") - 1, lax.axis_size(GY) - 1
     flags = jnp.stack([gx > 0, gx < last_x, gy > 0, gy < last_y]).astype(F32)
 
     feat = jnp.transpose(features, (1, 2, 0, 3)).reshape(4, 4 * C, Z)
     before, after = neighbours(feat, "gx")
-    feat = jnp.concatenate([before, feat, after], axis=0)
-    feat, cot = lax.optimization_barrier((feat, cotangent.astype(BF)))
-    feat_l, feat_r = neighbours(feat, "gy")
-
-    cot = lax.all_to_all(
-        cot.reshape(12, 16, 2, Z), "gx", split_axis=1, concat_axis=0, tiled=True
-    )
-    cot = jnp.transpose(cot.reshape(CC, 2, Z), (1, 0, 2))
-
     one = conv_one.reshape(27, C, C // 2)
     two = conv_two.reshape(27, C, C // 2)
     down = down_weight.reshape(8, CD, C)
     w_coarse = coarse_weight.reshape(9, 3 * CC, CD)
-    w_one, w_two, w_down = call(
-        ahead_kernel, [shape((144, 432)), shape((144, 432)), shape((CD, 8 * C))], [], 0, 0,
-        one, two, down,
-    )
-
-    act_one, slope_one, slope_two, down_own, coarse_in = call(
+    before, after, one, two, down, w_coarse = lax.optimization_barrier(
+        (before, after, one, two, down, w_coarse)
+    )
+    feat = jnp.concatenate([before, feat, after], axis=0)
+    cot = jnp.transpose(cotangent.reshape(12, 16, 2, Z), (1, 0, 2, 3)).astype(BF)
+    feat, cot = lax.optimization_barrier((feat, cot))
+    feat_l, feat_r = neighbours(feat, GY)
+    cot = lax.all_to_all(cot, "gx", 0, 0, tiled=True)
+
+    kept_six, kept_eight, coarse_in = call(
         fine_kernel,
+        [shape((18, 6 * C, Z)), shape((10, 8 * C, Z)), shape((4, CD, 3 * Z))],
         [
-            shape((6, 6 * C, Z)), shape((6, 6 * C, Z), F32), shape((8, 8 * C, Z), F32),
-            shape((2, 8 * C, Z)), shape((4, CD, 3 * Z)),
-        ],
-        [
+            pltpu.VMEM((144, 432), BF), pltpu.VMEM((144, 432), BF), pltpu.VMEM((CD, 8 * C), BF),
             pltpu.VMEM((9 * C, 10 * Z), BF), pltpu.VMEM((10, 10 * C, Z), BF),
             pltpu.VMEM((6 * C, 2 * Z), BF), pltpu.VMEM((4, 8 * C, 3 * Z), BF),
+            pltpu.VMEM((6, 6 * C, Z), BF), pltpu.VMEM((8, 8 * C, Z), BF),
+            pltpu.SemaphoreType.DMA((7,)),
         ],
         1, 16_000_000_000,
-        flags, feat_l, feat, feat_r, w_one, w_two, w_down,
-    )
+        flags, feat_l, feat, feat_r, one, two, down, far_out=range(2),
+    )
+    coarse_in, cot = lax.optimization_barrier((coarse_in, cot))
+    cot = jnp.transpose(cot.reshape(CC, 2, Z), (1, 0, 2))
     coarse_out, grad_three = call(
         coarse_kernel, [shape((2, CC, Z)), shape((2, CC, Z))], [], 0, 300_000_000,
         coarse_in, w_coarse, cot,
     )
 
     before, after = neighbours(grad_three, "gx")
-    one, two, down, coarse_t, grad_three = lax.optimization_barrier(
-        (one, two, down, w_coarse, grad_three)
-    )
+    grad_three, one, two, down, w_coarse = lax.optimization_barrier(
+        (grad_three, one, two, down, w_coarse)
+    )
+    backs = [shape((144, 432)), shape((144, 432)), shape((4 * C, 2 * CD)), shape((9, 3 * CD, CC))]
     w_one_t, w_two_t, w_down_t, w_coarse_t = call(
-        back_kernel,
-        [shape((144, 432)), shape((144, 432)), shape((4 * C, 2 * CD)), shape((9, 3 * CD, CC))],
-        [], 0, 0, one, two, down, coarse_t,
-    )
+        back_kernel, backs,
+        [pltpu.VMEM(w.shape, BF) for w in backs] + [pltpu.SemaphoreType.DMA((4,))], 0, 0,
+        one, two, down, w_coarse, far_out=range(4),
+    )
+    before, after, w_one_t, w_two_t, w_down_t, w_coarse_t = lax.optimization_barrier(
+        (before, after, w_one_t, w_two_t, w_down_t, w_coarse_t)
+    )
+    wide = jnp.concatenate([before, grad_three, after], axis=0)
+    g_l, g_r = neighbours(wide, GY)
+    wide, grad_own = lax.optimization_barrier((wide, grad_three))
     (coarse_part,) = call(
         coarse_grad_kernel,
         [shape((4096, Z))],
         [pltpu.VMEM((2, 3, CC, Z), F32), pltpu.VMEM((3 * CC, 2 * Z), BF)],
         0, 500_000_000,
-        grad_three, coarse_in,
-    )
-    wide = jnp.concatenate([before, grad_three, after], axis=0)
-    g_l, g_r = neighbours(wide, "gy")
-    out = lax.all_to_all(
-        coarse_out.reshape(2, 16, 12, Z), "gx", split_axis=1, concat_axis=0, tiled=True
-    )
-    g_l, g_r, coarse_part, out = lax.optimization_barrier((g_l, g_r, coarse_part, out))
-    out = jnp.transpose(out.reshape(32, 12, Z), (1, 0, 2))
-    coarse_mine = shares(coarse_part)
-
-    grad_input, small = call(
+        grad_own, coarse_in,
+    )
+    slots = jnp.transpose(coarse_out.reshape(2, 16, 12, Z), (1, 0, 2, 3))
+    slots, coarse_part = lax.optimization_barrier((slots, coarse_part))
+    out = lax.all_to_all(slots, "gx", 0, 0, tiled=True)
+    g_l, g_r, coarse_part = lax.optimization_barrier((g_l, g_r, coarse_part))
+    coarse_mine = pair_sum(coarse_part, core)
+
+    mid_one, small = call(
         backward_kernel,
-        [shape((4, 4 * C, Z)), shape((1536, Z))],
+        [shape((6, 6 * C, Z)), shape((1024, Z))],
         [
+            pltpu.VMEM((9, 3 * CD, CC), BF), pltpu.VMEM((2, 8 * C, Z), BF),
+            pltpu.VMEM((4 * C, 2 * CD), BF), pltpu.VMEM((8, 8 * C, Z), BF),
+            pltpu.VMEM((6, 6 * C, Z), BF), pltpu.VMEM((144, 432), BF),
+            pltpu.VMEM((6, 6 * C, Z), BF), pltpu.VMEM((6, 6 * C, Z), BF),
             pltpu.VMEM((3, 6, CC, 2 * Z), BF), pltpu.VMEM((2 * CD, 4 * Z), BF),
             pltpu.VMEM((8, 8 * C, Z), BF), pltpu.VMEM((6, 6 * C, Z), BF),
             pltpu.VMEM((9 * C, 16 * Z), BF), pltpu.VMEM((144, 16 * Z), BF),
+            pltpu.SemaphoreType.DMA((9,)),
         ],
         0, 12_000_000_000,
-        g_l, wide, g_r, feat_l, feat, feat_r, act_one, slope_one, slope_two, down_own,
-        w_one_t, w_two_t, w_down_t, w_coarse_t,
-    )
-    small, coarse_mine = lax.optimization_barrier((small, coarse_mine))
-    sums = gathered(jnp.concatenate([coarse_mine, shares(small)], axis=0))
-    small_sum = sums[:, 32:].reshape(1536, Z)
-
+        g_l, wide, g_r, w_coarse_t, w_down_t, w_two_t, kept_six, kept_eight,
+        far_in=range(3, 8), far_out=(0,),
+    )
+    small, coarse_mine, out = lax.optimization_barrier((small, coarse_mine, out))
+    parts = jnp.concatenate([coarse_mine, pair_sum(small, core)], axis=1)
+    parts = lax.all_to_all(parts, SAME_CORE, 0, 0, tiled=True)
+    mine = jnp.sum(parts.astype(F32), axis=0).astype(BF)
+    (grad_input,) = call(
+        input_kernel, [shape((4, 4 * C, Z))], [pltpu.VMEM((9 * C, 4 * Z), BF)], 0, 1_000_000_000,
+        mid_one, w_one_t,
+    )
+    got = lax.all_to_all(
+        jnp.broadcast_to(mine[None], (64,) + mine.shape), SAME_CORE, 0, 0, tiled=True
+    )
+    other = other_core(got)
+    out = jnp.transpose(out.reshape(32, 12, Z), (1, 0, 2))
     grad_input = jnp.transpose(grad_input.reshape(4, 4, C, Z), (2, 0, 1, 3))
-    grad_one = fine_grad(small_sum[:576])
-    grad_two = fine_grad(small_sum[576:1152])
-    grad_down = jnp.transpose(
-        small_sum[1152:1440].reshape(3, CD, Z), (1, 0, 2)
-    ).reshape(CD, 8, C)
-    grad_down = jnp.swapaxes(grad_down, 0, 1).reshape(2, 2, 2, CD * C).astype(F32)
-    (grad_coarse,) = call(
-        final_kernel, [shape((3, 3, 3, CC * CD), F32)], [pltpu.VMEM((4096, Z), F32)], 0, 0,
-        sums[:, :32].reshape(4096, Z),
+
+    grad_coarse, grad_one, grad_two, grad_down = call(
+        final_kernel,
+        [
+            shape((3, 3, 3, CC * CD), F32), shape((3, 3, 3, C * 24), F32),
+            shape((3, 3, 3, C * 24), F32), shape((2, 2, 2, CD * C), F32),
+        ],
+        [pltpu.VMEM((4096, Z), F32), pltpu.VMEM((1024, Z), F32), pltpu.VMEM((3, 16, Z), F32)],
+        1, 0,
+        core.astype(jnp.int32).reshape(1), got, other,
     )
     return out, grad_input, grad_one, grad_two, grad_down, grad_coarse
 
 
 def solution(mesh):
-    placed = (P(None, "gx", "gy", None), P(), P(), P(), P(), P("gx", None, "gy"))
+    whole = jax.sharding.Mesh(mesh.devices.reshape(16, 4, 2), ("gx", "x", "core"))
+    fine, coarse = P(None, "gx", GY, None), P("gx", None, GY)
     return jax.shard_map(
         per_device,
-        mesh=mesh,
-        in_specs=placed,
-        out_specs=(P("gx", None, "gy"), P(None, "gx", "gy", None), P(), P(), P(), P()),
+        mesh=whole,
+        in_specs=(fine, P(), P(), P(), P(), coarse),
+        out_specs=(coarse, fine, P(), P(), P(), P()),
         check_vma=False,
     )

time: 185 us -> 149 us (0.81)
  waiting for transfers between devices: 40.7 us -> 1.02 us
  blocking collectives: 19.9 us -> 40.8 us
  starting transfers between devices: 56.6 us -> 46.9 us
  local copies, waits for them, and re-layouts: 25.1 us -> 15.9 us
  Pallas kernels: 37.9 us -> 39.9 us
    all_to_all x4 -> x2, waiting for transfers between devices: 34.1 us -> 0.01 us  [the longest x1 0.01 us: per_device(): cot = lax.all_to_all(cot, 'gx', 0, 0, tiled=True)]
    all_to_all x1 -> x2, blocking collectives: 19.9 us -> 40.8 us  [the longest x1 23.6 us: per_device(): parts = lax.all_to_all(parts, SAME_CORE, 0, 0, tiled=True)]
    all_to_all x4 -> x2, starting transfers between devices: 33 us -> 19.4 us  [the longest x1 10.2 us: per_device(): out = lax.all_to_all(slots, 'gx', 0, 0, tiled=True)]
    ppermute x8, waiting for transfers between devices: 6.62 us -> 0.02 us  [neighbours(): return (lax.ppermute(array, axis, up), lax.ppermute(array, axis, down))]
    ppermute x0 -> x3, starting transfers between devices: none -> 3.73 us  [other_core(): return lax.ppermute(array, 'core', [(0, 1), (1, 0)])]
    convert_element_type x8 -> x1, local copies, waits for them, and re-layouts: 3.55 us -> 0.71 us  [per_device(): jnp.transpose(cotangent.reshape(12, 16, 2, Z), (1, 0, 2, 3)).astype(BF)]
    reshape x8 -> x0, local copies, waits for them, and re-layouts: 2.47 us -> none  [the longest x2 1.57 us: fine_grad(): part = part.reshape(3, 2, 24, 3, 3, 2, 24)]
    pallas_call x7, Pallas kernels: 37.9 us -> 39.9 us  [call(): pl.pallas_call(kernel, out_shape=outs, in_specs=[smem if k < n_smem else...]
  transfers between devices with their start and end apart: 12 -> 13, of which waited for: 7 -> 1; matrix products, arithmetic and copies ran while one was open for 5% -> 6% of each run, Pallas kernels for 9% -> 24%
where the time goes in v2:
time: 149 us; the launch traced here: 148 us
  starting transfers between devices  46.9 us (31%)
  blocking collectives  40.8 us (27%)
  Pallas kernels  39.9 us (27%)
  local copies, waits for them, and re-layouts  15.9 us (11%)
  other arithmetic  2.56 us (2%)
    pallas_call x7, Pallas kernels, call(): pl.pallas_call(kernel, out_shape=outs, in_specs=[smem if k < n_smem else...  39.9 us
    ppermute x8, starting transfers between devices, neighbours(): return (lax.ppermute(array, axis, up), lax.ppermute(array, axis, down))  23.8 us
    all_to_all x1, blocking collectives, per_device(): parts = lax.all_to_all(parts, SAME_CORE, 0, 0, tiled=True)  23.6 us
    all_to_all x1, blocking collectives, per_device(): lax.all_to_all(jnp.broadcast_to(mine[None], (64,) + mine.shape), SAME_COR...  17.2 us
    all_to_all x1, starting transfers between devices, per_device(): out = lax.all_to_all(slots, 'gx', 0, 0, tiled=True)  10.2 us
    all_to_all x1, starting transfers between devices, per_device(): cot = lax.all_to_all(cot, 'gx', 0, 0, tiled=True)  9.22 us
    unnamed x18, local copies, waits for them, and re-layouts  6.96 us
    ppermute x3, starting transfers between devices, other_core(): return lax.ppermute(array, 'core', [(0, 1), (1, 0)])  3.73 us
  transfers between devices with their start and end apart: 13, of which 1 were waited for; matrix products, arithmetic and copies ran while one was open for 6% of the time, Pallas kernels for 24%

profile of v2, /device:TPU:1, one launch (start us, length us, event | category | flops | bytes accessed | tf_op | source)
XLA Modules:
  0.0 148.1 jit_solution(11793120219289897890)
XLA Ops:
  0.7 1.8 %copy.21 = bf16[4,4,48,128]{3,2,1,0:T(8,128)(2,1)} copy(bf16[4,4,48,128]{3,1,0,2:T(4,128)(2,1)} %bitcast.34) | data formatting | bytes 393216 | tf_op jit(solution)/shard_map/transpose | solution.py:510
  2.4 1.3 collective-permute-start.1
  3.7 5.7 %collective-permute-start = (bf16[4,192,128]{2,1,0:T(8,128)(2,1)}, bf16[4,192,128]{2,1,0:T(8,128)(2,1)}, u32[]{:S(2)}, u32[]{:S(2)}) collective-permute-start(bf16[4,192,128]{2,1,0:T(8,128)(2,1)} %bitcast.5), channel_id=1, source_target_pairs={{0,8},{8,16},{16,24},{24,32},{32,40},{40,48},{48,56},{56,64},{64,7... | collective-permute-start | bytes 589832 | tf_op jit(solution)/shard_map/ppermute | solution.py:490
  12.1 1.4 reshape.52.one
  14.0 1.2 reshape.55.w_coarse.coarse
  16.4 2.9 %collective-permute-start.3 = (bf16[12,192,128]{2,1,0:T(8,128)(2,1)S(1)}, bf16[12,192,128]{2,1,0:T(8,128)(2,1)}, u32[]{:S(2)}, u32[]{:S(2)}) collective-permute-start(bf16[12,192,128]{2,1,0:T(8,128)(2,1)S(1)} %pad_maximum_fusion.1.feat_m), channel_id=1, source_target_pairs={{1,0},{2,1},{3,2},{4,3},{5,4},{6,5},{7,6},{9,8},{10,9},{11,10},{12... | collective-permute-start | bytes 1769480 | tf_op jit(solution)/shard_map/ppermute | solution.py:490
  19.3 3.1 %collective-permute-start.2 = (bf16[12,192,128]{2,1,0:T(8,128)(2,1)S(1)}, bf16[12,192,128]{2,1,0:T(8,128)(2,1)}, u32[]{:S(2)}, u32[]{:S(2)}) collective-permute-start(bf16[12,192,128]{2,1,0:T(8,128)(2,1)S(1)} %pad_maximum_fusion.1.feat_m), channel_id=1, source_target_pairs={{0,1},{1,2},{2,3},{3,4},{4,5},{5,6},{6,7},{8,9},{9,10},{10,11},{11... | collective-permute-start | bytes 1769480 | tf_op jit(solution)/shard_map/ppermute | solution.py:490
  22.5 9.2 %all-to-all-start = ((bf16[16,12,2,128]{3,2,1,0:T(2,128)(2,1)}), bf16[16,12,2,128]{3,2,1,0:T(2,128)(2,1)S(1)}, u32[]{:S(2)}, u32[]{:S(2)}) async-start(bf16[16,12,2,128]{3,2,1,0:T(2,128)(2,1)} %bitcast.31), calls=%async_computation | async-start | bytes 196608 | tf_op jit(solution)/shard_map/all_to_all | solution.py:523
  31.7 17.9 %shard_map.109 = (bf16[18,288,128]{2,1,0:T(8,128)(2,1)S(1)}, bf16[10,384,128]{2,1,0:T(8,128)(2,1)S(1)}, bf16[4,96,384]{2,1,0:T(8,128)(2,1)S(1)}) custom-call(f32[4]{0:T(128)S(1)} %add_convert_fusion.2.flags, bf16[12,192,128]{2,1,0:T(8,128)(2,1)} %collective-permute-done.2.feat_l, bf16[12,192,128]{2,1,0:T(8,128)(2,1)S(1)} %pad_maximum_fusion.1.feat_m, ...), custom_call_target="tpu_custom_call" | custom-call | flops 16000000000 | bytes 4572688 | tf_op jit(solution)/shard_map/pallas_call | solution.py:469
  52.6 1.3 collective-permute-start.5
  53.9 4.0 %collective-permute-start.4 = (bf16[2,192,128]{2,1,0:T(8,128)(2,1)S(1)}, bf16[2,192,128]{2,1,0:T(8,128)(2,1)S(1)}, u32[]{:S(2)}, u32[]{:S(2)}) collective-permute-start(bf16[2,192,128]{2,1,0:T(8,128)(2,1)S(1)} %get-tuple-element.76.grad_three), channel_id=1, source_target_pairs={{0,8},{8,16},{16,24},{24,32},{32,40},{40,48},{48,56},{56,64},{64,7... | collective-permute-start | bytes 294920 | tf_op jit(solution)/shard_map/ppermute | solution.py:490
  57.9 3.7 %shard_map.111 = (bf16[144,432]{1,0:T(8,128)(2,1)S(1)}, bf16[144,432]{1,0:T(8,128)(2,1)S(1)}, bf16[192,192]{1,0:T(8,128)(2,1)S(1)}, bf16[9,288,192]{2,1,0:T(8,128)(2,1)S(1)}) custom-call(bf16[27,48,24]{2,1,0:T(8,128)(2,1)S(1)} %reshape.52.one, bf16[27,48,24]{2,1,0:T(8,128)(2,1)S(1)} %reshape.53.two, bf16[8,96,48]{2,1,0:T(8,128)(2,1)S(1)} %reshape.54.down, ...), custom_call_target="tpu_custom_call" | custom-call | bytes 2511360 | tf_op jit(solution)/shard_map/pallas_call | solution.py:469
  62.8 3.0 %collective-permute-start.7 = (bf16[6,192,128]{2,1,0:T(8,128)(2,1)S(1)}, bf16[6,192,128]{2,1,0:T(8,128)(2,1)S(1)}, u32[]{:S(2)}, u32[]{:S(2)}) collective-permute-start(bf16[6,192,128]{2,1,0:T(8,128)(2,1)S(1)} %constant_dynamic-update-slice_fusion.g_m), channel_id=1, source_target_pairs={{1,0},{2,1},{3,2},{4,3},{5,4},{6,5},{7,6},{9,8},{10,9},{11,10},{12... | collective-permute-start | bytes 884744 | tf_op jit(solution)/shard_map/ppermute | solution.py:490
  65.7 2.6 %collective-permute-start.6 = (bf16[6,192,128]{2,1,0:T(8,128)(2,1)S(1)}, bf16[6,192,128]{2,1,0:T(8,128)(2,1)S(1)}, u32[]{:S(2)}, u32[]{:S(2)}) collective-permute-start(bf16[6,192,128]{2,1,0:T(8,128)(2,1)S(1)} %constant_dynamic-update-slice_fusion.g_m), channel_id=1, source_target_pairs={{0,1},{1,2},{2,3},{3,4},{4,5},{5,6},{6,7},{8,9},{9,10},{10,11},{11... | collective-permute-start | bytes 884744 | tf_op jit(solution)/shard_map/ppermute | solution.py:490
  70.1 10.2 %all-to-all-start.1 = ((bf16[16,2,12,128]{3,1,2,0:T(2,128)(2,1)}), bf16[16,2,12,128]{3,1,2,0:T(2,128)(2,1)S(1)}, u32[]{:S(2)}, u32[]{:S(2)}) async-start(bf16[16,2,12,128]{3,1,2,0:T(2,128)(2,1)} %bitcast.11), calls=%async_computation.1 | async-start | bytes 196608 | tf_op jit(solution)/shard_map/all_to_all | solution.py:570
  80.7 1.3 copy-done.1
  82.0 1.3 copy-done.3
  83.3 1.2 copy-done.5
  84.5 11.3 %shard_map.113 = (bf16[6,288,128]{2,1,0:T(8,128)(2,1)S(1)}, bf16[1024,128]{1,0:T(8,128)(2,1)S(1)}) custom-call(bf16[6,192,128]{2,1,0:T(8,128)(2,1)S(1)} %collective-permute-done.6.g_l, bf16[6,192,128]{2,1,0:T(8,128)(2,1)S(1)} %constant_dynamic-update-slice_fusion.g_m, bf16[6,192,128]{2,1,0:T(8,128)(2,1)S(1)} %collective-permute-done.7.g_r, ...), custom_call_target="tpu_custom_call" | custom-call | flops 12000000000 | bytes 5092864 | tf_op jit(solution)/shard_map/pallas_call | solution.py:469
  97.7 23.6 %all_to_all.20 = bf16[64,40,128]{2,1,0:T(8,128)(2,1)S(1)} all-to-all(bf16[64,40,128]{2,1,0:T(8,128)(2,1)S(1)} %pad_maximum_fusion), channel_id=1, replica_groups=mesh['gx'=16,'x'=4,'core'=2] {'gx','x'}, dimensions={0} | all-to-all | bytes 1310720 | tf_op jit(solution)/shard_map/all_to_all | solution.py:593
  121.4 17.2 %all_to_all.21.got = bf16[64,40,128]{2,1,0:T(8,128)(2,1)S(1)} all-to-all(bf16[64,40,128]{2,1,0:T(8,128)(2,1)S(1)} %broadcast_in_dim.2), channel_id=1, replica_groups=mesh['gx'=16,'x'=4,'core'=2] {'gx','x'}, dimensions={0} | all-to-all | bytes 1310720 | tf_op jit(solution)/shard_map/all_to_all | solution.py:599
  138.7 2.9 %collective-permute-start.10 = (bf16[64,40,128]{2,1,0:T(8,128)(2,1)S(1)}, bf16[64,40,128]{2,1,0:T(8,128)(2,1)S(1)}, u32[]{:S(2)}, u32[]{:S(2)}) collective-permute-start(bf16[64,40,128]{2,1,0:T(8,128)(2,1)S(1)} %all_to_all.21.got), channel_id=1, source_target_pairs={{0,1},{1,0},{2,3},{3,2},{4,5},{5,4},{6,7},{7,6},{8,9},{9,8},{10,11... | collective-permute-start | bytes 1966088 | tf_op jit(solution)/shard_map/ppermute | solution.py:494
  141.5 1.4 shard_map.114
  144.5 3.6 %shard_map.115 = (f32[3,3,3,18432]{3,2,1,0:T(4,128)}, f32[3,3,3,1152]{3,2,1,0:T(4,128)}, f32[3,3,3,1152]{3,2,1,0:T(4,128)}, f32[2,2,2,4608]{3,2,1,0:T(2,128)}) custom-call(s32[1]{0:T(128)} %bitcast.17.core, bf16[64,40,128]{2,1,0:T(8,128)(2,1)S(1)} %all_to_all.21.got, bf16[64,40,128]{2,1,0:T(8,128)(2,1)S(1)} %collective-permute-done.10.other), custom_call_target="tpu_custom_call" | custom-call | bytes 3697668 | tf_op jit(solution)/shard_map/pallas_call | solution.py:469
  (50 shorter events, 14.1 us)
Async XLA Ops:
  0.6 12.9 %copy-start.7 = (bf16[3,3,3,1152]{3,2,1,0:T(4,128)(2,1)S(1)}, bf16[3,3,3,1152]{3,2,1,0:T(4,128)(2,1)}, u32[]{:S(2)}) copy-start(bf16[3,3,3,1152]{3,2,1,0:T(4,128)(2,1)} %param.8) | copy-start | bytes 186628
  0.6 13.3 %copy-start.6 = (bf16[3,3,3,18432]{3,2,1,0:T(4,128)(2,1)S(1)}, bf16[3,3,3,18432]{3,2,1,0:T(4,128)(2,1)}, u32[]{:S(2)}) copy-start(bf16[3,3,3,18432]{3,2,1,0:T(4,128)(2,1)} %param.10) | copy-start | bytes 2985988
  2.4 12.8 %collective-permute-start.1 = (bf16[4,192,128]{2,1,0:T(8,128)(2,1)}, bf16[4,192,128]{2,1,0:T(8,128)(2,1)}, u32[]{:S(2)}, u32[]{:S(2)}) collective-permute-start(bf16[4,192,128]{2,1,0:T(8,128)(2,1)} %bitcast.5), channel_id=1, source_target_pairs={{8,0},{16,8},{24,16},{32,24},{40,32},{48,40},{56,48},{64,56},{72,6... | collective-permute-start | bytes 589832 | tf_op jit(solution)/shard_map/ppermute | solution.py:490
  3.7 11.5 %collective-permute-start = (bf16[4,192,128]{2,1,0:T(8,128)(2,1)}, bf16[4,192,128]{2,1,0:T(8,128)(2,1)}, u32[]{:S(2)}, u32[]{:S(2)}) collective-permute-start(bf16[4,192,128]{2,1,0:T(8,128)(2,1)} %bitcast.5), channel_id=1, source_target_pairs={{0,8},{8,16},{16,24},{24,32},{32,40},{40,48},{48,56},{56,64},{64,7... | collective-permute-start | bytes 589832 | tf_op jit(solution)/shard_map/ppermute | solution.py:490
  16.4 15.3 %collective-permute-start.3 = (bf16[12,192,128]{2,1,0:T(8,128)(2,1)S(1)}, bf16[12,192,128]{2,1,0:T(8,128)(2,1)}, u32[]{:S(2)}, u32[]{:S(2)}) collective-permute-start(bf16[12,192,128]{2,1,0:T(8,128)(2,1)S(1)} %pad_maximum_fusion.1.feat_m), channel_id=1, source_target_pairs={{1,0},{2,1},{3,2},{4,3},{5,4},{6,5},{7,6},{9,8},{10,9},{11,10},{12... | collective-permute-start | bytes 1769480 | tf_op jit(solution)/shard_map/ppermute | solution.py:490
  19.3 12.4 %collective-permute-start.2 = (bf16[12,192,128]{2,1,0:T(8,128)(2,1)S(1)}, bf16[12,192,128]{2,1,0:T(8,128)(2,1)}, u32[]{:S(2)}, u32[]{:S(2)}) collective-permute-start(bf16[12,192,128]{2,1,0:T(8,128)(2,1)S(1)} %pad_maximum_fusion.1.feat_m), channel_id=1, source_target_pairs={{0,1},{1,2},{2,3},{3,4},{4,5},{5,6},{6,7},{8,9},{9,10},{10,11},{11... | collective-permute-start | bytes 1769480 | tf_op jit(solution)/shard_map/ppermute | solution.py:490
  22.5 29.2 %all-to-all-start = ((bf16[16,12,2,128]{3,2,1,0:T(2,128)(2,1)}), bf16[16,12,2,128]{3,2,1,0:T(2,128)(2,1)S(1)}, u32[]{:S(2)}, u32[]{:S(2)}) async-start(bf16[16,12,2,128]{3,2,1,0:T(2,128)(2,1)} %bitcast.31), calls=%async_computation | async-start | bytes 196608 | tf_op jit(solution)/shard_map/all_to_all | solution.py:523
  49.6 1.1 copy-start.2
  50.7 1.0 copy-start.4
  52.6 10.1 %collective-permute-start.5 = (bf16[2,192,128]{2,1,0:T(8,128)(2,1)S(1)}, bf16[2,192,128]{2,1,0:T(8,128)(2,1)S(1)}, u32[]{:S(2)}, u32[]{:S(2)}) collective-permute-start(bf16[2,192,128]{2,1,0:T(8,128)(2,1)S(1)} %get-tuple-element.76.grad_three), channel_id=1, source_target_pairs={{8,0},{16,8},{24,16},{32,24},{40,32},{48,40},{56,48},{64,56},{72,6... | collective-permute-start | bytes 294920 | tf_op jit(solution)/shard_map/ppermute | solution.py:490
  53.9 8.8 %collective-permute-start.4 = (bf16[2,192,128]{2,1,0:T(8,128)(2,1)S(1)}, bf16[2,192,128]{2,1,0:T(8,128)(2,1)S(1)}, u32[]{:S(2)}, u32[]{:S(2)}) collective-permute-start(bf16[2,192,128]{2,1,0:T(8,128)(2,1)S(1)} %get-tuple-element.76.grad_three), channel_id=1, source_target_pairs={{0,8},{8,16},{16,24},{24,32},{32,40},{40,48},{48,56},{56,64},{64,7... | collective-permute-start | bytes 294920 | tf_op jit(solution)/shard_map/ppermute | solution.py:490
  61.6 1.1 copy-start
  62.8 17.6 %collective-permute-start.7 = (bf16[6,192,128]{2,1,0:T(8,128)(2,1)S(1)}, bf16[6,192,128]{2,1,0:T(8,128)(2,1)S(1)}, u32[]{:S(2)}, u32[]{:S(2)}) collective-permute-start(bf16[6,192,128]{2,1,0:T(8,128)(2,1)S(1)} %constant_dynamic-update-slice_fusion.g_m), channel_id=1, source_target_pairs={{1,0},{2,1},{3,2},{4,3},{5,4},{6,5},{7,6},{9,8},{10,9},{11,10},{12... | collective-permute-start | bytes 884744 | tf_op jit(solution)/shard_map/ppermute | solution.py:490
  65.7 14.6 %collective-permute-start.6 = (bf16[6,192,128]{2,1,0:T(8,128)(2,1)S(1)}, bf16[6,192,128]{2,1,0:T(8,128)(2,1)S(1)}, u32[]{:S(2)}, u32[]{:S(2)}) collective-permute-start(bf16[6,192,128]{2,1,0:T(8,128)(2,1)S(1)} %constant_dynamic-update-slice_fusion.g_m), channel_id=1, source_target_pairs={{0,1},{1,2},{2,3},{3,4},{4,5},{5,6},{6,7},{8,9},{9,10},{10,11},{11... | collective-permute-start | bytes 884744 | tf_op jit(solution)/shard_map/ppermute | solution.py:490
  70.1 25.9 %all-to-all-start.1 = ((bf16[16,2,12,128]{3,1,2,0:T(2,128)(2,1)}), bf16[16,2,12,128]{3,1,2,0:T(2,128)(2,1)S(1)}, u32[]{:S(2)}, u32[]{:S(2)}) async-start(bf16[16,2,12,128]{3,1,2,0:T(2,128)(2,1)} %bitcast.11), calls=%async_computation.1 | async-start | bytes 196608 | tf_op jit(solution)/shard_map/all_to_all | solution.py:570
  80.4 15.4 %collective-permute-start.8 = (bf16[2048,128]{1,0:T(8,128)(2,1)S(1)}, bf16[2048,128]{1,0:T(8,128)(2,1)S(1)}, u32[]{:S(2)}, u32[]{:S(2)}) collective-permute-start(bf16[2048,128]{1,0:T(8,128)(2,1)S(1)} %constant_dynamic-slice_fusion.1), channel_id=1, source_target_pairs={{0,1},{1,0},{2,3},{3,2},{4,5},{5,4},{6,7},{7,6},{8,9},{9,8},{10,11... | collective-permute-start | bytes 1572872 | tf_op jit(solution)/shard_map/ppermute | solution.py:494
  80.7 1.3 copy-start.1
  82.0 1.3 copy-start.3
  83.3 1.2 copy-start.5
  96.0 1.6 %collective-permute-start.9 = (bf16[512,128]{1,0:T(8,128)(2,1)S(1)}, bf16[512,128]{1,0:T(8,128)(2,1)S(1)}, u32[]{:S(2)}, u32[]{:S(2)}) collective-permute-start(bf16[512,128]{1,0:T(8,128)(2,1)S(1)} %constant_dynamic-slice_fusion), channel_id=1, source_target_pairs={{0,1},{1,0},{2,3},{3,2},{4,5},{5,4},{6,7},{7,6},{8,9},{9,8},{10,11... | collective-permute-start | bytes 393224 | tf_op jit(solution)/shard_map/ppermute | solution.py:494
  138.7 5.8 %collective-permute-start.10 = (bf16[64,40,128]{2,1,0:T(8,128)(2,1)S(1)}, bf16[64,40,128]{2,1,0:T(8,128)(2,1)S(1)}, u32[]{:S(2)}, u32[]{:S(2)}) collective-permute-start(bf16[64,40,128]{2,1,0:T(8,128)(2,1)S(1)} %all_to_all.21.got), channel_id=1, source_target_pairs={{0,1},{1,0},{2,3},{3,2},{4,5},{5,4},{6,7},{7,6},{8,9},{9,8},{10,11... | collective-permute-start | bytes 1966088 | tf_op jit(solution)/shard_map/ppermute | solution.py:494

commit v3 on v2

--- a/solution.py
+++ b/solution.py
@@ -53,10 +53,36 @@
     return lax.broadcasted_iota(jnp.int32, shape, 1) < Z // 2
 
 
+def put(taps, x, piece, y, count):
+    for b in range(3):
+        if 0 <= y - b < count:
+            at = x * (3 * C) + b * C
+            if not isinstance(x, int):
+                at = pl.multiple_of(at, 16)
+            taps[pl.ds(at, C), (y - b) * Z : (y - b + 1) * Z] = piece
+
+
+def put_back(taps, x, piece, y, count):
+    for b in range(3):
+        if 0 <= y - 2 + b < count:
+            at = x * (3 * C) + b * C
+            if not isinstance(x, int):
+                at = pl.multiple_of(at, 16)
+            taps[pl.ds(at, C), (y - 2 + b) * Z : (y - 1 + b) * Z] = piece
+
+
+def put_left(left, x, y, grad):
+    lanes = slice(y * Z, (y + 1) * Z)
+    wide = grad.astype(F32)
+    left[x, :C, lanes] = from_after(wide, Z).astype(BF)
+    left[x, C : 2 * C, lanes] = grad
+    left[x, 2 * C :, lanes] = from_before(wide, Z).astype(BF)
+
+
 def fine_kernel(
     flags, feat_l, feat_m, feat_r, one, two, down,
     kept_six, kept_eight, coarse_in,
-    w_one, w_two, w_down, stack, field, rows_two, down_all, slope_a, slope_b, sems,
+    w_one, w_two, w_down, taps_one, taps_two, act_v, rows_two, down_all, slope_a, slope_b, sems,
 ):
     feats = (feat_l, feat_m, feat_r)
     inner = pl.ds(3, 6)
@@ -71,9 +97,11 @@
             feat_r.at[inner, pl.ds(0, C), :], kept_six.at[pl.ds(12, 6), pl.ds(5 * C, C), :], sems.at[2]
         ),
         pltpu.make_async_copy(
-            field.at[pl.ds(2, 6), pl.ds(2 * C, 6 * C), :], kept_six.at[pl.ds(0, 6)], sems.at[3]
+            act_v.at[pl.ds(2, 6)], kept_six.at[pl.ds(0, 6)], sems.at[3]
         ),
-        pltpu.make_async_copy(slope_a, kept_six.at[pl.ds(6, 6)], sems.at[4]),
+        pltpu.make_async_copy(
+            slope_a.at[pl.ds(2, 6)], kept_six.at[pl.ds(6, 6)], sems.at[4]
+        ),
         pltpu.make_async_copy(slope_b, kept_eight.at[pl.ds(0, 8)], sems.at[5]),
         pltpu.make_async_copy(
             down_all.at[pl.ds(1, 2), :, pl.ds(Z, Z)], kept_eight.at[pl.ds(8, 2)], sems.at[6]
@@ -97,31 +125,31 @@
             return flags[3]
         return 1.0
 
+    def spread_one(x, carry):
+        for y in range(12):
+            piece = feats[y // 4][x, (y % 4) * C : (y % 4 + 1) * C, :]
+            put(taps_one, x, piece, y, 10)
+        return carry
+
+    lax.fori_loop(0, 12, spread_one, 0, unroll=2)
+
     def step_one(x, carry):
-        for a in range(3):
-            for y in range(12):
-                piece = feats[y // 4][x + a, (y % 4) * C : (y % 4 + 1) * C, :]
-                for b in range(3):
-                    if 0 <= y - b < 10:
-                        stack[(a * 3 + b) * C : (a * 3 + b + 1) * C, (y - b) * Z : (y - b + 1) * Z] = piece
-        prod = dot(w_one[...], stack[...])
+        prod = dot(w_one[...], taps_one[pl.ds(pl.multiple_of(x * 3 * C, 16), 9 * C), :])
         ok_x = valid(x, 3, 7)
         for y in range(10):
             pre = tap_sum(prod, y, C, Z, False)
             sig = sigmoid(pre)
             ok = ok_x * valid_y(y, 3, 7)
             act = (pre * sig * ok).astype(BF)
-            field[x, y * C : (y + 1) * C, :] = act
+            put(taps_two, x, act, y, 8)
             if 2 <= y < 8:
                 slp = (sig * (1.0 + pre * (1.0 - sig)) * ok).astype(BF)
 
-                @pl.when(jnp.logical_and(x >= 2, x < 8))
-                def _():
-                    slope_a[x - 2, (y - 2) * C : (y - 1) * C, :] = slp
-
+                act_v[x, (y - 2) * C : (y - 1) * C, :] = act
+                slope_a[x, (y - 2) * C : (y - 1) * C, :] = slp
         return carry
 
-    lax.fori_loop(0, 10, step_one, 0)
+    lax.fori_loop(0, 10, step_one, 0, unroll=5)
     copies[3].start()
     copies[4].start()
 
@@ -131,13 +159,7 @@
     select = jnp.where(same & (row % Z == 2 * (col % (Z // 2)) + col // Z), 1.0, 0.0).astype(BF)
 
     def step_two(x, carry):
-        for a in range(3):
-            for y in range(10):
-                piece = field[x + a, y * C : (y + 1) * C, :]
-                for b in range(3):
-                    if 0 <= y - b < 8:
-                        stack[(a * 3 + b) * C : (a * 3 + b + 1) * C, (y - b) * Z : (y - b + 1) * Z] = piece
-        prod = dot(w_two[...], stack[:, : 8 * Z])
+        prod = dot(w_two[...], taps_two[pl.ds(pl.multiple_of(x * 3 * C, 16), 9 * C), :])
         ok_x = valid(x, 2, 6)
         for y in range(8):
             pre = tap_sum(prod, y, C, Z, False)
@@ -161,7 +183,7 @@
                     ]
         return carry
 
-    lax.fori_loop(0, 8, step_two, 0)
+    lax.fori_loop(0, 8, step_two, 0, unroll=4)
     copies[5].start()
     copies[6].start()
     for x in range(4):
@@ -206,7 +228,11 @@
         for c in range(3):
             turned = grouped(taps, c).T
             out[c * C : (c + 1) * C, :] = jnp.concatenate(
-                [turned[ab * C : (ab + 1) * C, :] for ab in range(9)], axis=1
+                [
+                    turned[ab * C : (ab + 1) * C, :]
+                    for ab in (6, 7, 8, 3, 4, 5, 0, 1, 2)
+                ],
+                axis=1,
             ).astype(BF)
     for ab in range(4):
         w_down_t[ab * C : (ab + 1) * C, :] = jnp.concatenate(
@@ -310,7 +336,7 @@
     g_l, g_m, g_r, coarse_hbm, down_hbm, two_hbm, kept_six, kept_eight,
     mid_out, small,
     w_coarse_t, down_own, w_down_t, slope_two, act_one, w_two_t, slope_one, feat_six,
-    halves, spread, mid_two, mid_one, stack, left, sems,
+    halves, spread, mid_one, taps, taps_mid, left, sems,
 ):
     loads = [
         pltpu.make_async_copy(src, dst, sems.at[k])
@@ -370,31 +396,22 @@
                 for y in range(4):
                     rows = slice((2 * y + b) * C, (2 * y + b + 1) * C)
                     part = fine[(a * 2 + b) * C : (a * 2 + b + 1) * C, y * Z : (y + 1) * Z]
-                    mid_two[2 * x + a, rows, :] = (
-                        part * slope_two[2 * x + a, rows, :].astype(F32)
-                    ).astype(BF)
+                    mid = (part * slope_two[2 * x + a, rows, :].astype(F32)).astype(BF)
+                    put_back(taps_mid, 2 * x + a, mid, 2 * y + b, 6)
+                    if 0 < x < 3 and 0 < y < 3:
+                        put_left(left, 2 * x + a - 2, 2 * y + b - 2, mid)
     for s in range(3):
         small[576 + s * CD : 576 + (s + 1) * CD, :] = grad_down[:, s * Z : (s + 1) * Z].astype(BF)
 
     small[864:, :] = jnp.zeros((1024 - 864, Z), BF)
 
-    def kernel_grad(grad_of, field_of, at):
-        for x in range(4):
-            for y in range(4):
-                lanes = slice((x * 4 + y) * Z, (x * 4 + y + 1) * Z)
-                grad = grad_of(x, y).astype(F32)
-                left[:C, lanes] = from_after(grad, Z).astype(BF)
-                left[C : 2 * C, lanes] = grad.astype(BF)
-                left[2 * C :, lanes] = from_before(grad, Z).astype(BF)
+    def kernel_grad(field, at):
         for x in range(6):
             for y in range(6):
-                piece = field_of(x, y)
-                for a in range(3):
-                    for b in range(3):
-                        if 0 <= x - a < 4 and 0 <= y - b < 4:
-                            cell = (x - a) * 4 + (y - b)
-                            stack[(a * 3 + b) * C : (a * 3 + b + 1) * C, cell * Z : (cell + 1) * Z] = piece
-        part = dot_t(left[...], stack[...])
+                put(taps, x, field[x, y * C : (y + 1) * C, :], y, 4)
+        part = jnp.zeros((3 * C, 9 * C), F32)
+        for x in range(4):
+            part = part + dot_t(left[x], taps[x * 3 * C : (x + 3) * 3 * C, :])
         row = lax.broadcasted_iota(jnp.int32, part.shape, 0)
         col = lax.broadcasted_iota(jnp.int32, part.shape, 1)
         part = jnp.where((row % C) // 24 == (col % C) // 24, part, 0.0).astype(BF)
@@ -406,60 +423,42 @@
             small[at + s * 144 : at + (s + 1) * 144, :] = part[:, s * Z : (s + 1) * Z]
 
     loads[4].wait()
-    kernel_grad(
-        lambda x, y: mid_two[x + 2, (y + 2) * C : (y + 3) * C, :],
-        lambda x, y: act_one[x, y * C : (y + 1) * C, :],
-        288,
-    )
+    kernel_grad(act_one, 288)
 
     loads[5].wait()
     loads[6].wait()
 
     def step_two(x, carry):
-        for a in range(3):
-            for y in range(8):
-                piece = mid_two[x + 2 - a, y * C : (y + 1) * C, :]
-                for b in range(3):
-                    at = y - 2 + b
-                    if 0 <= at < 6:
-                        stack[(a * 3 + b) * C : (a * 3 + b + 1) * C, at * Z : (at + 1) * Z] = piece
-        prod = dot(w_two_t[...], stack[:, : 6 * Z])
+        prod = dot(w_two_t[...], taps_mid[pl.ds(pl.multiple_of(x * 3 * C, 16), 9 * C), :])
         for y in range(6):
             rows = slice(y * C, (y + 1) * C)
             grad = tap_sum(prod, y, C, Z, True)
-            mid_one[x, rows, :] = (grad * slope_one[x, rows, :].astype(F32)).astype(BF)
+            mid = (grad * slope_one[x, rows, :].astype(F32)).astype(BF)
+            mid_one[x, rows, :] = mid
         return carry
 
-    lax.fori_loop(0, 6, step_two, 0)
+    lax.fori_loop(0, 6, step_two, 0, unroll=3)
 
     store.start()
+    for x in range(4):
+        for y in range(4):
+            put_left(left, x, y, mid_one[x + 1, (y + 1) * C : (y + 2) * C, :])
     loads[7].wait()
-    kernel_grad(
-        lambda x, y: mid_one[x + 1, (y + 1) * C : (y + 2) * C, :],
-        lambda x, y: feat_six[x, y * C : (y + 1) * C, :],
-        0,
-    )
+    kernel_grad(feat_six, 0)
     store.wait()
 
 
-def input_kernel(mid_one, w_one_t, grad_input, stack):
-    def step_one(x, carry):
-        for a in range(3):
-            for y in range(6):
-                piece = mid_one[x + 2 - a, y * C : (y + 1) * C, :]
-                for b in range(3):
-                    at = y - 2 + b
-                    if 0 <= at < 4:
-                        stack[(a * 3 + b) * C : (a * 3 + b + 1) * C, at * Z : (at + 1) * Z] = piece
-        prod = dot(w_one_t[...], stack[:, : 4 * Z])
+def input_kernel(mid_one, w_one_t, grad_input, taps):
+    for x in range(6):
+        for y in range(6):
+            put_back(taps, x, mid_one[x, y * C : (y + 1) * C, :], y, 4)
+    for x in range(4):
+        prod = dot(w_one_t[...], taps[x * 3 * C : (x + 3) * 3 * C, :])
         for y in range(4):
             grad_input[x, y * C : (y + 1) * C, :] = tap_sum(prod, y, C, Z, True).astype(BF)
-        return carry
-
-    lax.fori_loop(0, 4, step_one, 0)
-
-
-def call(kernel, outs, scratch, n_smem, flops, *args, far_in=(), far_out=()):
+
+
+def call(kernel, outs, scratch, n_smem, flops, *args, far_in=(), far_out=(), limit=20):
     vmem = pl.BlockSpec(memory_space=pltpu.VMEM)
     hbm = pl.BlockSpec(memory_space=pltpu.HBM)
     smem = pl.BlockSpec(memory_space=pltpu.SMEM)
@@ -474,7 +473,7 @@
         ],
         out_specs=[hbm if k in far_out else vmem for k in range(len(outs))],
         scratch_shapes=scratch,
-        compiler_params=pltpu.CompilerParams(vmem_limit_bytes=14 * 1024 * 1024),
+        compiler_params=pltpu.CompilerParams(vmem_limit_bytes=limit * 1024 * 1024),
         cost_estimate=pl.CostEstimate(flops=flops, bytes_accessed=moved, transcendentals=0),
     )(*args)
 
@@ -527,13 +526,13 @@
         [shape((18, 6 * C, Z)), shape((10, 8 * C, Z)), shape((4, CD, 3 * Z))],
         [
             pltpu.VMEM((144, 432), BF), pltpu.VMEM((144, 432), BF), pltpu.VMEM((CD, 8 * C), BF),
-            pltpu.VMEM((9 * C, 10 * Z), BF), pltpu.VMEM((10, 10 * C, Z), BF),
-            pltpu.VMEM((6 * C, 2 * Z), BF), pltpu.VMEM((4, 8 * C, 3 * Z), BF),
-            pltpu.VMEM((6, 6 * C, Z), BF), pltpu.VMEM((8, 8 * C, Z), BF),
+            pltpu.VMEM((36 * C, 10 * Z), BF), pltpu.VMEM((30 * C, 8 * Z), BF),
+            pltpu.VMEM((10, 6 * C, Z), BF), pltpu.VMEM((6 * C, 2 * Z), BF), pltpu.VMEM((4, 8 * C, 3 * Z), BF),
+            pltpu.VMEM((10, 6 * C, Z), BF), pltpu.VMEM((8, 8 * C, Z), BF),
             pltpu.SemaphoreType.DMA((7,)),
         ],
         1, 16_000_000_000,
-        flags, feat_l, feat, feat_r, one, two, down, far_out=range(2),
+        flags, feat_l, feat, feat_r, one, two, down, far_out=range(2), limit=20,
     )
     coarse_in, cot = lax.optimization_barrier((coarse_in, cot))
     cot = jnp.transpose(cot.reshape(CC, 2, Z), (1, 0, 2))
@@ -550,7 +549,7 @@
     w_one_t, w_two_t, w_down_t, w_coarse_t = call(
         back_kernel, backs,
         [pltpu.VMEM(w.shape, BF) for w in backs] + [pltpu.SemaphoreType.DMA((4,))], 0, 0,
-        one, two, down, w_coarse, far_out=range(4),
+        one, two, down, w_coarse, far_out=range(4), limit=20,
     )
     before, after, w_one_t, w_two_t, w_down_t, w_coarse_t = lax.optimization_barrier(
         (before, after, w_one_t, w_two_t, w_down_t, w_coarse_t)
@@ -580,20 +579,20 @@
             pltpu.VMEM((6, 6 * C, Z), BF), pltpu.VMEM((144, 432), BF),
             pltpu.VMEM((6, 6 * C, Z), BF), pltpu.VMEM((6, 6 * C, Z), BF),
             pltpu.VMEM((3, 6, CC, 2 * Z), BF), pltpu.VMEM((2 * CD, 4 * Z), BF),
-            pltpu.VMEM((8, 8 * C, Z), BF), pltpu.VMEM((6, 6 * C, Z), BF),
-            pltpu.VMEM((9 * C, 16 * Z), BF), pltpu.VMEM((144, 16 * Z), BF),
+            pltpu.VMEM((6, 6 * C, Z), BF), pltpu.VMEM((18 * C, 4 * Z), BF),
+            pltpu.VMEM((24 * C, 6 * Z), BF), pltpu.VMEM((4, 3 * C, 4 * Z), BF),
             pltpu.SemaphoreType.DMA((9,)),
         ],
         0, 12_000_000_000,
         g_l, wide, g_r, w_coarse_t, w_down_t, w_two_t, kept_six, kept_eight,
-        far_in=range(3, 8), far_out=(0,),
+        far_in=range(3, 8), far_out=(0,), limit=58,
     )
     small, coarse_mine, out = lax.optimization_barrier((small, coarse_mine, out))
     parts = jnp.concatenate([coarse_mine, pair_sum(small, core)], axis=1)
     parts = lax.all_to_all(parts, SAME_CORE, 0, 0, tiled=True)
     mine = jnp.sum(parts.astype(F32), axis=0).astype(BF)
     (grad_input,) = call(
-        input_kernel, [shape((4, 4 * C, Z))], [pltpu.VMEM((9 * C, 4 * Z), BF)], 0, 1_000_000_000,
+        input_kernel, [shape((4, 4 * C, Z))], [pltpu.VMEM((18 * C, 4 * Z), BF)], 0, 1_000_000_000,
         mid_one, w_one_t,
     )
     got = lax.all_to_all(

time: 149 us -> 137 us (0.919)
  Pallas kernels: 39.9 us -> 30.7 us
  local copies, waits for them, and re-layouts: 15.9 us -> 13.5 us
    pallas_call x7, Pallas kernels: 39.9 us -> 30.7 us  [call(): pl.pallas_call(kernel, out_shape=outs, in_specs=[smem if k < n_smem else...]
    unnamed x18 -> x24, local copies, waits for them, and re-layouts: 6.96 us -> 4.62 us
  transfers between devices with their start and end apart: 13 -> 13, of which waited for: 1 -> 1; matrix products, arithmetic and copies ran while one was open for 6% -> 6% of each run, Pallas kernels for 24% -> 19%
where the time goes in v3:
time: 137 us
  starting transfers between devices  47 us (34%)
  blocking collectives  40.8 us (30%)
  Pallas kernels  30.7 us (22%)
  local copies, waits for them, and re-layouts  13.5 us (10%)
  other arithmetic  2.56 us (2%)
    pallas_call x7, Pallas kernels, call(): pl.pallas_call(kernel, out_shape=outs, in_specs=[smem if k < n_smem else...  30.7 us
    ppermute x8, starting transfers between devices, neighbours(): return (lax.ppermute(array, axis, up), lax.ppermute(array, axis, down))  23.8 us
    all_to_all x1, blocking collectives, per_device(): parts = lax.all_to_all(parts, SAME_CORE, 0, 0, tiled=True)  23.5 us
    all_to_all x1, blocking collectives, per_device(): lax.all_to_all(jnp.broadcast_to(mine[None], (64,) + mine.shape), SAME_COR...  17.2 us
    all_to_all x1, starting transfers between devices, per_device(): out = lax.all_to_all(slots, 'gx', 0, 0, tiled=True)  10.2 us
    all_to_all x1, starting transfers between devices, per_device(): cot = lax.all_to_all(cot, 'gx', 0, 0, tiled=True)  9.21 us
    unnamed x24, local copies, waits for them, and re-layouts  4.62 us
    ppermute x3, starting transfers between devices, other_core(): return lax.ppermute(array, 'core', [(0, 1), (1, 0)])  3.73 us
  transfers between devices with their start and end apart: 13, of which 1 were waited for; matrix products, arithmetic and copies ran while one was open for 6% of the time, Pallas kernels for 19%

profile of v3, /device:TPU:1, one launch (start us, length us, event | category | flops | bytes accessed | tf_op | source)
XLA Modules:
  0.0 136.6 jit_solution(1360250433939045174)
XLA Ops:
  0.7 1.8 %copy.21 = bf16[4,4,48,128]{3,2,1,0:T(8,128)(2,1)} copy(bf16[4,4,48,128]{3,1,0,2:T(4,128)(2,1)} %bitcast.34) | data formatting | bytes 393216 | tf_op jit(solution)/shard_map/transpose | solution.py:509
  2.4 1.3 collective-permute-start.1
  3.7 5.7 %collective-permute-start = (bf16[4,192,128]{2,1,0:T(8,128)(2,1)}, bf16[4,192,128]{2,1,0:T(8,128)(2,1)}, u32[]{:S(2)}, u32[]{:S(2)}) collective-permute-start(bf16[4,192,128]{2,1,0:T(8,128)(2,1)} %bitcast.5), channel_id=1, source_target_pairs={{0,8},{8,16},{16,24},{24,32},{32,40},{40,48},{48,56},{56,64},{64,7... | collective-permute-start | bytes 589832 | tf_op jit(solution)/shard_map/ppermute | solution.py:489
  11.0 1.1 reshape.54.down
  12.1 1.4 reshape.52.one
  14.0 1.2 reshape.55.w_coarse.coarse
  15.2 1.2 pad_maximum_fusion.1.feat_m
  16.4 2.9 %collective-permute-start.3 = (bf16[12,192,128]{2,1,0:T(8,128)(2,1)S(1)}, bf16[12,192,128]{2,1,0:T(8,128)(2,1)}, u32[]{:S(2)}, u32[]{:S(2)}) collective-permute-start(bf16[12,192,128]{2,1,0:T(8,128)(2,1)S(1)} %pad_maximum_fusion.1.feat_m), channel_id=1, source_target_pairs={{1,0},{2,1},{3,2},{4,3},{5,4},{6,5},{7,6},{9,8},{10,9},{11,10},{12... | collective-permute-start | bytes 1769480 | tf_op jit(solution)/shard_map/ppermute | solution.py:489
  19.3 3.1 %collective-permute-start.2 = (bf16[12,192,128]{2,1,0:T(8,128)(2,1)S(1)}, bf16[12,192,128]{2,1,0:T(8,128)(2,1)}, u32[]{:S(2)}, u32[]{:S(2)}) collective-permute-start(bf16[12,192,128]{2,1,0:T(8,128)(2,1)S(1)} %pad_maximum_fusion.1.feat_m), channel_id=1, source_target_pairs={{0,1},{1,2},{2,3},{3,4},{4,5},{5,6},{6,7},{8,9},{9,10},{10,11},{11... | collective-permute-start | bytes 1769480 | tf_op jit(solution)/shard_map/ppermute | solution.py:489
  22.5 9.2 %all-to-all-start = ((bf16[16,12,2,128]{3,2,1,0:T(2,128)(2,1)}), bf16[16,12,2,128]{3,2,1,0:T(2,128)(2,1)S(1)}, u32[]{:S(2)}, u32[]{:S(2)}) async-start(bf16[16,12,2,128]{3,2,1,0:T(2,128)(2,1)} %bitcast.31), calls=%async_computation | async-start | bytes 196608 | tf_op jit(solution)/shard_map/all_to_all | solution.py:522
  31.7 9.6 %shard_map.109 = (bf16[18,288,128]{2,1,0:T(8,128)(2,1)S(1)}, bf16[10,384,128]{2,1,0:T(8,128)(2,1)S(1)}, bf16[4,96,384]{2,1,0:T(8,128)(2,1)S(1)}) custom-call(f32[4]{0:T(128)S(1)} %add_convert_fusion.2.flags, bf16[12,192,128]{2,1,0:T(8,128)(2,1)} %collective-permute-done.2.feat_l, bf16[12,192,128]{2,1,0:T(8,128)(2,1)S(1)} %pad_maximum_fusion.1.feat_m, ...), custom_call_target="tpu_custom_call" | custom-call | flops 16000000000 | bytes 4572688 | tf_op jit(solution)/shard_map/pallas_call | solution.py:468
  41.4 1.1 copy-done.4
  44.4 1.3 collective-permute-start.5
  45.7 4.0 %collective-permute-start.4 = (bf16[2,192,128]{2,1,0:T(8,128)(2,1)S(1)}, bf16[2,192,128]{2,1,0:T(8,128)(2,1)S(1)}, u32[]{:S(2)}, u32[]{:S(2)}) collective-permute-start(bf16[2,192,128]{2,1,0:T(8,128)(2,1)S(1)} %get-tuple-element.76.grad_three), channel_id=1, source_target_pairs={{0,8},{8,16},{16,24},{24,32},{32,40},{40,48},{48,56},{56,64},{64,7... | collective-permute-start | bytes 294920 | tf_op jit(solution)/shard_map/ppermute | solution.py:489
  49.7 3.8 %shard_map.111 = (bf16[144,432]{1,0:T(8,128)(2,1)S(1)}, bf16[144,432]{1,0:T(8,128)(2,1)S(1)}, bf16[192,192]{1,0:T(8,128)(2,1)S(1)}, bf16[9,288,192]{2,1,0:T(8,128)(2,1)S(1)}) custom-call(bf16[27,48,24]{2,1,0:T(8,128)(2,1)S(1)} %reshape.52.one, bf16[27,48,24]{2,1,0:T(8,128)(2,1)S(1)} %reshape.53.two, bf16[8,96,48]{2,1,0:T(8,128)(2,1)S(1)} %reshape.54.down, ...), custom_call_target="tpu_custom_call" | custom-call | bytes 2511360 | tf_op jit(solution)/shard_map/pallas_call | solution.py:468
  53.5 1.1 copy-done
  54.7 3.0 %collective-permute-start.7 = (bf16[6,192,128]{2,1,0:T(8,128)(2,1)S(1)}, bf16[6,192,128]{2,1,0:T(8,128)(2,1)S(1)}, u32[]{:S(2)}, u32[]{:S(2)}) collective-permute-start(bf16[6,192,128]{2,1,0:T(8,128)(2,1)S(1)} %constant_dynamic-update-slice_fusion.g_m), channel_id=1, source_target_pairs={{1,0},{2,1},{3,2},{4,3},{5,4},{6,5},{7,6},{9,8},{10,9},{11,10},{12... | collective-permute-start | bytes 884744 | tf_op jit(solution)/shard_map/ppermute | solution.py:489
  57.6 2.6 %collective-permute-start.6 = (bf16[6,192,128]{2,1,0:T(8,128)(2,1)S(1)}, bf16[6,192,128]{2,1,0:T(8,128)(2,1)}, u32[]{:S(2)}, u32[]{:S(2)}) collective-permute-start(bf16[6,192,128]{2,1,0:T(8,128)(2,1)S(1)} %constant_dynamic-update-slice_fusion.g_m), channel_id=1, source_target_pairs={{0,1},{1,2},{2,3},{3,4},{4,5},{5,6},{6,7},{8,9},{9,10},{10,11},{11... | collective-permute-start | bytes 884744 | tf_op jit(solution)/shard_map/ppermute | solution.py:489
  62.0 10.2 %all-to-all-start.1 = ((bf16[16,2,12,128]{3,1,2,0:T(2,128)(2,1)}), bf16[16,2,12,128]{3,1,2,0:T(2,128)(2,1)S(1)}, u32[]{:S(2)}, u32[]{:S(2)}) async-start(bf16[16,2,12,128]{3,1,2,0:T(2,128)(2,1)} %bitcast.11), calls=%async_computation.1 | async-start | bytes 196608 | tf_op jit(solution)/shard_map/all_to_all | solution.py:569
  73.3 11.1 %shard_map.113 = (bf16[6,288,128]{2,1,0:T(8,128)(2,1)}, bf16[1024,128]{1,0:T(8,128)(2,1)}) custom-call(bf16[6,192,128]{2,1,0:T(8,128)(2,1)} %collective-permute-done.6.g_l, bf16[6,192,128]{2,1,0:T(8,128)(2,1)} %copy-done.9, bf16[6,192,128]{2,1,0:T(8,128)(2,1)} %copy-done.10, bf16[9,288,192]{2,1,0:T(8,128)(2,1)} %copy-done, bf16[192,192]{1,0:T(8,128)(2,1)} %copy-done.2, ...), custom_call_target="tpu_custom_call" | custom-call | flops 12000000000 | bytes 5092864 | tf_op jit(solution)/shard_map/pallas_call | solution.py:468
  87.1 23.5 %all_to_all.20 = bf16[64,40,128]{2,1,0:T(8,128)(2,1)S(1)} all-to-all(bf16[64,40,128]{2,1,0:T(8,128)(2,1)S(1)} %pad_maximum_fusion), channel_id=1, replica_groups=mesh['gx'=16,'x'=4,'core'=2] {'gx','x'}, dimensions={0} | all-to-all | bytes 1310720 | tf_op jit(solution)/shard_map/all_to_all | solution.py:592
  110.8 17.2 %all_to_all.21.got = bf16[64,40,128]{2,1,0:T(8,128)(2,1)S(1)} all-to-all(bf16[64,40,128]{2,1,0:T(8,128)(2,1)S(1)} %broadcast_in_dim.2), channel_id=1, replica_groups=mesh['gx'=16,'x'=4,'core'=2] {'gx','x'}, dimensions={0} | all-to-all | bytes 1310720 | tf_op jit(solution)/shard_map/all_to_all | solution.py:598
  128.0 2.9 %collective-permute-start.10 = (bf16[64,40,128]{2,1,0:T(8,128)(2,1)S(1)}, bf16[64,40,128]{2,1,0:T(8,128)(2,1)S(1)}, u32[]{:S(2)}, u32[]{:S(2)}) collective-permute-start(bf16[64,40,128]{2,1,0:T(8,128)(2,1)S(1)} %all_to_all.21.got), channel_id=1, source_target_pairs={{0,1},{1,0},{2,3},{3,2},{4,5},{5,4},{6,7},{7,6},{8,9},{9,8},{10,11... | collective-permute-start | bytes 1966088 | tf_op jit(solution)/shard_map/ppermute | solution.py:493
  133.0 3.6 %shard_map.115 = (f32[3,3,3,18432]{3,2,1,0:T(4,128)}, f32[3,3,3,1152]{3,2,1,0:T(4,128)}, f32[3,3,3,1152]{3,2,1,0:T(4,128)}, f32[2,2,2,4608]{3,2,1,0:T(2,128)}) custom-call(s32[1]{0:T(128)} %bitcast.17.core, bf16[64,40,128]{2,1,0:T(8,128)(2,1)S(1)} %all_to_all.21.got, bf16[64,40,128]{2,1,0:T(8,128)(2,1)S(1)} %collective-permute-done.10.other), custom_call_target="tpu_custom_call" | custom-call | bytes 3697668 | tf_op jit(solution)/shard_map/pallas_call | solution.py:468
  (56 shorter events, 11.8 us)
Async XLA Ops:
  0.6 12.9 %copy-start.8 = (bf16[3,3,3,1152]{3,2,1,0:T(4,128)(2,1)S(1)}, bf16[3,3,3,1152]{3,2,1,0:T(4,128)(2,1)}, u32[]{:S(2)}) copy-start(bf16[3,3,3,1152]{3,2,1,0:T(4,128)(2,1)} %param.8) | copy-start | bytes 186628
  0.6 13.3 %copy-start.6 = (bf16[3,3,3,18432]{3,2,1,0:T(4,128)(2,1)S(1)}, bf16[3,3,3,18432]{3,2,1,0:T(4,128)(2,1)}, u32[]{:S(2)}) copy-start(bf16[3,3,3,18432]{3,2,1,0:T(4,128)(2,1)} %param.10) | copy-start | bytes 2985988
  2.4 12.8 %collective-permute-start.1 = (bf16[4,192,128]{2,1,0:T(8,128)(2,1)}, bf16[4,192,128]{2,1,0:T(8,128)(2,1)}, u32[]{:S(2)}, u32[]{:S(2)}) collective-permute-start(bf16[4,192,128]{2,1,0:T(8,128)(2,1)} %bitcast.5), channel_id=1, source_target_pairs={{8,0},{16,8},{24,16},{32,24},{40,32},{48,40},{56,48},{64,56},{72,6... | collective-permute-start | bytes 589832 | tf_op jit(solution)/shard_map/ppermute | solution.py:489
  3.7 11.5 %collective-permute-start = (bf16[4,192,128]{2,1,0:T(8,128)(2,1)}, bf16[4,192,128]{2,1,0:T(8,128)(2,1)}, u32[]{:S(2)}, u32[]{:S(2)}) collective-permute-start(bf16[4,192,128]{2,1,0:T(8,128)(2,1)} %bitcast.5), channel_id=1, source_target_pairs={{0,8},{8,16},{16,24},{24,32},{32,40},{40,48},{48,56},{56,64},{64,7... | collective-permute-start | bytes 589832 | tf_op jit(solution)/shard_map/ppermute | solution.py:489
  16.4 15.3 %collective-permute-start.3 = (bf16[12,192,128]{2,1,0:T(8,128)(2,1)S(1)}, bf16[12,192,128]{2,1,0:T(8,128)(2,1)}, u32[]{:S(2)}, u32[]{:S(2)}) collective-permute-start(bf16[12,192,128]{2,1,0:T(8,128)(2,1)S(1)} %pad_maximum_fusion.1.feat_m), channel_id=1, source_target_pairs={{1,0},{2,1},{3,2},{4,3},{5,4},{6,5},{7,6},{9,8},{10,9},{11,10},{12... | collective-permute-start | bytes 1769480 | tf_op jit(solution)/shard_map/ppermute | solution.py:489
  19.3 12.4 %collective-permute-start.2 = (bf16[12,192,128]{2,1,0:T(8,128)(2,1)S(1)}, bf16[12,192,128]{2,1,0:T(8,128)(2,1)}, u32[]{:S(2)}, u32[]{:S(2)}) collective-permute-start(bf16[12,192,128]{2,1,0:T(8,128)(2,1)S(1)} %pad_maximum_fusion.1.feat_m), channel_id=1, source_target_pairs={{0,1},{1,2},{2,3},{3,4},{4,5},{5,6},{6,7},{8,9},{9,10},{10,11},{11... | collective-permute-start | bytes 1769480 | tf_op jit(solution)/shard_map/ppermute | solution.py:489
  22.5 20.9 %all-to-all-start = ((bf16[16,12,2,128]{3,2,1,0:T(2,128)(2,1)}), bf16[16,12,2,128]{3,2,1,0:T(2,128)(2,1)S(1)}, u32[]{:S(2)}, u32[]{:S(2)}) async-start(bf16[16,12,2,128]{3,2,1,0:T(2,128)(2,1)} %bitcast.31), calls=%async_computation | async-start | bytes 196608 | tf_op jit(solution)/shard_map/all_to_all | solution.py:522
  41.3 1.1 copy-start.4
  42.4 0.9 copy-start.5
  44.4 10.2 %collective-permute-start.5 = (bf16[2,192,128]{2,1,0:T(8,128)(2,1)S(1)}, bf16[2,192,128]{2,1,0:T(8,128)(2,1)S(1)}, u32[]{:S(2)}, u32[]{:S(2)}) collective-permute-start(bf16[2,192,128]{2,1,0:T(8,128)(2,1)S(1)} %get-tuple-element.76.grad_three), channel_id=1, source_target_pairs={{8,0},{16,8},{24,16},{32,24},{40,32},{48,40},{56,48},{64,56},{72,6... | collective-permute-start | bytes 294920 | tf_op jit(solution)/shard_map/ppermute | solution.py:489
  45.7 8.9 %collective-permute-start.4 = (bf16[2,192,128]{2,1,0:T(8,128)(2,1)S(1)}, bf16[2,192,128]{2,1,0:T(8,128)(2,1)S(1)}, u32[]{:S(2)}, u32[]{:S(2)}) collective-permute-start(bf16[2,192,128]{2,1,0:T(8,128)(2,1)S(1)} %get-tuple-element.76.grad_three), channel_id=1, source_target_pairs={{0,8},{8,16},{16,24},{24,32},{32,40},{40,48},{48,56},{56,64},{64,7... | collective-permute-start | bytes 294920 | tf_op jit(solution)/shard_map/ppermute | solution.py:489
  53.5 1.1 copy-start
  54.6 7.4 %copy-start.1 = (bf16[144,432]{1,0:T(8,128)(2,1)}, bf16[144,432]{1,0:T(8,128)(2,1)S(1)}, u32[]{:S(2)}) copy-start(bf16[144,432]{1,0:T(8,128)(2,1)S(1)} %get-tuple-element.83.two_hbm) | copy-start | bytes 373252
  54.6 7.4 %copy-start.2 = (bf16[192,192]{1,0:T(8,128)(2,1)}, bf16[192,192]{1,0:T(8,128)(2,1)S(1)}, u32[]{:S(2)}) copy-start(bf16[192,192]{1,0:T(8,128)(2,1)S(1)} %get-tuple-element.82.down_hbm) | copy-start | bytes 221188
  54.6 18.4 %copy-start.9 = (bf16[6,192,128]{2,1,0:T(8,128)(2,1)}, bf16[6,192,128]{2,1,0:T(8,128)(2,1)S(1)}, u32[]{:S(2)}) copy-start(bf16[6,192,128]{2,1,0:T(8,128)(2,1)S(1)} %constant_dynamic-update-slice_fusion.g_m) | copy-start | bytes 884740
  54.7 17.6 %collective-permute-start.7 = (bf16[6,192,128]{2,1,0:T(8,128)(2,1)S(1)}, bf16[6,192,128]{2,1,0:T(8,128)(2,1)S(1)}, u32[]{:S(2)}, u32[]{:S(2)}) collective-permute-start(bf16[6,192,128]{2,1,0:T(8,128)(2,1)S(1)} %constant_dynamic-update-slice_fusion.g_m), channel_id=1, source_target_pairs={{1,0},{2,1},{3,2},{4,3},{5,4},{6,5},{7,6},{9,8},{10,9},{11,10},{12... | collective-permute-start | bytes 884744 | tf_op jit(solution)/shard_map/ppermute | solution.py:489
  57.6 15.3 %collective-permute-start.6 = (bf16[6,192,128]{2,1,0:T(8,128)(2,1)S(1)}, bf16[6,192,128]{2,1,0:T(8,128)(2,1)}, u32[]{:S(2)}, u32[]{:S(2)}) collective-permute-start(bf16[6,192,128]{2,1,0:T(8,128)(2,1)S(1)} %constant_dynamic-update-slice_fusion.g_m), channel_id=1, source_target_pairs={{0,1},{1,2},{2,3},{3,4},{4,5},{5,6},{6,7},{8,9},{9,10},{10,11},{11... | collective-permute-start | bytes 884744 | tf_op jit(solution)/shard_map/ppermute | solution.py:489
  62.0 22.6 %all-to-all-start.1 = ((bf16[16,2,12,128]{3,1,2,0:T(2,128)(2,1)}), bf16[16,2,12,128]{3,1,2,0:T(2,128)(2,1)S(1)}, u32[]{:S(2)}, u32[]{:S(2)}) async-start(bf16[16,2,12,128]{3,1,2,0:T(2,128)(2,1)} %bitcast.11), calls=%async_computation.1 | async-start | bytes 196608 | tf_op jit(solution)/shard_map/all_to_all | solution.py:569
  72.2 0.7 copy-start.10
  73.0 11.4 %collective-permute-start.8 = (bf16[2048,128]{1,0:T(8,128)(2,1)S(1)}, bf16[2048,128]{1,0:T(8,128)(2,1)S(1)}, u32[]{:S(2)}, u32[]{:S(2)}) collective-permute-start(bf16[2048,128]{1,0:T(8,128)(2,1)S(1)} %constant_dynamic-slice_fusion.1), channel_id=1, source_target_pairs={{0,1},{1,0},{2,3},{3,2},{4,5},{5,4},{6,7},{7,6},{8,9},{9,8},{10,11... | collective-permute-start | bytes 1572872 | tf_op jit(solution)/shard_map/ppermute | solution.py:493
  84.4 1.0 copy-start.7
  85.4 1.6 %collective-permute-start.9 = (bf16[512,128]{1,0:T(8,128)(2,1)S(1)}, bf16[512,128]{1,0:T(8,128)(2,1)S(1)}, u32[]{:S(2)}, u32[]{:S(2)}) collective-permute-start(bf16[512,128]{1,0:T(8,128)(2,1)S(1)} %constant_dynamic-slice_fusion), channel_id=1, source_target_pairs={{0,1},{1,0},{2,3},{3,2},{4,5},{5,4},{6,7},{7,6},{8,9},{9,8},{10,11... | collective-permute-start | bytes 393224 | tf_op jit(solution)/shard_map/ppermute | solution.py:493
  110.6 20.3 %copy-start.3 = (bf16[6,288,128]{2,1,0:T(8,128)(2,1)S(1)}, bf16[6,288,128]{2,1,0:T(8,128)(2,1)}, u32[]{:S(2)}) copy-start(bf16[6,288,128]{2,1,0:T(8,128)(2,1)} %get-tuple-element.90.mid_one) | copy-start | bytes 1327108
  128.0 5.0 %collective-permute-start.10 = (bf16[64,40,128]{2,1,0:T(8,128)(2,1)S(1)}, bf16[64,40,128]{2,1,0:T(8,128)(2,1)S(1)}, u32[]{:S(2)}, u32[]{:S(2)}) collective-permute-start(bf16[64,40,128]{2,1,0:T(8,128)(2,1)S(1)} %all_to_all.21.got), channel_id=1, source_target_pairs={{0,1},{1,0},{2,3},{3,2},{4,5},{5,4},{6,7},{7,6},{8,9},{9,8},{10,11... | collective-permute-start | bytes 1966088 | tf_op jit(solution)/shard_map/ppermute | solution.py:493

commit v4 on v3

--- a/solution.py
+++ b/solution.py
@@ -221,7 +221,7 @@
     copies = [
         pltpu.make_async_copy(src, dst, sems.at[k])
         for k, (src, dst) in enumerate((
-            (w_one_t, one_out), (w_two_t, two_out), (w_down_t, down_out), (w_coarse_t, coarse_out)
+            (w_one_t, one_out), (w_two_t, two_out), (w_down_t, down_out), (w_coarse_t, coarse_out.at[pl.ds(0, 9)])
         ))
     ]
     for taps, out in ((one, w_one_t), (two, w_two_t)):
@@ -341,7 +341,7 @@
     loads = [
         pltpu.make_async_copy(src, dst, sems.at[k])
         for k, (src, dst) in enumerate((
-            (coarse_hbm, w_coarse_t), (kept_eight.at[pl.ds(8, 2)], down_own),
+            (coarse_hbm.at[pl.ds(0, 9)], w_coarse_t), (kept_eight.at[pl.ds(8, 2)], down_own),
             (down_hbm, w_down_t), (kept_eight.at[pl.ds(0, 8)], slope_two),
             (kept_six.at[pl.ds(0, 6)], act_one), (two_hbm, w_two_t),
             (kept_six.at[pl.ds(6, 6)], slope_one), (kept_six.at[pl.ds(12, 6)], feat_six),
@@ -523,7 +523,7 @@
 
     kept_six, kept_eight, coarse_in = call(
         fine_kernel,
-        [shape((18, 6 * C, Z)), shape((10, 8 * C, Z)), shape((4, CD, 3 * Z))],
+        [shape((400, 6 * C, Z)), shape((300, 8 * C, Z)), shape((4, CD, 3 * Z))],
         [
             pltpu.VMEM((144, 432), BF), pltpu.VMEM((144, 432), BF), pltpu.VMEM((CD, 8 * C), BF),
             pltpu.VMEM((36 * C, 10 * Z), BF), pltpu.VMEM((30 * C, 8 * Z), BF),
@@ -532,7 +532,7 @@
             pltpu.SemaphoreType.DMA((7,)),
         ],
         1, 16_000_000_000,
-        flags, feat_l, feat, feat_r, one, two, down, far_out=range(2), limit=20,
+        flags, feat_l, feat, feat_r, one, two, down, far_out=range(2), limit=40,
     )
     coarse_in, cot = lax.optimization_barrier((coarse_in, cot))
     cot = jnp.transpose(cot.reshape(CC, 2, Z), (1, 0, 2))
@@ -545,11 +545,12 @@
     grad_three, one, two, down, w_coarse = lax.optimization_barrier(
         (grad_three, one, two, down, w_coarse)
     )
-    backs = [shape((144, 432)), shape((144, 432)), shape((4 * C, 2 * CD)), shape((9, 3 * CD, CC))]
+    backs = [shape((144, 432)), shape((144, 432)), shape((4 * C, 2 * CD)), shape((200, 3 * CD, CC))]
     w_one_t, w_two_t, w_down_t, w_coarse_t = call(
         back_kernel, backs,
-        [pltpu.VMEM(w.shape, BF) for w in backs] + [pltpu.SemaphoreType.DMA((4,))], 0, 0,
-        one, two, down, w_coarse, far_out=range(4), limit=20,
+        [pltpu.VMEM(w.shape, BF) for w in backs[:3]]
+        + [pltpu.VMEM((9, 3 * CD, CC), BF), pltpu.SemaphoreType.DMA((4,))], 0, 0,
+        one, two, down, w_coarse, far_out=range(4), limit=40,
     )
     before, after, w_one_t, w_two_t, w_down_t, w_coarse_t = lax.optimization_barrier(
         (before, after, w_one_t, w_two_t, w_down_t, w_coarse_t)
@@ -564,11 +565,11 @@
         0, 500_000_000,
         grad_own, coarse_in,
     )
-    slots = jnp.transpose(coarse_out.reshape(2, 16, 12, Z), (1, 0, 2, 3))
-    slots, coarse_part = lax.optimization_barrier((slots, coarse_part))
-    out = lax.all_to_all(slots, "gx", 0, 0, tiled=True)
     g_l, g_r, coarse_part = lax.optimization_barrier((g_l, g_r, coarse_part))
     coarse_mine = pair_sum(coarse_part, core)
+    slots = jnp.transpose(coarse_out.reshape(2, 16, 12, Z), (1, 0, 2, 3)).reshape(16, 1, 24, Z)
+    there = lax.broadcasted_iota(jnp.int32, (16, 4, 24, Z), 1) == lax.axis_index("x")
+    slots = jnp.where(there, slots, jnp.zeros((), BF)).reshape(64, 24, Z)
 
     mid_one, small = call(
         backward_kernel,
@@ -585,12 +586,15 @@
         ],
         0, 12_000_000_000,
         g_l, wide, g_r, w_coarse_t, w_down_t, w_two_t, kept_six, kept_eight,
-        far_in=range(3, 8), far_out=(0,), limit=58,
-    )
-    small, coarse_mine, out = lax.optimization_barrier((small, coarse_mine, out))
-    parts = jnp.concatenate([coarse_mine, pair_sum(small, core)], axis=1)
+        far_in=range(3, 8), far_out=(0,), limit=40,
+    )
+    small, coarse_mine, slots = lax.optimization_barrier((small, coarse_mine, slots))
+    parts = jnp.concatenate([coarse_mine, pair_sum(small, core), slots], axis=1)
     parts = lax.all_to_all(parts, SAME_CORE, 0, 0, tiled=True)
-    mine = jnp.sum(parts.astype(F32), axis=0).astype(BF)
+    out = lax.dynamic_index_in_dim(
+        parts[:, 40:].reshape(16, 4, 24, Z), lax.axis_index("x"), 1, keepdims=False
+    )
+    mine = jnp.sum(parts[:, :40].astype(F32), axis=0).astype(BF)
     (grad_input,) = call(
         input_kernel, [shape((4, 4 * C, Z))], [pltpu.VMEM((18 * C, 4 * Z), BF)], 0, 1_000_000_000,
         mid_one, w_one_t,

time: 137 us -> 132 us (0.964)
  starting transfers between devices: 47 us -> 36.1 us
  blocking collectives: 40.8 us -> 46 us
  waiting for transfers between devices: 1.02 us -> 5.95 us
  local copies, waits for them, and re-layouts: 13.5 us -> 10.3 us
    all_to_all x1 -> x0, starting transfers between devices: 10.2 us -> none  [per_device(): out = lax.all_to_all(slots, 'gx', 0, 0, tiled=True)]
    all_to_all x1, blocking collectives: 23.5 us -> 29.2 us  [per_device(): parts = lax.all_to_all(parts, SAME_CORE, 0, 0, tiled=True)]
    ppermute x8, waiting for transfers between devices: 0.02 us -> 4.96 us  [neighbours(): return (lax.ppermute(array, axis, up), lax.ppermute(array, axis, down))]
    unnamed x24 -> x5, local copies, waits for them, and re-layouts: 4.62 us -> 0.7 us
    reshape x1, local copies, waits for them, and re-layouts: 1.18 us -> 2.81 us  [per_device(): w_coarse = coarse_weight.reshape(9, 3 * CC, CD)]
  transfers between devices with their start and end apart: 13 -> 12, of which waited for: 1 -> 4; matrix products, arithmetic and copies ran while one was open for 6% -> 7% of each run, Pallas kernels for 19% -> 19%
where the time goes in v4:
time: 132 us; the launch traced here: 131 us
  blocking collectives  46 us (35%)
  starting transfers between devices  36.1 us (27%)
  Pallas kernels  30 us (23%)
  local copies, waits for them, and re-layouts  10.3 us (8%)
  waiting for transfers between devices  5.95 us (5%)
  other arithmetic  1.67 us (1%)
    pallas_call x7, Pallas kernels, call(): pl.pallas_call(kernel, out_shape=outs, in_specs=[smem if k < n_smem else...  30 us
    all_to_all x1, blocking collectives, per_device(): parts = lax.all_to_all(parts, SAME_CORE, 0, 0, tiled=True)  29.2 us
    ppermute x8, starting transfers between devices, neighbours(): return (lax.ppermute(array, axis, up), lax.ppermute(array, axis, down))  23.2 us
    all_to_all x1, blocking collectives, per_device(): lax.all_to_all(jnp.broadcast_to(mine[None], (64,) + mine.shape), SAME_COR...  16.8 us
    all_to_all x1, starting transfers between devices, per_device(): cot = lax.all_to_all(cot, 'gx', 0, 0, tiled=True)  8.98 us
    ppermute x8, waiting for transfers between devices, neighbours(): return (lax.ppermute(array, axis, up), lax.ppermute(array, axis, down))  4.96 us
    ppermute x3, starting transfers between devices, other_core(): return lax.ppermute(array, 'core', [(0, 1), (1, 0)])  3.91 us
    reshape x1, local copies, waits for them, and re-layouts, per_device(): w_coarse = coarse_weight.reshape(9, 3 * CC, CD)  2.81 us
  transfers between devices with their start and end apart: 12, of which 4 were waited for; matrix products, arithmetic and copies ran while one was open for 7% of the time, Pallas kernels for 19%

profile of v4, /device:TPU:1, one launch (start us, length us, event | category | flops | bytes accessed | tf_op | source)
XLA Modules:
  0.0 131.0 jit_solution(4079526328628253001)
XLA Ops:
  0.6 1.0 copy.23
  1.7 4.4 %collective-permute-start = (bf16[4,192,128]{2,1,0:T(8,128)(2,1)S(1)}, bf16[4,192,128]{2,1,0:T(8,128)(2,1)S(1)}, u32[]{:S(2)}, u32[]{:S(2)}) collective-permute-start(bf16[4,192,128]{2,1,0:T(8,128)(2,1)S(1)} %bitcast.35), channel_id=1, source_target_pairs={{0,8},{8,16},{16,24},{24,32},{32,40},{40,48},{48,56},{56,64},{64,7... | collective-permute-start | bytes 589832 | tf_op jit(solution)/shard_map/ppermute | solution.py:489
  6.1 1.3 collective-permute-start.1
  7.4 1.4 %reshape.61.one = bf16[27,48,24]{2,1,0:T(8,128)(2,1)S(1)} reshape(bf16[3,3,3,1152]{3,2,1,0:T(4,128)(2,1)} %param.7) | data formatting | bytes 124416 | tf_op jit(solution)/shard_map/reshape | solution.py:511
  8.7 1.4 %reshape.62.two = bf16[27,48,24]{2,1,0:T(8,128)(2,1)S(1)} reshape(bf16[3,3,3,1152]{3,2,1,0:T(4,128)(2,1)} %param.8) | data formatting | bytes 124416 | tf_op jit(solution)/shard_map/reshape | solution.py:512
  10.1 1.1 reshape.63.down
  11.2 2.8 %reshape.64.w_coarse.coarse = bf16[9,576,96]{2,1,0:T(8,128)(2,1)S(1)} reshape(bf16[3,3,3,18432]{3,2,1,0:T(4,128)(2,1)} %param.10) | data formatting | bytes 1990656 | tf_op jit(solution)/shard_map/reshape | solution.py:514
  14.8 1.0 pad_maximum_fusion.1.feat_m
  15.8 4.0 %collective-permute-start.2 = (bf16[12,192,128]{2,1,0:T(8,128)(2,1)S(1)}, bf16[12,192,128]{2,1,0:T(8,128)(2,1)}, u32[]{:S(2)}, u32[]{:S(2)}) collective-permute-start(bf16[12,192,128]{2,1,0:T(8,128)(2,1)S(1)} %pad_maximum_fusion.1.feat_m), channel_id=1, source_target_pairs={{0,1},{1,2},{2,3},{3,4},{4,5},{5,6},{6,7},{8,9},{9,10},{10,11},{11... | collective-permute-start | bytes 1769480 | tf_op jit(solution)/shard_map/ppermute | solution.py:489
  19.7 1.9 %collective-permute-start.3 = (bf16[12,192,128]{2,1,0:T(8,128)(2,1)S(1)}, bf16[12,192,128]{2,1,0:T(8,128)(2,1)}, u32[]{:S(2)}, u32[]{:S(2)}) collective-permute-start(bf16[12,192,128]{2,1,0:T(8,128)(2,1)S(1)} %pad_maximum_fusion.1.feat_m), channel_id=1, source_target_pairs={{1,0},{2,1},{3,2},{4,3},{5,4},{6,5},{7,6},{9,8},{10,9},{11,10},{12... | collective-permute-start | bytes 1769480 | tf_op jit(solution)/shard_map/ppermute | solution.py:489
  21.7 9.0 %all-to-all-start = ((bf16[16,12,2,128]{3,2,1,0:T(2,128)(2,1)}), bf16[16,12,2,128]{3,2,1,0:T(2,128)(2,1)S(1)}, u32[]{:S(2)}, u32[]{:S(2)}) async-start(bf16[16,12,2,128]{3,2,1,0:T(2,128)(2,1)} %bitcast.31), calls=%async_computation | async-start | bytes 196608 | tf_op jit(solution)/shard_map/all_to_all | solution.py:522
  31.0 9.5 %shard_map.109 = (bf16[400,288,128]{2,1,0:T(8,128)(2,1)}, bf16[300,384,128]{2,1,0:T(8,128)(2,1)}, bf16[4,96,384]{2,1,0:T(8,128)(2,1)S(1)}) custom-call(f32[4]{0:T(128)S(1)} %add_convert_fusion.2.flags, bf16[12,192,128]{2,1,0:T(8,128)(2,1)} %collective-permute-done.2.feat_l, bf16[12,192,128]{2,1,0:T(8,128)(2,1)S(1)} %pad_maximum_fusion.1.feat_m, ...), custom_call_target="tpu_custom_call" | custom-call | flops 16000000000 | bytes 61244944 | tf_op jit(solution)/shard_map/pallas_call | solution.py:468
  41.5 4.3 %collective-permute-start.4 = (bf16[2,192,128]{2,1,0:T(8,128)(2,1)S(1)}, bf16[2,192,128]{2,1,0:T(8,128)(2,1)S(1)}, u32[]{:S(2)}, u32[]{:S(2)}) collective-permute-start(bf16[2,192,128]{2,1,0:T(8,128)(2,1)S(1)} %get-tuple-element.73.grad_three), channel_id=1, source_target_pairs={{0,8},{8,16},{16,24},{24,32},{32,40},{40,48},{48,56},{56,64},{64,7... | collective-permute-start | bytes 294920 | tf_op jit(solution)/shard_map/ppermute | solution.py:489
  45.8 1.3 collective-permute-start.5
  47.1 4.8 %shard_map.111 = (bf16[144,432]{1,0:T(8,128)(2,1)S(1)}, bf16[144,432]{1,0:T(8,128)(2,1)S(1)}, bf16[192,192]{1,0:T(8,128)(2,1)S(1)}, bf16[200,288,192]{2,1,0:T(8,128)(2,1)}) custom-call(bf16[27,48,24]{2,1,0:T(8,128)(2,1)S(1)} %reshape.61.one, bf16[27,48,24]{2,1,0:T(8,128)(2,1)S(1)} %reshape.62.two, bf16[8,96,48]{2,1,0:T(8,128)(2,1)S(1)} %reshape.63.down, ...), custom_call_target="tpu_custom_call" | custom-call | bytes 23634432 | tf_op jit(solution)/shard_map/pallas_call | solution.py:468
  52.0 4.2 %collective-permute-start.6 = (bf16[6,192,128]{2,1,0:T(8,128)(2,1)S(1)}, bf16[6,192,128]{2,1,0:T(8,128)(2,1)S(1)}, u32[]{:S(2)}, u32[]{:S(2)}) collective-permute-start(bf16[6,192,128]{2,1,0:T(8,128)(2,1)S(1)} %constant_dynamic-update-slice_fusion.g_m), channel_id=1, source_target_pairs={{0,1},{1,2},{2,3},{3,4},{4,5},{5,6},{6,7},{8,9},{9,10},{10,11},{11... | collective-permute-start | bytes 884744 | tf_op jit(solution)/shard_map/ppermute | solution.py:489
  56.1 1.9 %collective-permute-start.7 = (bf16[6,192,128]{2,1,0:T(8,128)(2,1)S(1)}, bf16[6,192,128]{2,1,0:T(8,128)(2,1)S(1)}, u32[]{:S(2)}, u32[]{:S(2)}) collective-permute-start(bf16[6,192,128]{2,1,0:T(8,128)(2,1)S(1)} %constant_dynamic-update-slice_fusion.g_m), channel_id=1, source_target_pairs={{1,0},{2,1},{3,2},{4,3},{5,4},{6,5},{7,6},{9,8},{10,9},{11,10},{12... | collective-permute-start | bytes 884744 | tf_op jit(solution)/shard_map/ppermute | solution.py:489
  58.5 1.0 shard_map.112
  59.8 4.4 %collective-permute-done.7.g_r = bf16[6,192,128]{2,1,0:T(8,128)(2,1)S(1)} collective-permute-done((bf16[6,192,128]{2,1,0:T(8,128)(2,1)S(1)}, bf16[6,192,128]{2,1,0:T(8,128)(2,1)S(1)}, u32[]{:S(2)}, u32[]{:S(2)}) %collective-permute-start.7) | collective-permute-done | bytes 294944 | tf_op jit(solution)/shard_map/ppermute | solution.py:489
  64.5 9.5 %shard_map.113 = (bf16[6,288,128]{2,1,0:T(8,128)(2,1)S(1)}, bf16[1024,128]{1,0:T(8,128)(2,1)S(1)}) custom-call(bf16[6,192,128]{2,1,0:T(8,128)(2,1)S(1)} %collective-permute-done.6.g_l, bf16[6,192,128]{2,1,0:T(8,128)(2,1)S(1)} %constant_dynamic-update-slice_fusion.g_m, bf16[6,192,128]{2,1,0:T(8,128)(2,1)S(1)} %collective-permute-done.7.g_r, ...), custom_call_target="tpu_custom_call" | custom-call | flops 12000000000 | bytes 82888192 | tf_op jit(solution)/shard_map/pallas_call | solution.py:468
  75.9 29.2 %all_to_all.15 = bf16[64,64,128]{2,1,0:T(8,128)(2,1)S(1)} all-to-all(bf16[64,64,128]{2,1,0:T(8,128)(2,1)S(1)} %pad_maximum_fusion), channel_id=1, replica_groups=mesh['gx'=16,'x'=4,'core'=2] {'gx','x'}, dimensions={0} | all-to-all | bytes 2097152 | tf_op jit(solution)/shard_map/all_to_all | solution.py:593
  105.4 16.8 %all_to_all.16.got = bf16[64,40,128]{2,1,0:T(8,128)(2,1)S(1)} all-to-all(bf16[64,40,128]{2,1,0:T(8,128)(2,1)S(1)} %broadcast_in_dim.26), channel_id=1, replica_groups=mesh['gx'=16,'x'=4,'core'=2] {'gx','x'}, dimensions={0} | all-to-all | bytes 1310720 | tf_op jit(solution)/shard_map/all_to_all | solution.py:602
  122.1 3.1 %collective-permute-start.10 = (bf16[64,40,128]{2,1,0:T(8,128)(2,1)S(1)}, bf16[64,40,128]{2,1,0:T(8,128)(2,1)S(1)}, u32[]{:S(2)}, u32[]{:S(2)}) collective-permute-start(bf16[64,40,128]{2,1,0:T(8,128)(2,1)S(1)} %all_to_all.16.got), channel_id=1, source_target_pairs={{0,1},{1,0},{2,3},{3,2},{4,5},{5,4},{6,7},{7,6},{8,9},{9,8},{10,11... | collective-permute-start | bytes 1966088 | tf_op jit(solution)/shard_map/ppermute | solution.py:493
  127.3 3.6 %shard_map.115 = (f32[3,3,3,18432]{3,2,1,0:T(4,128)}, f32[3,3,3,1152]{3,2,1,0:T(4,128)}, f32[3,3,3,1152]{3,2,1,0:T(4,128)}, f32[2,2,2,4608]{3,2,1,0:T(2,128)}) custom-call(s32[1]{0:T(128)} %bitcast.20.core, bf16[64,40,128]{2,1,0:T(8,128)(2,1)S(1)} %all_to_all.16.got, bf16[64,40,128]{2,1,0:T(8,128)(2,1)S(1)} %collective-permute-done.10.other), custom_call_target="tpu_custom_call" | custom-call | bytes 3697668 | tf_op jit(solution)/shard_map/pallas_call | solution.py:468
  (43 shorter events, 7.3 us)
Async XLA Ops:
  0.6 13.4 %copy-start = (f32[12,32,128]{2,1,0:T(8,128)S(1)}, f32[12,32,128]{2,1,0:T(8,128)}, u32[]{:S(2)}) copy-start(f32[12,32,128]{2,1,0:T(8,128)} %param.11) | copy-start | bytes 589828
  1.7 13.1 %collective-permute-start = (bf16[4,192,128]{2,1,0:T(8,128)(2,1)S(1)}, bf16[4,192,128]{2,1,0:T(8,128)(2,1)S(1)}, u32[]{:S(2)}, u32[]{:S(2)}) collective-permute-start(bf16[4,192,128]{2,1,0:T(8,128)(2,1)S(1)} %bitcast.35), channel_id=1, source_target_pairs={{0,8},{8,16},{16,24},{24,32},{32,40},{40,48},{48,56},{56,64},{64,7... | collective-permute-start | bytes 589832 | tf_op jit(solution)/shard_map/ppermute | solution.py:489
  6.1 8.7 %collective-permute-start.1 = (bf16[4,192,128]{2,1,0:T(8,128)(2,1)S(1)}, bf16[4,192,128]{2,1,0:T(8,128)(2,1)}, u32[]{:S(2)}, u32[]{:S(2)}) collective-permute-start(bf16[4,192,128]{2,1,0:T(8,128)(2,1)S(1)} %bitcast.36), channel_id=1, source_target_pairs={{8,0},{16,8},{24,16},{32,24},{40,32},{48,40},{56,48},{64,56},{72,6... | collective-permute-start | bytes 589832 | tf_op jit(solution)/shard_map/ppermute | solution.py:489
  15.8 15.0 %collective-permute-start.2 = (bf16[12,192,128]{2,1,0:T(8,128)(2,1)S(1)}, bf16[12,192,128]{2,1,0:T(8,128)(2,1)}, u32[]{:S(2)}, u32[]{:S(2)}) collective-permute-start(bf16[12,192,128]{2,1,0:T(8,128)(2,1)S(1)} %pad_maximum_fusion.1.feat_m), channel_id=1, source_target_pairs={{0,1},{1,2},{2,3},{3,4},{4,5},{5,6},{6,7},{8,9},{9,10},{10,11},{11... | collective-permute-start | bytes 1769480 | tf_op jit(solution)/shard_map/ppermute | solution.py:489
  19.7 11.3 %collective-permute-start.3 = (bf16[12,192,128]{2,1,0:T(8,128)(2,1)S(1)}, bf16[12,192,128]{2,1,0:T(8,128)(2,1)}, u32[]{:S(2)}, u32[]{:S(2)}) collective-permute-start(bf16[12,192,128]{2,1,0:T(8,128)(2,1)S(1)} %pad_maximum_fusion.1.feat_m), channel_id=1, source_target_pairs={{1,0},{2,1},{3,2},{4,3},{5,4},{6,5},{7,6},{9,8},{10,9},{11,10},{12... | collective-permute-start | bytes 1769480 | tf_op jit(solution)/shard_map/ppermute | solution.py:489
  21.7 18.8 %all-to-all-start = ((bf16[16,12,2,128]{3,2,1,0:T(2,128)(2,1)}), bf16[16,12,2,128]{3,2,1,0:T(2,128)(2,1)S(1)}, u32[]{:S(2)}, u32[]{:S(2)}) async-start(bf16[16,12,2,128]{3,2,1,0:T(2,128)(2,1)} %bitcast.31), calls=%async_computation | async-start | bytes 196608 | tf_op jit(solution)/shard_map/all_to_all | solution.py:522
  41.5 10.4 %collective-permute-start.4 = (bf16[2,192,128]{2,1,0:T(8,128)(2,1)S(1)}, bf16[2,192,128]{2,1,0:T(8,128)(2,1)S(1)}, u32[]{:S(2)}, u32[]{:S(2)}) collective-permute-start(bf16[2,192,128]{2,1,0:T(8,128)(2,1)S(1)} %get-tuple-element.73.grad_three), channel_id=1, source_target_pairs={{0,8},{8,16},{16,24},{24,32},{32,40},{40,48},{48,56},{56,64},{64,7... | collective-permute-start | bytes 294920 | tf_op jit(solution)/shard_map/ppermute | solution.py:489
  45.8 6.1 %collective-permute-start.5 = (bf16[2,192,128]{2,1,0:T(8,128)(2,1)S(1)}, bf16[2,192,128]{2,1,0:T(8,128)(2,1)S(1)}, u32[]{:S(2)}, u32[]{:S(2)}) collective-permute-start(bf16[2,192,128]{2,1,0:T(8,128)(2,1)S(1)} %get-tuple-element.73.grad_three), channel_id=1, source_target_pairs={{8,0},{16,8},{24,16},{32,24},{40,32},{48,40},{56,48},{64,56},{72,6... | collective-permute-start | bytes 294920 | tf_op jit(solution)/shard_map/ppermute | solution.py:489
  52.0 7.8 %collective-permute-start.6 = (bf16[6,192,128]{2,1,0:T(8,128)(2,1)S(1)}, bf16[6,192,128]{2,1,0:T(8,128)(2,1)S(1)}, u32[]{:S(2)}, u32[]{:S(2)}) collective-permute-start(bf16[6,192,128]{2,1,0:T(8,128)(2,1)S(1)} %constant_dynamic-update-slice_fusion.g_m), channel_id=1, source_target_pairs={{0,1},{1,2},{2,3},{3,4},{4,5},{5,6},{6,7},{8,9},{9,10},{10,11},{11... | collective-permute-start | bytes 884744 | tf_op jit(solution)/shard_map/ppermute | solution.py:489
  56.1 8.0 %collective-permute-start.7 = (bf16[6,192,128]{2,1,0:T(8,128)(2,1)S(1)}, bf16[6,192,128]{2,1,0:T(8,128)(2,1)S(1)}, u32[]{:S(2)}, u32[]{:S(2)}) collective-permute-start(bf16[6,192,128]{2,1,0:T(8,128)(2,1)S(1)} %constant_dynamic-update-slice_fusion.g_m), channel_id=1, source_target_pairs={{1,0},{2,1},{3,2},{4,3},{5,4},{6,5},{7,6},{9,8},{10,9},{11,10},{12... | collective-permute-start | bytes 884744 | tf_op jit(solution)/shard_map/ppermute | solution.py:489
  64.2 9.8 %collective-permute-start.8 = (bf16[2048,128]{1,0:T(8,128)(2,1)S(1)}, bf16[2048,128]{1,0:T(8,128)(2,1)S(1)}, u32[]{:S(2)}, u32[]{:S(2)}) collective-permute-start(bf16[2048,128]{1,0:T(8,128)(2,1)S(1)} %constant_dynamic-slice_fusion.2), channel_id=1, source_target_pairs={{0,1},{1,0},{2,3},{3,2},{4,5},{5,4},{6,7},{7,6},{8,9},{9,8},{10,11... | collective-permute-start | bytes 1572872 | tf_op jit(solution)/shard_map/ppermute | solution.py:493
  74.2 1.6 %collective-permute-start.9 = (bf16[512,128]{1,0:T(8,128)(2,1)S(1)}, bf16[512,128]{1,0:T(8,128)(2,1)S(1)}, u32[]{:S(2)}, u32[]{:S(2)}) collective-permute-start(bf16[512,128]{1,0:T(8,128)(2,1)S(1)} %constant_dynamic-slice_fusion.1), channel_id=1, source_target_pairs={{0,1},{1,0},{2,3},{3,2},{4,5},{5,4},{6,7},{7,6},{8,9},{9,8},{10,11... | collective-permute-start | bytes 393224 | tf_op jit(solution)/shard_map/ppermute | solution.py:493
  122.1 5.2 %collective-permute-start.10 = (bf16[64,40,128]{2,1,0:T(8,128)(2,1)S(1)}, bf16[64,40,128]{2,1,0:T(8,128)(2,1)S(1)}, u32[]{:S(2)}, u32[]{:S(2)}) collective-permute-start(bf16[64,40,128]{2,1,0:T(8,128)(2,1)S(1)} %all_to_all.16.got), channel_id=1, source_target_pairs={{0,1},{1,0},{2,3},{3,2},{4,5},{5,4},{6,7},{7,6},{8,9},{9,8},{10,11... | collective-permute-start | bytes 1966088 | tf_op jit(solution)/shard_map/ppermute | solution.py:493

commit v5 on v4

--- a/solution.py
+++ b/solution.py
@@ -131,7 +131,7 @@
             put(taps_one, x, piece, y, 10)
         return carry
 
-    lax.fori_loop(0, 12, spread_one, 0, unroll=2)
+    lax.fori_loop(0, 12, spread_one, 0, unroll=4)
 
     def step_one(x, carry):
         prod = dot(w_one[...], taps_one[pl.ds(pl.multiple_of(x * 3 * C, 16), 9 * C), :])
@@ -149,7 +149,7 @@
                 slope_a[x, (y - 2) * C : (y - 1) * C, :] = slp
         return carry
 
-    lax.fori_loop(0, 10, step_one, 0, unroll=5)
+    lax.fori_loop(0, 10, step_one, 0, unroll=10)
     copies[3].start()
     copies[4].start()
 
@@ -183,7 +183,7 @@
                     ]
         return carry
 
-    lax.fori_loop(0, 8, step_two, 0, unroll=4)
+    lax.fori_loop(0, 8, step_two, 0, unroll=8)
     copies[5].start()
     copies[6].start()
     for x in range(4):
@@ -248,7 +248,7 @@
 
     for copy in copies[:3]:
         copy.start()
-    lax.fori_loop(0, 9, turn, 0)
+    lax.fori_loop(0, 9, turn, 0, unroll=3)
     copies[3].start()
     for copy in copies:
         copy.wait()
@@ -437,7 +437,7 @@
             mid_one[x, rows, :] = mid
         return carry
 
-    lax.fori_loop(0, 6, step_two, 0, unroll=3)
+    lax.fori_loop(0, 6, step_two, 0, unroll=6)
 
     store.start()
     for x in range(4):
@@ -493,9 +493,9 @@
     return lax.ppermute(array, "core", [(0, 1), (1, 0)])
 
 
-def pair_sum(parts, core):
+def pair_sum(parts, core, kept=None):
     half = parts.shape[0] // 2
-    keep = lax.dynamic_slice_in_dim(parts, core * half, half, 0)
+    keep = lax.dynamic_slice_in_dim(parts if kept is None else kept, core * half, half, 0)
     send = lax.dynamic_slice_in_dim(parts, (1 - core) * half, half, 0)
     both = keep.astype(F32) + other_core(send).astype(F32)
     return both.astype(BF).reshape(64, half // 64, Z)
@@ -565,8 +565,8 @@
         0, 500_000_000,
         grad_own, coarse_in,
     )
-    g_l, g_r, coarse_part = lax.optimization_barrier((g_l, g_r, coarse_part))
-    coarse_mine = pair_sum(coarse_part, core)
+    g_l, g_r, kept = lax.optimization_barrier((g_l, g_r, coarse_part))
+    coarse_mine = pair_sum(coarse_part, core, kept)
     slots = jnp.transpose(coarse_out.reshape(2, 16, 12, Z), (1, 0, 2, 3)).reshape(16, 1, 24, Z)
     there = lax.broadcasted_iota(jnp.int32, (16, 4, 24, Z), 1) == lax.axis_index("x")
     slots = jnp.where(there, slots, jnp.zeros((), BF)).reshape(64, 24, Z)

time: 132 us -> 131 us (level)
  no operation moved by 1% of the time
where the time goes in v5:
time: 131 us; the launch traced here: 130 us
  blocking collectives  46.2 us (35%)
  starting transfers between devices  35.9 us (27%)
  Pallas kernels  28.9 us (22%)
  local copies, waits for them, and re-layouts  10.3 us (8%)
  waiting for transfers between devices  6.09 us (5%)
  other arithmetic  1.67 us (1%)
    all_to_all x1, blocking collectives, per_device(): parts = lax.all_to_all(parts, SAME_CORE, 0, 0, tiled=True)  29.5 us
    pallas_call x7, Pallas kernels, call(): pl.pallas_call(kernel, out_shape=outs, in_specs=[smem if k < n_smem else...  28.9 us
    ppermute x8, starting transfers between devices, neighbours(): return (lax.ppermute(array, axis, up), lax.ppermute(array, axis, down))  23.6 us
    all_to_all x1, blocking collectives, per_device(): lax.all_to_all(jnp.broadcast_to(mine[None], (64,) + mine.shape), SAME_COR...  16.7 us
    all_to_all x1, starting transfers between devices, per_device(): cot = lax.all_to_all(cot, 'gx', 0, 0, tiled=True)  8.98 us
    ppermute x8, waiting for transfers between devices, neighbours(): return (lax.ppermute(array, axis, up), lax.ppermute(array, axis, down))  4.75 us
    ppermute x3, starting transfers between devices, other_core(): return lax.ppermute(array, 'core', [(0, 1), (1, 0)])  3.29 us
    reshape x1, local copies, waits for them, and re-layouts, per_device(): w_coarse = coarse_weight.reshape(9, 3 * CC, CD)  2.81 us
  transfers between devices with their start and end apart: 12, of which 4 were waited for; matrix products, arithmetic and copies ran while one was open for 7% of the time, Pallas kernels for 19%

profile of v5, /device:TPU:1, one launch (start us, length us, event | category | flops | bytes accessed | tf_op | source)
XLA Modules:
  0.0 130.1 jit_solution(6061677144359589939)
XLA Ops:
  0.6 1.0 copy.23
  1.7 4.4 %collective-permute-start = (bf16[4,192,128]{2,1,0:T(8,128)(2,1)S(1)}, bf16[4,192,128]{2,1,0:T(8,128)(2,1)S(1)}, u32[]{:S(2)}, u32[]{:S(2)}) collective-permute-start(bf16[4,192,128]{2,1,0:T(8,128)(2,1)S(1)} %bitcast.35), channel_id=1, source_target_pairs={{0,8},{8,16},{16,24},{24,32},{32,40},{40,48},{48,56},{56,64},{64,7... | collective-permute-start | bytes 589832 | tf_op jit(solution)/shard_map/ppermute | solution.py:489
  6.1 1.3 collective-permute-start.1
  7.4 1.4 %reshape.61.one = bf16[27,48,24]{2,1,0:T(8,128)(2,1)S(1)} reshape(bf16[3,3,3,1152]{3,2,1,0:T(4,128)(2,1)} %param.7) | data formatting | bytes 124416 | tf_op jit(solution)/shard_map/reshape | solution.py:511
  8.7 1.4 %reshape.62.two = bf16[27,48,24]{2,1,0:T(8,128)(2,1)S(1)} reshape(bf16[3,3,3,1152]{3,2,1,0:T(4,128)(2,1)} %param.8) | data formatting | bytes 124416 | tf_op jit(solution)/shard_map/reshape | solution.py:512
  10.1 1.1 reshape.63.down
  11.2 2.8 %reshape.64.w_coarse.coarse = bf16[9,576,96]{2,1,0:T(8,128)(2,1)S(1)} reshape(bf16[3,3,3,18432]{3,2,1,0:T(4,128)(2,1)} %param.10) | data formatting | bytes 1990656 | tf_op jit(solution)/shard_map/reshape | solution.py:514
  15.8 4.0 %collective-permute-start.2 = (bf16[12,192,128]{2,1,0:T(8,128)(2,1)S(1)}, bf16[12,192,128]{2,1,0:T(8,128)(2,1)}, u32[]{:S(2)}, u32[]{:S(2)}) collective-permute-start(bf16[12,192,128]{2,1,0:T(8,128)(2,1)S(1)} %pad_maximum_fusion.1.feat_m), channel_id=1, source_target_pairs={{0,1},{1,2},{2,3},{3,4},{4,5},{5,6},{6,7},{8,9},{9,10},{10,11},{11... | collective-permute-start | bytes 1769480 | tf_op jit(solution)/shard_map/ppermute | solution.py:489
  19.7 1.9 %collective-permute-start.3 = (bf16[12,192,128]{2,1,0:T(8,128)(2,1)S(1)}, bf16[12,192,128]{2,1,0:T(8,128)(2,1)}, u32[]{:S(2)}, u32[]{:S(2)}) collective-permute-start(bf16[12,192,128]{2,1,0:T(8,128)(2,1)S(1)} %pad_maximum_fusion.1.feat_m), channel_id=1, source_target_pairs={{1,0},{2,1},{3,2},{4,3},{5,4},{6,5},{7,6},{9,8},{10,9},{11,10},{12... | collective-permute-start | bytes 1769480 | tf_op jit(solution)/shard_map/ppermute | solution.py:489
  21.7 9.0 %all-to-all-start = ((bf16[16,12,2,128]{3,2,1,0:T(2,128)(2,1)}), bf16[16,12,2,128]{3,2,1,0:T(2,128)(2,1)S(1)}, u32[]{:S(2)}, u32[]{:S(2)}) async-start(bf16[16,12,2,128]{3,2,1,0:T(2,128)(2,1)} %bitcast.31), calls=%async_computation | async-start | bytes 196608 | tf_op jit(solution)/shard_map/all_to_all | solution.py:522
  31.0 9.1 %shard_map.109 = (bf16[400,288,128]{2,1,0:T(8,128)(2,1)}, bf16[300,384,128]{2,1,0:T(8,128)(2,1)}, bf16[4,96,384]{2,1,0:T(8,128)(2,1)S(1)}) custom-call(f32[4]{0:T(128)S(1)} %add_convert_fusion.2.flags, bf16[12,192,128]{2,1,0:T(8,128)(2,1)} %collective-permute-done.2.feat_l, bf16[12,192,128]{2,1,0:T(8,128)(2,1)S(1)} %pad_maximum_fusion.1.feat_m, ...), custom_call_target="tpu_custom_call" | custom-call | flops 16000000000 | bytes 61244944 | tf_op jit(solution)/shard_map/pallas_call | solution.py:468
  41.1 4.3 %collective-permute-start.4 = (bf16[2,192,128]{2,1,0:T(8,128)(2,1)S(1)}, bf16[2,192,128]{2,1,0:T(8,128)(2,1)S(1)}, u32[]{:S(2)}, u32[]{:S(2)}) collective-permute-start(bf16[2,192,128]{2,1,0:T(8,128)(2,1)S(1)} %get-tuple-element.73.grad_three), channel_id=1, source_target_pairs={{0,8},{8,16},{16,24},{24,32},{32,40},{40,48},{48,56},{56,64},{64,7... | collective-permute-start | bytes 294920 | tf_op jit(solution)/shard_map/ppermute | solution.py:489
  45.4 1.3 collective-permute-start.5
  46.7 4.3 %shard_map.111 = (bf16[144,432]{1,0:T(8,128)(2,1)S(1)}, bf16[144,432]{1,0:T(8,128)(2,1)S(1)}, bf16[192,192]{1,0:T(8,128)(2,1)S(1)}, bf16[200,288,192]{2,1,0:T(8,128)(2,1)}) custom-call(bf16[27,48,24]{2,1,0:T(8,128)(2,1)S(1)} %reshape.61.one, bf16[27,48,24]{2,1,0:T(8,128)(2,1)S(1)} %reshape.62.two, bf16[8,96,48]{2,1,0:T(8,128)(2,1)S(1)} %reshape.63.down, ...), custom_call_target="tpu_custom_call" | custom-call | bytes 23634432 | tf_op jit(solution)/shard_map/pallas_call | solution.py:468
  51.2 4.6 %collective-permute-start.6 = (bf16[6,192,128]{2,1,0:T(8,128)(2,1)S(1)}, bf16[6,192,128]{2,1,0:T(8,128)(2,1)S(1)}, u32[]{:S(2)}, u32[]{:S(2)}) collective-permute-start(bf16[6,192,128]{2,1,0:T(8,128)(2,1)S(1)} %constant_dynamic-update-slice_fusion.g_m), channel_id=1, source_target_pairs={{0,1},{1,2},{2,3},{3,4},{4,5},{5,6},{6,7},{8,9},{9,10},{10,11},{11... | collective-permute-start | bytes 884744 | tf_op jit(solution)/shard_map/ppermute | solution.py:489
  55.7 1.9 %collective-permute-start.7 = (bf16[6,192,128]{2,1,0:T(8,128)(2,1)S(1)}, bf16[6,192,128]{2,1,0:T(8,128)(2,1)S(1)}, u32[]{:S(2)}, u32[]{:S(2)}) collective-permute-start(bf16[6,192,128]{2,1,0:T(8,128)(2,1)S(1)} %constant_dynamic-update-slice_fusion.g_m), channel_id=1, source_target_pairs={{1,0},{2,1},{3,2},{4,3},{5,4},{6,5},{7,6},{9,8},{10,9},{11,10},{12... | collective-permute-start | bytes 884744 | tf_op jit(solution)/shard_map/ppermute | solution.py:489
  58.1 1.0 shard_map.112
  59.4 4.3 %collective-permute-done.7.g_r = bf16[6,192,128]{2,1,0:T(8,128)(2,1)S(1)} collective-permute-done((bf16[6,192,128]{2,1,0:T(8,128)(2,1)S(1)}, bf16[6,192,128]{2,1,0:T(8,128)(2,1)S(1)}, u32[]{:S(2)}, u32[]{:S(2)}) %collective-permute-start.7) | collective-permute-done | bytes 294944 | tf_op jit(solution)/shard_map/ppermute | solution.py:489
  63.8 9.4 %shard_map.113 = (bf16[6,288,128]{2,1,0:T(8,128)(2,1)S(1)}, bf16[1024,128]{1,0:T(8,128)(2,1)S(1)}) custom-call(bf16[6,192,128]{2,1,0:T(8,128)(2,1)S(1)} %collective-permute-done.6.g_l, bf16[6,192,128]{2,1,0:T(8,128)(2,1)S(1)} %constant_dynamic-update-slice_fusion.g_m, bf16[6,192,128]{2,1,0:T(8,128)(2,1)S(1)} %collective-permute-done.7.g_r, ...), custom_call_target="tpu_custom_call" | custom-call | flops 12000000000 | bytes 82888192 | tf_op jit(solution)/shard_map/pallas_call | solution.py:468
  73.4 1.3 %collective-permute-done.9 = bf16[512,128]{1,0:T(8,128)(2,1)S(1)} collective-permute-done((bf16[512,128]{1,0:T(8,128)(2,1)S(1)}, bf16[512,128]{1,0:T(8,128)(2,1)S(1)}, u32[]{:S(2)}, u32[]{:S(2)}) %collective-permute-start.9) | collective-permute-done | bytes 131104 | tf_op jit(solution)/shard_map/ppermute | solution.py:493
  74.9 29.5 %all_to_all.15 = bf16[64,64,128]{2,1,0:T(8,128)(2,1)S(1)} all-to-all(bf16[64,64,128]{2,1,0:T(8,128)(2,1)S(1)} %pad_maximum_fusion), channel_id=1, replica_groups=mesh['gx'=16,'x'=4,'core'=2] {'gx','x'}, dimensions={0} | all-to-all | bytes 2097152 | tf_op jit(solution)/shard_map/all_to_all | solution.py:593
  104.7 16.7 %all_to_all.16.got = bf16[64,40,128]{2,1,0:T(8,128)(2,1)S(1)} all-to-all(bf16[64,40,128]{2,1,0:T(8,128)(2,1)S(1)} %broadcast_in_dim.26), channel_id=1, replica_groups=mesh['gx'=16,'x'=4,'core'=2] {'gx','x'}, dimensions={0} | all-to-all | bytes 1310720 | tf_op jit(solution)/shard_map/all_to_all | solution.py:602
  121.4 2.9 %collective-permute-start.10 = (bf16[64,40,128]{2,1,0:T(8,128)(2,1)S(1)}, bf16[64,40,128]{2,1,0:T(8,128)(2,1)S(1)}, u32[]{:S(2)}, u32[]{:S(2)}) collective-permute-start(bf16[64,40,128]{2,1,0:T(8,128)(2,1)S(1)} %all_to_all.16.got), channel_id=1, source_target_pairs={{0,1},{1,0},{2,3},{3,2},{4,5},{5,4},{6,7},{7,6},{8,9},{9,8},{10,11... | collective-permute-start | bytes 1966088 | tf_op jit(solution)/shard_map/ppermute | solution.py:493
  126.4 3.6 %shard_map.115 = (f32[3,3,3,18432]{3,2,1,0:T(4,128)}, f32[3,3,3,1152]{3,2,1,0:T(4,128)}, f32[3,3,3,1152]{3,2,1,0:T(4,128)}, f32[2,2,2,4608]{3,2,1,0:T(2,128)}) custom-call(s32[1]{0:T(128)} %bitcast.20.core, bf16[64,40,128]{2,1,0:T(8,128)(2,1)S(1)} %all_to_all.16.got, bf16[64,40,128]{2,1,0:T(8,128)(2,1)S(1)} %collective-permute-done.10.other), custom_call_target="tpu_custom_call" | custom-call | bytes 3697668 | tf_op jit(solution)/shard_map/pallas_call | solution.py:468
  (43 shorter events, 6.7 us)
Async XLA Ops:
  0.6 13.4 %copy-start = (f32[12,32,128]{2,1,0:T(8,128)S(1)}, f32[12,32,128]{2,1,0:T(8,128)}, u32[]{:S(2)}) copy-start(f32[12,32,128]{2,1,0:T(8,128)} %param.11) | copy-start | bytes 589828
  1.7 13.1 %collective-permute-start = (bf16[4,192,128]{2,1,0:T(8,128)(2,1)S(1)}, bf16[4,192,128]{2,1,0:T(8,128)(2,1)S(1)}, u32[]{:S(2)}, u32[]{:S(2)}) collective-permute-start(bf16[4,192,128]{2,1,0:T(8,128)(2,1)S(1)} %bitcast.35), channel_id=1, source_target_pairs={{0,8},{8,16},{16,24},{24,32},{32,40},{40,48},{48,56},{56,64},{64,7... | collective-permute-start | bytes 589832 | tf_op jit(solution)/shard_map/ppermute | solution.py:489
  6.1 8.7 %collective-permute-start.1 = (bf16[4,192,128]{2,1,0:T(8,128)(2,1)S(1)}, bf16[4,192,128]{2,1,0:T(8,128)(2,1)}, u32[]{:S(2)}, u32[]{:S(2)}) collective-permute-start(bf16[4,192,128]{2,1,0:T(8,128)(2,1)S(1)} %bitcast.36), channel_id=1, source_target_pairs={{8,0},{16,8},{24,16},{32,24},{40,32},{48,40},{56,48},{64,56},{72,6... | collective-permute-start | bytes 589832 | tf_op jit(solution)/shard_map/ppermute | solution.py:489
  15.8 15.0 %collective-permute-start.2 = (bf16[12,192,128]{2,1,0:T(8,128)(2,1)S(1)}, bf16[12,192,128]{2,1,0:T(8,128)(2,1)}, u32[]{:S(2)}, u32[]{:S(2)}) collective-permute-start(bf16[12,192,128]{2,1,0:T(8,128)(2,1)S(1)} %pad_maximum_fusion.1.feat_m), channel_id=1, source_target_pairs={{0,1},{1,2},{2,3},{3,4},{4,5},{5,6},{6,7},{8,9},{9,10},{10,11},{11... | collective-permute-start | bytes 1769480 | tf_op jit(solution)/shard_map/ppermute | solution.py:489
  19.7 11.3 %collective-permute-start.3 = (bf16[12,192,128]{2,1,0:T(8,128)(2,1)S(1)}, bf16[12,192,128]{2,1,0:T(8,128)(2,1)}, u32[]{:S(2)}, u32[]{:S(2)}) collective-permute-start(bf16[12,192,128]{2,1,0:T(8,128)(2,1)S(1)} %pad_maximum_fusion.1.feat_m), channel_id=1, source_target_pairs={{1,0},{2,1},{3,2},{4,3},{5,4},{6,5},{7,6},{9,8},{10,9},{11,10},{12... | collective-permute-start | bytes 1769480 | tf_op jit(solution)/shard_map/ppermute | solution.py:489
  21.7 18.4 %all-to-all-start = ((bf16[16,12,2,128]{3,2,1,0:T(2,128)(2,1)}), bf16[16,12,2,128]{3,2,1,0:T(2,128)(2,1)S(1)}, u32[]{:S(2)}, u32[]{:S(2)}) async-start(bf16[16,12,2,128]{3,2,1,0:T(2,128)(2,1)} %bitcast.31), calls=%async_computation | async-start | bytes 196608 | tf_op jit(solution)/shard_map/all_to_all | solution.py:522
  41.1 9.9 %collective-permute-start.4 = (bf16[2,192,128]{2,1,0:T(8,128)(2,1)S(1)}, bf16[2,192,128]{2,1,0:T(8,128)(2,1)S(1)}, u32[]{:S(2)}, u32[]{:S(2)}) collective-permute-start(bf16[2,192,128]{2,1,0:T(8,128)(2,1)S(1)} %get-tuple-element.73.grad_three), channel_id=1, source_target_pairs={{0,8},{8,16},{16,24},{24,32},{32,40},{40,48},{48,56},{56,64},{64,7... | collective-permute-start | bytes 294920 | tf_op jit(solution)/shard_map/ppermute | solution.py:489
  45.4 5.7 %collective-permute-start.5 = (bf16[2,192,128]{2,1,0:T(8,128)(2,1)S(1)}, bf16[2,192,128]{2,1,0:T(8,128)(2,1)S(1)}, u32[]{:S(2)}, u32[]{:S(2)}) collective-permute-start(bf16[2,192,128]{2,1,0:T(8,128)(2,1)S(1)} %get-tuple-element.73.grad_three), channel_id=1, source_target_pairs={{8,0},{16,8},{24,16},{32,24},{40,32},{48,40},{56,48},{64,56},{72,6... | collective-permute-start | bytes 294920 | tf_op jit(solution)/shard_map/ppermute | solution.py:489
  51.2 8.3 %collective-permute-start.6 = (bf16[6,192,128]{2,1,0:T(8,128)(2,1)S(1)}, bf16[6,192,128]{2,1,0:T(8,128)(2,1)S(1)}, u32[]{:S(2)}, u32[]{:S(2)}) collective-permute-start(bf16[6,192,128]{2,1,0:T(8,128)(2,1)S(1)} %constant_dynamic-update-slice_fusion.g_m), channel_id=1, source_target_pairs={{0,1},{1,2},{2,3},{3,4},{4,5},{5,6},{6,7},{8,9},{9,10},{10,11},{11... | collective-permute-start | bytes 884744 | tf_op jit(solution)/shard_map/ppermute | solution.py:489
  55.7 8.0 %collective-permute-start.7 = (bf16[6,192,128]{2,1,0:T(8,128)(2,1)S(1)}, bf16[6,192,128]{2,1,0:T(8,128)(2,1)S(1)}, u32[]{:S(2)}, u32[]{:S(2)}) collective-permute-start(bf16[6,192,128]{2,1,0:T(8,128)(2,1)S(1)} %constant_dynamic-update-slice_fusion.g_m), channel_id=1, source_target_pairs={{1,0},{2,1},{3,2},{4,3},{5,4},{6,5},{7,6},{9,8},{10,9},{11,10},{12... | collective-permute-start | bytes 884744 | tf_op jit(solution)/shard_map/ppermute | solution.py:489
  59.2 14.0 %collective-permute-start.8 = (bf16[2048,128]{1,0:T(8,128)(2,1)S(1)}, bf16[2048,128]{1,0:T(8,128)(2,1)S(1)}, u32[]{:S(2)}, u32[]{:S(2)}) collective-permute-start(bf16[2048,128]{1,0:T(8,128)(2,1)S(1)} %constant_dynamic-slice_fusion.2), channel_id=1, source_target_pairs={{0,1},{1,0},{2,3},{3,2},{4,5},{5,4},{6,7},{7,6},{8,9},{9,8},{10,11... | collective-permute-start | bytes 1572872 | tf_op jit(solution)/shard_map/ppermute | solution.py:493
  73.3 1.4 %collective-permute-start.9 = (bf16[512,128]{1,0:T(8,128)(2,1)S(1)}, bf16[512,128]{1,0:T(8,128)(2,1)S(1)}, u32[]{:S(2)}, u32[]{:S(2)}) collective-permute-start(bf16[512,128]{1,0:T(8,128)(2,1)S(1)} %constant_dynamic-slice_fusion.1), channel_id=1, source_target_pairs={{0,1},{1,0},{2,3},{3,2},{4,5},{5,4},{6,7},{7,6},{8,9},{9,8},{10,11... | collective-permute-start | bytes 393224 | tf_op jit(solution)/shard_map/ppermute | solution.py:493
  121.4 5.1 %collective-permute-start.10 = (bf16[64,40,128]{2,1,0:T(8,128)(2,1)S(1)}, bf16[64,40,128]{2,1,0:T(8,128)(2,1)S(1)}, u32[]{:S(2)}, u32[]{:S(2)}) collective-permute-start(bf16[64,40,128]{2,1,0:T(8,128)(2,1)S(1)} %all_to_all.16.got), channel_id=1, source_target_pairs={{0,1},{1,0},{2,3},{3,2},{4,5},{5,4},{6,7},{7,6},{8,9},{9,8},{10,11... | collective-permute-start | bytes 1966088 | tf_op jit(solution)/shard_map/ppermute | solution.py:493

commit v6 on v5

--- a/solution.py
+++ b/solution.py
@@ -510,14 +510,14 @@
     before, after = neighbours(feat, "gx")
     one = conv_one.reshape(27, C, C // 2)
     two = conv_two.reshape(27, C, C // 2)
-    down = down_weight.reshape(8, CD, C)
     w_coarse = coarse_weight.reshape(9, 3 * CC, CD)
-    before, after, one, two, down, w_coarse = lax.optimization_barrier(
-        (before, after, one, two, down, w_coarse)
+    before, after, one, two, w_coarse = lax.optimization_barrier(
+        (before, after, one, two, w_coarse)
     )
     feat = jnp.concatenate([before, feat, after], axis=0)
     cot = jnp.transpose(cotangent.reshape(12, 16, 2, Z), (1, 0, 2, 3)).astype(BF)
-    feat, cot = lax.optimization_barrier((feat, cot))
+    feat, cot, down_weight = lax.optimization_barrier((feat, cot, down_weight))
+    down = down_weight.reshape(8, CD, C)
     feat_l, feat_r = neighbours(feat, GY)
     cot = lax.all_to_all(cot, "gx", 0, 0, tiled=True)
 

time: 131 us -> 129 us (0.985)
  transfers between devices with their start and end apart: 12 -> 12, of which waited for: 4 -> 5; matrix products, arithmetic and copies ran while one was open for 7% -> 7% of each run, Pallas kernels for 19% -> 19%
where the time goes in v6:
time: 129 us; the launch traced here: 128 us
  blocking collectives  46.2 us (36%)
  starting transfers between devices  34.9 us (27%)
  Pallas kernels  28.9 us (22%)
  local copies, waits for them, and re-layouts  9.45 us (7%)
  waiting for transfers between devices  6.86 us (5%)
    all_to_all x1, blocking collectives, per_device(): parts = lax.all_to_all(parts, SAME_CORE, 0, 0, tiled=True)  29.5 us
    pallas_call x7, Pallas kernels, call(): pl.pallas_call(kernel, out_shape=outs, in_specs=[smem if k < n_smem else...  28.9 us
    ppermute x8, starting transfers between devices, neighbours(): return (lax.ppermute(array, axis, up), lax.ppermute(array, axis, down))  23.5 us
    all_to_all x1, blocking collectives, per_device(): lax.all_to_all(jnp.broadcast_to(mine[None], (64,) + mine.shape), SAME_COR...  16.7 us
    all_to_all x1, starting transfers between devices, per_device(): cot = lax.all_to_all(cot, 'gx', 0, 0, tiled=True)  8.08 us
    ppermute x8, waiting for transfers between devices, neighbours(): return (lax.ppermute(array, axis, up), lax.ppermute(array, axis, down))  5.52 us
    ppermute x3, starting transfers between devices, other_core(): return lax.ppermute(array, 'core', [(0, 1), (1, 0)])  3.29 us
    reshape x1, local copies, waits for them, and re-layouts, per_device(): w_coarse = coarse_weight.reshape(9, 3 * CC, CD)  2.84 us
  transfers between devices with their start and end apart: 12, of which 5 were waited for; matrix products, arithmetic and copies ran while one was open for 7% of the time, Pallas kernels for 19%

profile of v6, /device:TPU:1, one launch (start us, length us, event | category | flops | bytes accessed | tf_op | source)
XLA Modules:
  0.0 128.1 jit_solution(13362680430838622896)
XLA Ops:
  0.6 1.0 copy.23
  1.7 4.4 %collective-permute-start = (bf16[4,192,128]{2,1,0:T(8,128)(2,1)S(1)}, bf16[4,192,128]{2,1,0:T(8,128)(2,1)S(1)}, u32[]{:S(2)}, u32[]{:S(2)}) collective-permute-start(bf16[4,192,128]{2,1,0:T(8,128)(2,1)S(1)} %bitcast.35), channel_id=1, source_target_pairs={{0,8},{8,16},{16,24},{24,32},{32,40},{40,48},{48,56},{56,64},{64,7... | collective-permute-start | bytes 589832 | tf_op jit(solution)/shard_map/ppermute | solution.py:489
  6.1 1.3 %collective-permute-start.1 = (bf16[4,192,128]{2,1,0:T(8,128)(2,1)S(1)}, bf16[4,192,128]{2,1,0:T(8,128)(2,1)S(1)}, u32[]{:S(2)}, u32[]{:S(2)}) collective-permute-start(bf16[4,192,128]{2,1,0:T(8,128)(2,1)S(1)} %bitcast.36), channel_id=1, source_target_pairs={{8,0},{16,8},{24,16},{32,24},{40,32},{48,40},{56,48},{64,56},{72,6... | collective-permute-start | bytes 589832 | tf_op jit(solution)/shard_map/ppermute | solution.py:489
  7.4 1.4 %reshape.61.one = bf16[27,48,24]{2,1,0:T(8,128)(2,1)S(1)} reshape(bf16[3,3,3,1152]{3,2,1,0:T(4,128)(2,1)} %param.7) | data formatting | bytes 124416 | tf_op jit(solution)/shard_map/reshape | solution.py:511
  8.7 1.4 %reshape.62.two = bf16[27,48,24]{2,1,0:T(8,128)(2,1)S(1)} reshape(bf16[3,3,3,1152]{3,2,1,0:T(4,128)(2,1)} %param.8) | data formatting | bytes 124416 | tf_op jit(solution)/shard_map/reshape | solution.py:512
  10.1 2.8 %reshape.63.w_coarse.coarse = bf16[9,576,96]{2,1,0:T(8,128)(2,1)S(1)} reshape(bf16[3,3,3,18432]{3,2,1,0:T(4,128)(2,1)} %param.10) | data formatting | bytes 1990656 | tf_op jit(solution)/shard_map/reshape | solution.py:513
  13.8 4.7 %collective-permute-start.2 = (bf16[12,192,128]{2,1,0:T(8,128)(2,1)S(1)}, bf16[12,192,128]{2,1,0:T(8,128)(2,1)}, u32[]{:S(2)}, u32[]{:S(2)}) collective-permute-start(bf16[12,192,128]{2,1,0:T(8,128)(2,1)S(1)} %pad_maximum_fusion.1.feat_m), channel_id=1, source_target_pairs={{0,1},{1,2},{2,3},{3,4},{4,5},{5,6},{6,7},{8,9},{9,10},{10,11},{11... | collective-permute-start | bytes 1769480 | tf_op jit(solution)/shard_map/ppermute | solution.py:489
  18.5 1.9 %collective-permute-start.3 = (bf16[12,192,128]{2,1,0:T(8,128)(2,1)S(1)}, bf16[12,192,128]{2,1,0:T(8,128)(2,1)}, u32[]{:S(2)}, u32[]{:S(2)}) collective-permute-start(bf16[12,192,128]{2,1,0:T(8,128)(2,1)S(1)} %pad_maximum_fusion.1.feat_m), channel_id=1, source_target_pairs={{1,0},{2,1},{3,2},{4,3},{5,4},{6,5},{7,6},{9,8},{10,9},{11,10},{12... | collective-permute-start | bytes 1769480 | tf_op jit(solution)/shard_map/ppermute | solution.py:489
  20.8 8.1 %all-to-all-start = ((bf16[16,12,2,128]{3,2,1,0:T(2,128)(2,1)}), bf16[16,12,2,128]{3,2,1,0:T(2,128)(2,1)S(1)}, u32[]{:S(2)}, u32[]{:S(2)}) async-start(bf16[16,12,2,128]{3,2,1,0:T(2,128)(2,1)} %bitcast.31), calls=%async_computation | async-start | bytes 196608 | tf_op jit(solution)/shard_map/all_to_all | solution.py:522
  28.9 1.0 collective-permute-done.3.feat_r
  29.8 9.1 %shard_map.109 = (bf16[400,288,128]{2,1,0:T(8,128)(2,1)}, bf16[300,384,128]{2,1,0:T(8,128)(2,1)}, bf16[4,96,384]{2,1,0:T(8,128)(2,1)S(1)}) custom-call(f32[4]{0:T(128)S(1)} %add_convert_fusion.2.flags, bf16[12,192,128]{2,1,0:T(8,128)(2,1)} %collective-permute-done.2.feat_l, bf16[12,192,128]{2,1,0:T(8,128)(2,1)S(1)} %pad_maximum_fusion.1.feat_m, ...), custom_call_target="tpu_custom_call" | custom-call | flops 16000000000 | bytes 61244944 | tf_op jit(solution)/shard_map/pallas_call | solution.py:468
  39.9 3.5 %collective-permute-start.4 = (bf16[2,192,128]{2,1,0:T(8,128)(2,1)S(1)}, bf16[2,192,128]{2,1,0:T(8,128)(2,1)S(1)}, u32[]{:S(2)}, u32[]{:S(2)}) collective-permute-start(bf16[2,192,128]{2,1,0:T(8,128)(2,1)S(1)} %get-tuple-element.73.grad_three), channel_id=1, source_target_pairs={{0,8},{8,16},{16,24},{24,32},{32,40},{40,48},{48,56},{56,64},{64,7... | collective-permute-start | bytes 294920 | tf_op jit(solution)/shard_map/ppermute | solution.py:489
  43.4 1.3 %collective-permute-start.5 = (bf16[2,192,128]{2,1,0:T(8,128)(2,1)S(1)}, bf16[2,192,128]{2,1,0:T(8,128)(2,1)S(1)}, u32[]{:S(2)}, u32[]{:S(2)}) collective-permute-start(bf16[2,192,128]{2,1,0:T(8,128)(2,1)S(1)} %get-tuple-element.73.grad_three), channel_id=1, source_target_pairs={{8,0},{16,8},{24,16},{32,24},{40,32},{48,40},{56,48},{64,56},{72,6... | collective-permute-start | bytes 294920 | tf_op jit(solution)/shard_map/ppermute | solution.py:489
  44.7 4.3 %shard_map.111 = (bf16[144,432]{1,0:T(8,128)(2,1)S(1)}, bf16[144,432]{1,0:T(8,128)(2,1)S(1)}, bf16[192,192]{1,0:T(8,128)(2,1)S(1)}, bf16[200,288,192]{2,1,0:T(8,128)(2,1)}) custom-call(bf16[27,48,24]{2,1,0:T(8,128)(2,1)S(1)} %reshape.61.one, bf16[27,48,24]{2,1,0:T(8,128)(2,1)S(1)} %reshape.62.two, bf16[8,96,48]{2,1,0:T(8,128)(2,1)S(1)} %reshape.64.down, ...), custom_call_target="tpu_custom_call" | custom-call | bytes 23634432 | tf_op jit(solution)/shard_map/pallas_call | solution.py:468
  49.2 4.5 %collective-permute-start.6 = (bf16[6,192,128]{2,1,0:T(8,128)(2,1)S(1)}, bf16[6,192,128]{2,1,0:T(8,128)(2,1)S(1)}, u32[]{:S(2)}, u32[]{:S(2)}) collective-permute-start(bf16[6,192,128]{2,1,0:T(8,128)(2,1)S(1)} %constant_dynamic-update-slice_fusion.g_m), channel_id=1, source_target_pairs={{0,1},{1,2},{2,3},{3,4},{4,5},{5,6},{6,7},{8,9},{9,10},{10,11},{11... | collective-permute-start | bytes 884744 | tf_op jit(solution)/shard_map/ppermute | solution.py:489
  53.8 1.9 %collective-permute-start.7 = (bf16[6,192,128]{2,1,0:T(8,128)(2,1)S(1)}, bf16[6,192,128]{2,1,0:T(8,128)(2,1)S(1)}, u32[]{:S(2)}, u32[]{:S(2)}) collective-permute-start(bf16[6,192,128]{2,1,0:T(8,128)(2,1)S(1)} %constant_dynamic-update-slice_fusion.g_m), channel_id=1, source_target_pairs={{1,0},{2,1},{3,2},{4,3},{5,4},{6,5},{7,6},{9,8},{10,9},{11,10},{12... | collective-permute-start | bytes 884744 | tf_op jit(solution)/shard_map/ppermute | solution.py:489
  56.1 1.0 shard_map.112
  57.5 4.3 %collective-permute-done.7.g_r = bf16[6,192,128]{2,1,0:T(8,128)(2,1)S(1)} collective-permute-done((bf16[6,192,128]{2,1,0:T(8,128)(2,1)S(1)}, bf16[6,192,128]{2,1,0:T(8,128)(2,1)S(1)}, u32[]{:S(2)}, u32[]{:S(2)}) %collective-permute-start.7) | collective-permute-done | bytes 294944 | tf_op jit(solution)/shard_map/ppermute | solution.py:489
  61.8 9.4 %shard_map.113 = (bf16[6,288,128]{2,1,0:T(8,128)(2,1)S(1)}, bf16[1024,128]{1,0:T(8,128)(2,1)S(1)}) custom-call(bf16[6,192,128]{2,1,0:T(8,128)(2,1)S(1)} %collective-permute-done.6.g_l, bf16[6,192,128]{2,1,0:T(8,128)(2,1)S(1)} %constant_dynamic-update-slice_fusion.g_m, bf16[6,192,128]{2,1,0:T(8,128)(2,1)S(1)} %collective-permute-done.7.g_r, ...), custom_call_target="tpu_custom_call" | custom-call | flops 12000000000 | bytes 82888192 | tf_op jit(solution)/shard_map/pallas_call | solution.py:468
  71.5 1.3 %collective-permute-done.9 = bf16[512,128]{1,0:T(8,128)(2,1)S(1)} collective-permute-done((bf16[512,128]{1,0:T(8,128)(2,1)S(1)}, bf16[512,128]{1,0:T(8,128)(2,1)S(1)}, u32[]{:S(2)}, u32[]{:S(2)}) %collective-permute-start.9) | collective-permute-done | bytes 131104 | tf_op jit(solution)/shard_map/ppermute | solution.py:493
  73.0 29.5 %all_to_all.15 = bf16[64,64,128]{2,1,0:T(8,128)(2,1)S(1)} all-to-all(bf16[64,64,128]{2,1,0:T(8,128)(2,1)S(1)} %pad_maximum_fusion), channel_id=1, replica_groups=mesh['gx'=16,'x'=4,'core'=2] {'gx','x'}, dimensions={0} | all-to-all | bytes 2097152 | tf_op jit(solution)/shard_map/all_to_all | solution.py:593
  102.7 16.7 %all_to_all.16.got = bf16[64,40,128]{2,1,0:T(8,128)(2,1)S(1)} all-to-all(bf16[64,40,128]{2,1,0:T(8,128)(2,1)S(1)} %broadcast_in_dim.26), channel_id=1, replica_groups=mesh['gx'=16,'x'=4,'core'=2] {'gx','x'}, dimensions={0} | all-to-all | bytes 1310720 | tf_op jit(solution)/shard_map/all_to_all | solution.py:602
  119.4 2.9 %collective-permute-start.10 = (bf16[64,40,128]{2,1,0:T(8,128)(2,1)S(1)}, bf16[64,40,128]{2,1,0:T(8,128)(2,1)S(1)}, u32[]{:S(2)}, u32[]{:S(2)}) collective-permute-start(bf16[64,40,128]{2,1,0:T(8,128)(2,1)S(1)} %all_to_all.16.got), channel_id=1, source_target_pairs={{0,1},{1,0},{2,3},{3,2},{4,5},{5,4},{6,7},{7,6},{8,9},{9,8},{10,11... | collective-permute-start | bytes 1966088 | tf_op jit(solution)/shard_map/ppermute | solution.py:493
  124.5 3.6 %shard_map.115 = (f32[3,3,3,18432]{3,2,1,0:T(4,128)}, f32[3,3,3,1152]{3,2,1,0:T(4,128)}, f32[3,3,3,1152]{3,2,1,0:T(4,128)}, f32[2,2,2,4608]{3,2,1,0:T(2,128)}) custom-call(s32[1]{0:T(128)} %bitcast.20.core, bf16[64,40,128]{2,1,0:T(8,128)(2,1)S(1)} %all_to_all.16.got, bf16[64,40,128]{2,1,0:T(8,128)(2,1)S(1)} %collective-permute-done.10.other), custom_call_target="tpu_custom_call" | custom-call | bytes 3697668 | tf_op jit(solution)/shard_map/pallas_call | solution.py:468
  (45 shorter events, 5.7 us)
Async XLA Ops:
  0.6 12.3 %copy-start = (f32[12,32,128]{2,1,0:T(8,128)S(1)}, f32[12,32,128]{2,1,0:T(8,128)}, u32[]{:S(2)}) copy-start(f32[12,32,128]{2,1,0:T(8,128)} %param.11) | copy-start | bytes 589828
  1.7 12.0 %collective-permute-start = (bf16[4,192,128]{2,1,0:T(8,128)(2,1)S(1)}, bf16[4,192,128]{2,1,0:T(8,128)(2,1)S(1)}, u32[]{:S(2)}, u32[]{:S(2)}) collective-permute-start(bf16[4,192,128]{2,1,0:T(8,128)(2,1)S(1)} %bitcast.35), channel_id=1, source_target_pairs={{0,8},{8,16},{16,24},{24,32},{32,40},{40,48},{48,56},{56,64},{64,7... | collective-permute-start | bytes 589832 | tf_op jit(solution)/shard_map/ppermute | solution.py:489
  6.1 7.7 %collective-permute-start.1 = (bf16[4,192,128]{2,1,0:T(8,128)(2,1)S(1)}, bf16[4,192,128]{2,1,0:T(8,128)(2,1)S(1)}, u32[]{:S(2)}, u32[]{:S(2)}) collective-permute-start(bf16[4,192,128]{2,1,0:T(8,128)(2,1)S(1)} %bitcast.36), channel_id=1, source_target_pairs={{8,0},{16,8},{24,16},{32,24},{40,32},{48,40},{56,48},{64,56},{72,6... | collective-permute-start | bytes 589832 | tf_op jit(solution)/shard_map/ppermute | solution.py:489
  10.1 10.5 %copy-start.1 = (bf16[2,2,2,4608]{3,2,1,0:T(2,128)(2,1)S(1)}, bf16[2,2,2,4608]{3,2,1,0:T(2,128)(2,1)}, u32[]{:S(2)}) copy-start(bf16[2,2,2,4608]{3,2,1,0:T(2,128)(2,1)} %param.9) | copy-start | bytes 221188
  13.8 15.0 %collective-permute-start.2 = (bf16[12,192,128]{2,1,0:T(8,128)(2,1)S(1)}, bf16[12,192,128]{2,1,0:T(8,128)(2,1)}, u32[]{:S(2)}, u32[]{:S(2)}) collective-permute-start(bf16[12,192,128]{2,1,0:T(8,128)(2,1)S(1)} %pad_maximum_fusion.1.feat_m), channel_id=1, source_target_pairs={{0,1},{1,2},{2,3},{3,4},{4,5},{5,6},{6,7},{8,9},{9,10},{10,11},{11... | collective-permute-start | bytes 1769480 | tf_op jit(solution)/shard_map/ppermute | solution.py:489
  18.5 11.3 %collective-permute-start.3 = (bf16[12,192,128]{2,1,0:T(8,128)(2,1)S(1)}, bf16[12,192,128]{2,1,0:T(8,128)(2,1)}, u32[]{:S(2)}, u32[]{:S(2)}) collective-permute-start(bf16[12,192,128]{2,1,0:T(8,128)(2,1)S(1)} %pad_maximum_fusion.1.feat_m), channel_id=1, source_target_pairs={{1,0},{2,1},{3,2},{4,3},{5,4},{6,5},{7,6},{9,8},{10,9},{11,10},{12... | collective-permute-start | bytes 1769480 | tf_op jit(solution)/shard_map/ppermute | solution.py:489
  20.8 18.2 %all-to-all-start = ((bf16[16,12,2,128]{3,2,1,0:T(2,128)(2,1)}), bf16[16,12,2,128]{3,2,1,0:T(2,128)(2,1)S(1)}, u32[]{:S(2)}, u32[]{:S(2)}) async-start(bf16[16,12,2,128]{3,2,1,0:T(2,128)(2,1)} %bitcast.31), calls=%async_computation | async-start | bytes 196608 | tf_op jit(solution)/shard_map/all_to_all | solution.py:522
  39.9 9.1 %collective-permute-start.4 = (bf16[2,192,128]{2,1,0:T(8,128)(2,1)S(1)}, bf16[2,192,128]{2,1,0:T(8,128)(2,1)S(1)}, u32[]{:S(2)}, u32[]{:S(2)}) collective-permute-start(bf16[2,192,128]{2,1,0:T(8,128)(2,1)S(1)} %get-tuple-element.73.grad_three), channel_id=1, source_target_pairs={{0,8},{8,16},{16,24},{24,32},{32,40},{40,48},{48,56},{56,64},{64,7... | collective-permute-start | bytes 294920 | tf_op jit(solution)/shard_map/ppermute | solution.py:489
  43.4 5.7 %collective-permute-start.5 = (bf16[2,192,128]{2,1,0:T(8,128)(2,1)S(1)}, bf16[2,192,128]{2,1,0:T(8,128)(2,1)S(1)}, u32[]{:S(2)}, u32[]{:S(2)}) collective-permute-start(bf16[2,192,128]{2,1,0:T(8,128)(2,1)S(1)} %get-tuple-element.73.grad_three), channel_id=1, source_target_pairs={{8,0},{16,8},{24,16},{32,24},{40,32},{48,40},{56,48},{64,56},{72,6... | collective-permute-start | bytes 294920 | tf_op jit(solution)/shard_map/ppermute | solution.py:489
  49.2 8.3 %collective-permute-start.6 = (bf16[6,192,128]{2,1,0:T(8,128)(2,1)S(1)}, bf16[6,192,128]{2,1,0:T(8,128)(2,1)S(1)}, u32[]{:S(2)}, u32[]{:S(2)}) collective-permute-start(bf16[6,192,128]{2,1,0:T(8,128)(2,1)S(1)} %constant_dynamic-update-slice_fusion.g_m), channel_id=1, source_target_pairs={{0,1},{1,2},{2,3},{3,4},{4,5},{5,6},{6,7},{8,9},{9,10},{10,11},{11... | collective-permute-start | bytes 884744 | tf_op jit(solution)/shard_map/ppermute | solution.py:489
  53.8 8.0 %collective-permute-start.7 = (bf16[6,192,128]{2,1,0:T(8,128)(2,1)S(1)}, bf16[6,192,128]{2,1,0:T(8,128)(2,1)S(1)}, u32[]{:S(2)}, u32[]{:S(2)}) collective-permute-start(bf16[6,192,128]{2,1,0:T(8,128)(2,1)S(1)} %constant_dynamic-update-slice_fusion.g_m), channel_id=1, source_target_pairs={{1,0},{2,1},{3,2},{4,3},{5,4},{6,5},{7,6},{9,8},{10,9},{11,10},{12... | collective-permute-start | bytes 884744 | tf_op jit(solution)/shard_map/ppermute | solution.py:489
  57.2 14.0 %collective-permute-start.8 = (bf16[2048,128]{1,0:T(8,128)(2,1)S(1)}, bf16[2048,128]{1,0:T(8,128)(2,1)S(1)}, u32[]{:S(2)}, u32[]{:S(2)}) collective-permute-start(bf16[2048,128]{1,0:T(8,128)(2,1)S(1)} %constant_dynamic-slice_fusion.2), channel_id=1, source_target_pairs={{0,1},{1,0},{2,3},{3,2},{4,5},{5,4},{6,7},{7,6},{8,9},{9,8},{10,11... | collective-permute-start | bytes 1572872 | tf_op jit(solution)/shard_map/ppermute | solution.py:493
  71.4 1.4 %collective-permute-start.9 = (bf16[512,128]{1,0:T(8,128)(2,1)S(1)}, bf16[512,128]{1,0:T(8,128)(2,1)S(1)}, u32[]{:S(2)}, u32[]{:S(2)}) collective-permute-start(bf16[512,128]{1,0:T(8,128)(2,1)S(1)} %constant_dynamic-slice_fusion.1), channel_id=1, source_target_pairs={{0,1},{1,0},{2,3},{3,2},{4,5},{5,4},{6,7},{7,6},{8,9},{9,8},{10,11... | collective-permute-start | bytes 393224 | tf_op jit(solution)/shard_map/ppermute | solution.py:493
  119.4 5.1 %collective-permute-start.10 = (bf16[64,40,128]{2,1,0:T(8,128)(2,1)S(1)}, bf16[64,40,128]{2,1,0:T(8,128)(2,1)S(1)}, u32[]{:S(2)}, u32[]{:S(2)}) collective-permute-start(bf16[64,40,128]{2,1,0:T(8,128)(2,1)S(1)} %all_to_all.16.got), channel_id=1, source_target_pairs={{0,1},{1,0},{2,3},{3,2},{4,5},{5,4},{6,7},{7,6},{8,9},{9,8},{10,11... | collective-permute-start | bytes 1966088 | tf_op jit(solution)/shard_map/ppermute | solution.py:493
